TPU v7x, 128 devices: a whole 4x4x4 slice. The times are simulated.
128 devices in a mesh: row: 8 (over y, core), col: 16 (over x, z).
Axes of the slice: x: 4, y: 4, z: 4, core: 2. Of those that a mesh axis runs over, the one named last changes fastest.
Arguments:
- tokens: bfloat16 [1024, 16384], P('col', 'row'), may hold values from -6 to 6
- w_qkv: bfloat16 [2, 3, 1024, 1024], P(None, None, 'col', 'row'), may hold values from -0.1875 to 0.1875
- bias_qv: float32 [2, 2, 1024], P(None, None, 'col'), may hold values from -3 to 3
- w_out: bfloat16 [2, 1024, 1024], P(None, 'col', 'row'), may hold values from -3.5 to 3.5
- bias_out: float32 [2, 1024], P(None, 'col'), may hold values from -2 to 2
- gain_attn: float32 [2, 1024], P(None, 'col'), may hold values from 0.1 to 1.9
- shift_attn: float32 [2, 1024], P(None, 'col'), may hold values from -2 to 2
- w_up: bfloat16 [2, 4096, 1024], P(None, 'col', 'row'), may hold values from -0.1875 to 0.1875
- bias_up: float32 [2, 4096], P(None, 'col'), may hold values from -3 to 3
- w_down: bfloat16 [2, 1024, 4096], P(None, 'col', 'row'), may hold values from -0.125 to 0.125
- bias_down: float32 [2, 1024], P(None, 'col'), may hold values from -2 to 2
- gain_ffn: float32 [2, 1024], P(None, 'col'), may hold values from 0.1 to 1.9
- shift_ffn: float32 [2, 1024], P(None, 'col'), may hold values from -2 to 2
- cotangent: bfloat16 [1024, 16384], P('col', 'row'), may hold values from -6 to 6
Outputs:
- output: bfloat16 [1024, 16384], P('col', 'row')
- grad_tokens: float32 [1024, 16384], P('col', 'row')
- grad_w_qkv: float32 [2, 3, 1024, 1024], P(None, None, 'col', 'row')
- grad_bias_qv: float32 [2, 2, 1024], P(None, None, 'col')
- grad_w_out: float32 [2, 1024, 1024], P(None, 'col', 'row')
- grad_bias_out: float32 [2, 1024], P(None, 'col')
- grad_gain_attn: float32 [2, 1024], P(None, 'col')
- grad_shift_attn: float32 [2, 1024], P(None, 'col')
- grad_w_up: float32 [2, 4096, 1024], P(None, 'col', 'row')
- grad_bias_up: float32 [2, 4096], P(None, 'col')
- grad_w_down: float32 [2, 1024, 4096], P(None, 'col', 'row')
- grad_bias_down: float32 [2, 1024], P(None, 'col')
- grad_gain_ffn: float32 [2, 1024], P(None, 'col')
- grad_shift_ffn: float32 [2, 1024], P(None, 'col')
All inputs are finite; a program needn't handle non-finite values.
Results may differ from a plain program's by a relative error of at most 0.04.
Values may be sent and summed in bfloat16 or wider, within the bound.
No kernel may reach another device: no remote copies, remote signals or barrier semaphores. Data moves between devices by JAX's collectives and lax.ppermute only.
A program may use at most 256 MiB of HBM per device.

v0:
```python
from functools import partial

import jax
import jax.numpy as jnp
from jax import lax
from jax.sharding import PartitionSpec as P

HEAD = 64
D = 1024
LAYERS = 2
SEQ_LEN = 1024


epsilon = 1e-05


def spread(values):
    return lax.all_gather(values, "col", axis=0, tiled=True)


def collect(values):
    return lax.psum_scatter(
        values.astype(jnp.bfloat16), "col", scatter_dimension=0, tiled=True
    ).astype(jnp.float32)


def norm_forward(summed, gain, shift):
    centre = lax.psum(jnp.sum(summed, axis=0), "col") / D
    centred = summed - centre[None, :]
    variance = lax.psum(jnp.sum(centred * centred, axis=0), "col") / D
    scaled = lax.rsqrt(variance + epsilon)[None, :]
    normed = centred * scaled
    return (normed * gain[:, None] + shift[:, None], normed, scaled)


def norm_backward(incoming, normed, scaled, gain):
    grad_norm = incoming * gain[:, None]
    plain_sum, cross_sum = lax.psum(
        (jnp.sum(grad_norm, axis=0), jnp.sum(grad_norm * normed, axis=0)), "col"
    )
    return scaled * (grad_norm - plain_sum[None, :] / D - normed * cross_sum[None, :] / D)


def attend_forward(qkv_low):
    width = qkv_low.shape[1]
    token_count = qkv_low.shape[2]
    heads_here = width // HEAD
    seq_count = token_count // SEQ_LEN
    shaped = jnp.transpose(
        qkv_low.reshape(3, heads_here, HEAD, seq_count, SEQ_LEN), (3, 0, 1, 2, 4)
    )
    factor = HEAD ** (-0.5)

    def one_sequence(packed):
        scores = (
            jnp.einsum("hcq,hck->hqk", packed[0], packed[1], preferred_element_type=jnp.float32)
            * factor
        )
        highest_score = jnp.max(scores, axis=-1, keepdims=True)
        exps = jnp.exp(scores - highest_score)
        row_total = jnp.sum(exps, axis=-1, keepdims=True)
        probs_low = (exps / row_total).astype(jnp.bfloat16)
        blended = jnp.einsum(
            "hqk,hck->hcq", probs_low, packed[2], preferred_element_type=jnp.float32
        )
        return (blended, (highest_score + jnp.log(row_total))[..., 0])

    blended, logsum = lax.map(one_sequence, shaped)
    return (jnp.transpose(blended, (1, 2, 0, 3)).reshape(width, token_count), logsum)


def attend_backward(qkv_low, logsum, grad_blended):
    width = qkv_low.shape[1]
    token_count = qkv_low.shape[2]
    heads_here = width // HEAD
    seq_count = token_count // SEQ_LEN
    shaped = jnp.transpose(
        qkv_low.reshape(3, heads_here, HEAD, seq_count, SEQ_LEN), (3, 0, 1, 2, 4)
    )
    grad_shaped = jnp.transpose(
        grad_blended.reshape(heads_here, HEAD, seq_count, SEQ_LEN), (2, 0, 1, 3)
    )
    factor = HEAD ** (-0.5)

    def one_sequence(inputs):
        packed, grad_part, log_total = inputs
        queries = packed[0]
        key_part = packed[1]
        value_part = packed[2]
        scores = (
            jnp.einsum("hcq,hck->hqk", queries, key_part, preferred_element_type=jnp.float32)
            * factor
        )
        probs = jnp.exp(scores - log_total[..., None])
        grad_probs = jnp.einsum(
            "hcq,hck->hqk", grad_part, value_part, preferred_element_type=jnp.float32
        )
        grad_values = jnp.einsum(
            "hqk,hcq->hck",
            probs.astype(jnp.bfloat16),
            grad_part,
            preferred_element_type=jnp.float32,
        )
        grad_scores = probs * (grad_probs - jnp.sum(probs * grad_probs, axis=-1, keepdims=True))
        grad_scores = grad_scores.astype(jnp.bfloat16)
        grad_queries = (
            jnp.einsum("hqk,hck->hcq", grad_scores, key_part, preferred_element_type=jnp.float32)
            * factor
        )
        grad_keys = (
            jnp.einsum("hqk,hcq->hck", grad_scores, queries, preferred_element_type=jnp.float32)
            * factor
        )
        return jnp.stack([grad_queries, grad_keys, grad_values], axis=0)

    stacked = lax.map(one_sequence, (shaped, grad_shaped, logsum))
    return jnp.transpose(stacked, (1, 2, 3, 0, 4)).reshape(3, width, token_count)


def on_device(
    tokens,
    w_qkv,
    bias_qv,
    w_out,
    bias_out,
    gain_attn,
    shift_attn,
    w_up,
    bias_up,
    w_down,
    bias_down,
    gain_ffn,
    shift_ffn,
    cotangent,
):
    stream = tokens.astype(jnp.float32)
    stored = []
    for layer_idx in range(LAYERS):
        weights = (
            lax.all_gather(w_qkv[layer_idx], "row", axis=2, tiled=True),
            lax.all_gather(w_out[layer_idx], "row", axis=1, tiled=True),
            lax.all_gather(w_up[layer_idx], "row", axis=1, tiled=True),
            lax.all_gather(w_down[layer_idx], "row", axis=1, tiled=True),
        )
        seen = spread(stream.astype(jnp.bfloat16))
        bias_three = jnp.stack(
            [bias_qv[layer_idx, 0], jnp.zeros_like(bias_qv[layer_idx, 0]), bias_qv[layer_idx, 1]]
        )
        qkv_low = (
            jnp.einsum("jed,dt->jet", weights[0], seen, preferred_element_type=jnp.float32)
            + bias_three[:, :, None]
        ).astype(jnp.bfloat16)
        blended, logsum = attend_forward(qkv_low)
        blended_seen = spread(blended.astype(jnp.bfloat16))
        attn_out = (
            jnp.dot(weights[1], blended_seen, preferred_element_type=jnp.float32)
            + bias_out[layer_idx][:, None]
        )
        first_out, normed_attn, scaled_attn = norm_forward(
            stream + attn_out, gain_attn[layer_idx], shift_attn[layer_idx]
        )
        first_seen = spread(first_out.astype(jnp.bfloat16))
        upper_pre = (
            jnp.dot(weights[2], first_seen, preferred_element_type=jnp.float32)
            + bias_up[layer_idx][:, None]
        )
        activated, gelu_back = jax.vjp(partial(jax.nn.gelu, approximate=False), upper_pre)
        active_seen = lax.all_gather(activated.astype(jnp.bfloat16), "col", axis=0, tiled=True)
        lower_out = (
            jnp.dot(weights[3], active_seen, preferred_element_type=jnp.float32)
            + bias_down[layer_idx][:, None]
        )
        stream, normed_ffn, scaled_ffn = norm_forward(
            first_out + lower_out, gain_ffn[layer_idx], shift_ffn[layer_idx]
        )
        stored.append(
            (
                weights,
                seen,
                qkv_low,
                logsum,
                blended_seen,
                normed_attn,
                scaled_attn,
                first_seen,
                gelu_back,
                active_seen,
                normed_ffn,
                scaled_ffn,
            )
        )
    result = stream.astype(jnp.bfloat16)
    backward = cotangent.astype(jnp.float32)
    matrix_list = [None] * LAYERS
    minor_list = [None] * LAYERS
    for layer_idx in reversed(range(LAYERS)):
        (
            weights,
            seen,
            qkv_low,
            logsum,
            blended_seen,
            normed_attn,
            scaled_attn,
            first_seen,
            gelu_back,
            active_seen,
            normed_ffn,
            scaled_ffn,
        ) = stored[layer_idx]
        grad_sum = norm_backward(backward, normed_ffn, scaled_ffn, gain_ffn[layer_idx])
        part_gain_ffn = jnp.sum(backward * normed_ffn, axis=1)
        part_shift_ffn = jnp.sum(backward, axis=1)
        grad_lower = grad_sum.astype(jnp.bfloat16)
        part_down = jnp.sum(grad_lower, axis=1, dtype=jnp.float32)
        grad_w_down = jnp.einsum(
            "dt,ft->df", grad_lower, active_seen, preferred_element_type=jnp.float32
        )
        grad_active = lax.psum_scatter(
            jnp.einsum(
                "df,dt->ft", weights[3], grad_lower, preferred_element_type=jnp.float32
            ).astype(jnp.bfloat16),
            "col",
            scatter_dimension=0,
            tiled=True,
        ).astype(jnp.float32)
        grad_upper = gelu_back(grad_active)[0].astype(jnp.bfloat16)
        part_up = jnp.sum(grad_upper, axis=1, dtype=jnp.float32)
        grad_w_up = jnp.einsum(
            "ft,dt->fd", grad_upper, first_seen, preferred_element_type=jnp.float32
        )
        grad_first = (
            collect(
                jnp.einsum("fd,ft->dt", weights[2], grad_upper, preferred_element_type=jnp.float32)
            )
            + grad_sum
        )
        part_gain_attn = jnp.sum(grad_first * normed_attn, axis=1)
        part_shift_attn = jnp.sum(grad_first, axis=1)
        grad_total = norm_backward(grad_first, normed_attn, scaled_attn, gain_attn[layer_idx])
        grad_attn = grad_total.astype(jnp.bfloat16)
        part_out = jnp.sum(grad_attn, axis=1, dtype=jnp.float32)
        grad_w_out = jnp.einsum(
            "et,dt->ed", grad_attn, blended_seen, preferred_element_type=jnp.float32
        )
        grad_blended = lax.psum_scatter(
            jnp.einsum(
                "ed,et->dt", weights[1], grad_attn, preferred_element_type=jnp.float32
            ).astype(jnp.bfloat16),
            "col",
            scatter_dimension=0,
            tiled=True,
        )
        grad_qkv = attend_backward(qkv_low, logsum, grad_blended).astype(jnp.bfloat16)
        part_qv = jnp.stack(
            [
                jnp.sum(grad_qkv[0], axis=1, dtype=jnp.float32),
                jnp.sum(grad_qkv[2], axis=1, dtype=jnp.float32),
            ]
        )
        grad_w_qkv = jnp.einsum("jet,dt->jed", grad_qkv, seen, preferred_element_type=jnp.float32)
        backward = (
            collect(
                jnp.einsum("jed,jet->dt", weights[0], grad_qkv, preferred_element_type=jnp.float32)
            )
            + grad_total
        )
        matrix_list[layer_idx] = (
            lax.psum_scatter(
                grad_w_qkv.astype(jnp.bfloat16), "row", scatter_dimension=2, tiled=True
            ).astype(jnp.float32),
            lax.psum_scatter(
                grad_w_out.astype(jnp.bfloat16), "row", scatter_dimension=1, tiled=True
            ).astype(jnp.float32),
            lax.psum_scatter(
                grad_w_up.astype(jnp.bfloat16), "row", scatter_dimension=1, tiled=True
            ).astype(jnp.float32),
            lax.psum_scatter(
                grad_w_down.astype(jnp.bfloat16), "row", scatter_dimension=1, tiled=True
            ).astype(jnp.float32),
        )
        minor_list[layer_idx] = (
            part_qv,
            part_out,
            part_gain_attn,
            part_shift_attn,
            part_up,
            part_down,
            part_gain_ffn,
            part_shift_ffn,
        )
    (
        stack_qv,
        stack_out,
        stack_gain_attn,
        stack_shift_attn,
        stack_up,
        stack_down,
        stack_gain_ffn,
        stack_shift_ffn,
    ) = [jnp.stack([entry[member] for entry in minor_list]) for member in range(8)]
    summed_minor = lax.psum(
        (
            stack_qv,
            stack_out,
            stack_gain_attn,
            stack_shift_attn,
            stack_up,
            stack_down,
            stack_gain_ffn,
            stack_shift_ffn,
        ),
        "row",
    )
    final_qkv, final_out, final_up, final_down = [
        jnp.stack([entry[member] for entry in matrix_list]) for member in range(4)
    ]
    return (
        result,
        backward,
        final_qkv,
        summed_minor[0],
        final_out,
        summed_minor[1],
        summed_minor[2],
        summed_minor[3],
        final_up,
        summed_minor[4],
        final_down,
        summed_minor[5],
        summed_minor[6],
        summed_minor[7],
    )


def solution(mesh):
    in_specs = (
        P("col", "row"),
        P(None, None, "col", "row"),
        P(None, None, "col"),
        P(None, "col", "row"),
        P(None, "col"),
        P(None, "col"),
        P(None, "col"),
        P(None, "col", "row"),
        P(None, "col"),
        P(None, "col", "row"),
        P(None, "col"),
        P(None, "col"),
        P(None, "col"),
        P("col", "row"),
    )
    out_specs = (
        P("col", "row"),
        P("col", "row"),
        P(None, None, "col", "row"),
        P(None, None, "col"),
        P(None, "col", "row"),
        P(None, "col"),
        P(None, "col"),
        P(None, "col"),
        P(None, "col", "row"),
        P(None, "col"),
        P(None, "col", "row"),
        P(None, "col"),
        P(None, "col"),
        P(None, "col"),
    )
    return jax.shard_map(
        on_device, mesh=mesh, in_specs=in_specs, out_specs=out_specs, check_vma=False
    )
```

profile of v0, /device:TPU:1, one launch (start us, length us, event | category | flops | bytes accessed | tf_op | source)
XLA Modules:
  0.0 2240.3 jit_solution(36402141482899695)
XLA Ops:
  8.9 14.0 all-gather
  23.8 41.2 %all-gather.17.cloned.1.call-done = bf16[1024,2048]{1,0:T(8,128)(2,1)} async-done(((bf16[64,2048]{1,0:T(8,128)(2,1)}), bf16[1024,2048]{1,0:T(8,128)(2,1)}) %all-gather.17.cloned.1.call-update) | async-done | bytes 4194320 | tf_op jit(solution)/shard_map/all_gather | solution.py:18
  75.3 12.5 all-gather.1
  87.9 38.8 %all-gather.19.cloned.1.call-done = bf16[1024,2048]{1,0:T(8,128)(2,1)} async-done(((bf16[64,2048]{1,0:T(8,128)(2,1)}), bf16[1024,2048]{1,0:T(8,128)(2,1)}) %all-gather.19.cloned.1.call-update) | async-done | bytes 4194320 | tf_op jit(solution)/shard_map/all_gather | solution.py:18
  129.8 32.1 %psum.168 = f32[2048]{0:T(1024)S(1)} all-reduce(f32[2048]{0:T(1024)S(1)} %get-tuple-element.244), channel_id=1, replica_groups=mesh['row'=8,'col'=16] {'col'}, use_global_device_ids=true, to_apply=%region_5.6 | all-reduce | flops 2048 | bytes 16384 | tf_op jit(solution)/shard_map/psum | solution.py:28
  162.0 29.0 %psum.169 = f32[2048]{0:T(1024)S(1)} all-reduce(f32[2048]{0:T(1024)S(1)} %multiply_reduce_fusion.13), channel_id=1, replica_groups=mesh['row'=8,'col'=16] {'col'}, use_global_device_ids=true, to_apply=%region_7.8 | all-reduce | flops 2048 | bytes 16384 | tf_op jit(solution)/shard_map/psum | solution.py:30
  192.0 27.5 %all-gather.2 = bf16[1,256,1024]{2,1,0:T(8,128)(2,1)S(1)} all-gather(bf16[1,256,128]{2,1,0:T(8,128)(2,1)S(1)} %get-tuple-element.219), channel_id=4, replica_groups=mesh['row'=8,'col'=16] {'row'}, dimensions={2}, use_global_device_ids=true | all-gather | bytes 589824 | tf_op jit(solution)/shard_map/all_gather | solution.py:142
  219.5 35.7 %all-gather.21.cloned.1.call-done = bf16[1024,2048]{1,0:T(8,128)(2,1)} async-done(((bf16[64,2048]{1,0:T(8,128)(2,1)}), bf16[1024,2048]{1,0:T(8,128)(2,1)}) %all-gather.21.cloned.1.call-update) | async-done | bytes 4194320 | tf_op jit(solution)/shard_map/all_gather | solution.py:18
  255.2 10.1 fusion.110
  265.5 14.2 all-gather.3
  279.7 105.7 %all-gather.23.cloned.1.call-done = bf16[4096,2048]{0,1:T(8,128)(2,1)} async-done(((bf16[256,2048]{0,1:T(8,128)(2,1)}), bf16[4096,2048]{0,1:T(8,128)(2,1)}) %all-gather.23.cloned.1.call-update) | async-done | bytes 16777232 | tf_op jit(solution)/shard_map/all_gather | solution.py:168
  385.4 11.0 fusion.187
  396.4 31.4 %psum.170 = f32[2048]{0:T(1024)S(1)} all-reduce(f32[2048]{0:T(1024)S(1)} %get-tuple-element.247), channel_id=1, replica_groups=mesh['row'=8,'col'=16] {'col'}, use_global_device_ids=true, to_apply=%region_9.10 | all-reduce | flops 2048 | bytes 16384 | tf_op jit(solution)/shard_map/psum | solution.py:28
  427.9 29.0 %psum.171 = f32[2048]{0:T(1024)S(1)} all-reduce(f32[2048]{0:T(1024)S(1)} %multiply_reduce_fusion.12), channel_id=1, replica_groups=mesh['row'=8,'col'=16] {'col'}, use_global_device_ids=true, to_apply=%region_11.12 | all-reduce | flops 2048 | bytes 16384 | tf_op jit(solution)/shard_map/psum | solution.py:30
  457.8 28.3 %all-gather.4 = bf16[1,3,64,1024]{3,2,1,0:T(8,128)(2,1)S(1)} all-gather(bf16[1,3,64,128]{3,2,1,0:T(8,128)(2,1)S(1)} %get-tuple-element.220), channel_id=6, replica_groups=mesh['row'=8,'col'=16] {'row'}, dimensions={3}, use_global_device_ids=true | all-gather | bytes 442368 | tf_op jit(solution)/shard_map/all_gather | solution.py:140
  486.1 36.2 %all-gather.25.cloned.1.call-done = bf16[1024,2048]{1,0:T(8,128)(2,1)} async-done(((bf16[64,2048]{1,0:T(8,128)(2,1)}), bf16[1024,2048]{1,0:T(8,128)(2,1)}) %all-gather.25.cloned.1.call-update) | async-done | bytes 4194320 | tf_op jit(solution)/shard_map/all_gather | solution.py:18
  532.5 12.5 all-gather.5
  545.0 38.9 %all-gather.27.cloned.1.call-done = bf16[1024,2048]{1,0:T(8,128)(2,1)} async-done(((bf16[64,2048]{1,0:T(8,128)(2,1)}), bf16[1024,2048]{1,0:T(8,128)(2,1)}) %all-gather.27.cloned.1.call-update) | async-done | bytes 4194320 | tf_op jit(solution)/shard_map/all_gather | solution.py:18
  587.0 32.1 %psum.172 = f32[2048]{0:T(1024)S(1)} all-reduce(f32[2048]{0:T(1024)S(1)} %get-tuple-element.249), channel_id=1, replica_groups=mesh['row'=8,'col'=16] {'col'}, use_global_device_ids=true, to_apply=%region_17.18 | all-reduce | flops 2048 | bytes 16384 | tf_op jit(solution)/shard_map/psum | solution.py:28
  619.1 29.3 %psum.173 = f32[2048]{0:T(1024)S(1)} all-reduce(f32[2048]{0:T(1024)S(1)} %multiply_reduce_fusion.11), channel_id=1, replica_groups=mesh['row'=8,'col'=16] {'col'}, use_global_device_ids=true, to_apply=%region_19.20 | all-reduce | flops 2048 | bytes 16384 | tf_op jit(solution)/shard_map/psum | solution.py:30
  649.4 38.7 %all-gather.6 = bf16[1,256,1024]{2,1,0:T(8,128)(2,1)S(1)} all-gather(bf16[1,256,128]{2,1,0:T(8,128)(2,1)S(1)} %get-tuple-element.218), channel_id=8, replica_groups=mesh['row'=8,'col'=16] {'row'}, dimensions={2}, use_global_device_ids=true | all-gather | bytes 589824 | tf_op jit(solution)/shard_map/all_gather | solution.py:142
  688.0 24.3 %all-gather.29.cloned.1.call-done = bf16[1024,2048]{1,0:T(8,128)(2,1)} async-done(((bf16[64,2048]{1,0:T(8,128)(2,1)}), bf16[1024,2048]{1,0:T(8,128)(2,1)}) %all-gather.29.cloned.1.call-update) | async-done | bytes 4194320 | tf_op jit(solution)/shard_map/all_gather | solution.py:18
  722.5 14.0 all-gather.7
  736.4 106.0 %all-gather.31.cloned.1.call-done = bf16[4096,2048]{0,1:T(8,128)(2,1)} async-done(((bf16[256,2048]{0,1:T(8,128)(2,1)}), bf16[4096,2048]{0,1:T(8,128)(2,1)}) %all-gather.31.cloned.1.call-update) | async-done | bytes 16777232 | tf_op jit(solution)/shard_map/all_gather | solution.py:168
  842.4 11.0 fusion.189
  853.5 31.4 %psum.174 = f32[2048]{0:T(1024)S(1)} all-reduce(f32[2048]{0:T(1024)S(1)} %get-tuple-element.252), channel_id=1, replica_groups=mesh['row'=8,'col'=16] {'col'}, use_global_device_ids=true, to_apply=%region_21.22 | all-reduce | flops 2048 | bytes 16384 | tf_op jit(solution)/shard_map/psum | solution.py:28
  885.0 29.0 %psum.175 = f32[2048]{0:T(1024)S(1)} all-reduce(f32[2048]{0:T(1024)S(1)} %multiply_reduce_fusion.10), channel_id=1, replica_groups=mesh['row'=8,'col'=16] {'col'}, use_global_device_ids=true, to_apply=%region_23.24 | all-reduce | flops 2048 | bytes 16384 | tf_op jit(solution)/shard_map/psum | solution.py:30
  914.8 57.7 %all-reduce.3 = (f32[2048]{0:T(1024)S(1)}, f32[2048]{0:T(1024)S(1)}) all-reduce(f32[2048]{0:T(1024)S(1)} %get-tuple-element.127, f32[2048]{0:T(1024)S(1)} %get-tuple-element.140), channel_id=1, replica_groups=mesh['row'=8,'col'=16] {'col'}, use_global_device_ids=true, to_apply=%region_27.28 | all-reduce | flops 4096 | bytes 32768 | tf_op jit(solution)/shard_map/psum | solution.py:38
  982.2 135.5 %reduce-scatter.33.cloned.1.call-done = bf16[256,2048]{0,1:T(8,128)(2,1)} async-done(((bf16[4096,2048]{0,1:T(8,128)(2,1)}), bf16[256,2048]{0,1:T(8,128)(2,1)}) %reduce-scatter.33.cloned.1.call-update) | async-done | bytes 1048592 | tf_op jit(solution)/shard_map/reduce_scatter | solution.py:219
  1126.3 75.9 %reduce-scatter.35.cloned.1.call-done = bf16[64,2048]{1,0:T(8,128)(2,1)} async-done(((bf16[1024,2048]{1,0:T(8,128)(2,1)}), bf16[64,2048]{1,0:T(8,128)(2,1)}) %reduce-scatter.35.cloned.1.call-update) | async-done | bytes 262160 | tf_op jit(solution)/shard_map/reduce_scatter | solution.py:22
  1205.0 57.9 %all-reduce.2 = (f32[2048]{0:T(1024)S(1)}, f32[2048]{0:T(1024)S(1)}) all-reduce(f32[2048]{0:T(1024)S(1)} %get-tuple-element.125, f32[2048]{0:T(1024)S(1)} %get-tuple-element.136), channel_id=1, replica_groups=mesh['row'=8,'col'=16] {'col'}, use_global_device_ids=true, to_apply=%region_33.34 | all-reduce | flops 4096 | bytes 32768 | tf_op jit(solution)/shard_map/psum | solution.py:38
  1273.3 88.0 %reduce-scatter.49.cloned.1.call-done = bf16[64,2048]{1,0:T(8,128)(2,1)} async-done(((bf16[1024,2048]{1,0:T(8,128)(2,1)}), bf16[64,2048]{1,0:T(8,128)(2,1)}) %reduce-scatter.49.cloned.1.call-update) | async-done | bytes 262160
  1362.9 10.3 while.46
  1380.9 77.1 %reduce-scatter.37.cloned.1.call-done = bf16[64,2048]{1,0:T(8,128)(2,1)} async-done(((bf16[1024,2048]{1,0:T(8,128)(2,1)}), bf16[64,2048]{1,0:T(8,128)(2,1)}) %reduce-scatter.37.cloned.1.call-update) | async-done | bytes 262160 | tf_op jit(solution)/shard_map/reduce_scatter | solution.py:22
  1459.3 57.9 %all-reduce.1 = (f32[2048]{0:T(1024)S(1)}, f32[2048]{0:T(1024)S(1)}) all-reduce(f32[2048]{0:T(1024)S(1)} %get-tuple-element.121, f32[2048]{0:T(1024)S(1)} %get-tuple-element.129), channel_id=1, replica_groups=mesh['row'=8,'col'=16] {'col'}, use_global_device_ids=true, to_apply=%region_42.43 | all-reduce | flops 4096 | bytes 32768 | tf_op jit(solution)/shard_map/psum | solution.py:38
  1526.7 122.4 %reduce-scatter.39.cloned.1.call-done = bf16[256,2048]{0,1:T(8,128)(2,1)} async-done(((bf16[4096,2048]{0,1:T(8,128)(2,1)}), bf16[256,2048]{0,1:T(8,128)(2,1)}) %reduce-scatter.39.cloned.1.call-update) | async-done | bytes 1048592 | tf_op jit(solution)/shard_map/reduce_scatter | solution.py:219
  1657.2 75.9 %reduce-scatter.41.cloned.1.call-done = bf16[64,2048]{1,0:T(8,128)(2,1)} async-done(((bf16[1024,2048]{1,0:T(8,128)(2,1)}), bf16[64,2048]{1,0:T(8,128)(2,1)}) %reduce-scatter.41.cloned.1.call-update) | async-done | bytes 262160 | tf_op jit(solution)/shard_map/reduce_scatter | solution.py:22
  1735.0 57.9 %all-reduce = (f32[2048]{0:T(1024)S(1)}, f32[2048]{0:T(1024)S(1)}) all-reduce(f32[2048]{0:T(1024)S(1)} %get-tuple-element.123, f32[2048]{0:T(1024)S(1)} %get-tuple-element.128), channel_id=1, replica_groups=mesh['row'=8,'col'=16] {'col'}, use_global_device_ids=true, to_apply=%region_48.49 | all-reduce | flops 4096 | bytes 32768 | tf_op jit(solution)/shard_map/psum | solution.py:38
  1849.9 42.9 %reduce-scatter.51.cloned.1.call-done = bf16[64,2048]{1,0:T(8,128)(2,1)} async-done(((bf16[1024,2048]{1,0:T(8,128)(2,1)}), bf16[64,2048]{1,0:T(8,128)(2,1)}) %reduce-scatter.51.cloned.1.call-update) | async-done | bytes 262160
  1894.3 10.3 while.47
  1925.3 31.2 %reduce-scatter.59.cloned.1.call-done = bf16[128,64]{1,0:T(8,128)(2,1)} async-done(((bf16[1024,64]{1,0:T(8,128)(2,1)}), bf16[128,64]{1,0:T(8,128)(2,1)}) %reduce-scatter.59.cloned.1.call-update) | async-done | bytes 16400
  1957.5 31.7 %reduce-scatter.55.cloned.1.call-done = bf16[128,192]{1,0:T(8,128)(2,1)} async-done(((bf16[1024,192]{1,0:T(8,128)(2,1)}), bf16[128,192]{1,0:T(8,128)(2,1)}) %reduce-scatter.55.cloned.1.call-update) | async-done | bytes 49168
  1990.3 31.1 %reduce-scatter.47.cloned.1.call-done = bf16[64,512]{1,0:T(8,128)(2,1)} async-done(((bf16[64,4096]{1,0:T(8,128)(2,1)}), bf16[64,512]{1,0:T(8,128)(2,1)}) %reduce-scatter.47.cloned.1.call-update) | async-done | bytes 65552 | tf_op jit(solution)/shard_map/reduce_scatter | solution.py:278
  2021.4 32.2 %reduce-scatter.45.cloned.1.call-done = bf16[64,512]{1,0:T(8,128)(2,1)} async-done(((bf16[64,4096]{1,0:T(8,128)(2,1)}), bf16[64,512]{1,0:T(8,128)(2,1)}) %reduce-scatter.45.cloned.1.call-update) | async-done | bytes 65552 | tf_op jit(solution)/shard_map/reduce_scatter | solution.py:278
  2055.2 30.6 %reduce-scatter.61.cloned.1.call-done = bf16[128,256]{1,0:T(8,128)(2,1)} async-done(((bf16[1024,256]{1,0:T(8,128)(2,1)}), bf16[128,256]{1,0:T(8,128)(2,1)}) %reduce-scatter.61.cloned.1.call-update) | async-done | bytes 65552
  2087.5 30.1 %reduce-scatter.57.cloned.1.call-done = bf16[128,64]{1,0:T(8,128)(2,1)} async-done(((bf16[1024,64]{1,0:T(8,128)(2,1)}), bf16[128,64]{1,0:T(8,128)(2,1)}) %reduce-scatter.57.cloned.1.call-update) | async-done | bytes 16400
  2119.3 23.6 %all-reduce.4 = (f32[2,2,64]{2,1,0:T(2,128)}, f32[2,64]{1,0:T(2,128)}, f32[2,64]{1,0:T(2,128)}, f32[2,64]{1,0:T(2,128)}, f32[2,256]{1,0:T(2,128)}, /*index=5*/f3...) all-reduce(f32[2,2,64]{2,1,0:T(2,128)S(1)} %pad_maximum_fusion.2, ...), channel_id=1, replica_groups=mesh['row'=8,'col'=16] {'row'}, use_global_device_ids=true, to_apply=%region_60.61 | all-reduce | flops 1536 | bytes 12288 | tf_op jit(solution)/shard_map/psum | solution.py:302
  2151.7 79.6 %reduce-scatter.43.cloned.1.call-done = bf16[64,2048]{1,0:T(8,128)(2,1)} async-done(((bf16[1024,2048]{1,0:T(8,128)(2,1)}), bf16[64,2048]{1,0:T(8,128)(2,1)}) %reduce-scatter.43.cloned.1.call-update) | async-done | bytes 262160 | tf_op jit(solution)/shard_map/reduce_scatter | solution.py:22
  (331 shorter events, 230.9 us)
Async XLA Ops:
  7.2 57.9 %all-gather.17.cloned.1.call-start = ((), (), s32[]{:S(2)}) async-start(), calls=%async_computation.16 | async-start | bytes 4456448 | tf_op jit(solution)/shard_map/all_gather | solution.py:18
  7.9 118.7 %all-gather.19.cloned.1.call-start = ((), (), s32[]{:S(2)}) async-start(), calls=%async_computation.17 | async-start | bytes 4456448 | tf_op jit(solution)/shard_map/all_gather | solution.py:18
  75.2 180.0 %all-gather.21.cloned.1.call-start = ((), (), s32[]{:S(2)}) async-start(), calls=%async_computation.18 | async-start | bytes 4456448 | tf_op jit(solution)/shard_map/all_gather | solution.py:18
  87.8 297.5 %copy-start.35 = (f32[64]{0:T(128)}, f32[64]{0:T(128)S(1)}, u32[]{:S(2)}) copy-start(f32[64]{0:T(128)S(1)} %get-tuple-element.237) | copy-start | bytes 772
  126.6 65.3 %copy-start.46 = (f32[2,256]{1,0:T(2,128)S(1)}, f32[2,256]{1,0:T(2,128)}, u32[]{:S(2)}) copy-start(f32[2,256]{1,0:T(2,128)} %param.30) | copy-start | bytes 6148
  126.6 65.3 %copy-start.31 = (bf16[2,256,128]{2,1,0:T(8,128)(2,1)S(1)}, bf16[2,256,128]{2,1,0:T(8,128)(2,1)}, u32[]{:S(2)}) copy-start(bf16[2,256,128]{2,1,0:T(8,128)(2,1)} %param.29) | copy-start | bytes 393220
  129.8 255.6 %copy-start.2 = (f32[64,2048]{1,0:T(8,128)}, f32[64,2048]{1,0:T(8,128)S(1)}, u32[]{:S(2)}) copy-start(f32[64,2048]{1,0:T(8,128)S(1)} %get-tuple-element.245) | copy-start | bytes 1572868
  161.9 223.5 %copy-start.27 = (f32[2048]{0:T(1024)}, f32[2048]{0:T(1024)S(1)}, u32[]{:S(2)}) copy-start(f32[2048]{0:T(1024)S(1)} %broadcast_multiply_fusion.7) | copy-start | bytes 24580
  191.0 194.4 %copy-start.29 = (f32[2048]{0:T(1024)}, f32[2048]{0:T(1024)S(1)}, u32[]{:S(2)}) copy-start(f32[2048]{0:T(1024)S(1)} %add_rsqrt_fusion.3) | copy-start | bytes 24580
  191.9 193.5 %all-gather.23.cloned.1.call-start = ((), (), s32[]{:S(2)}) async-start(), calls=%async_computation.19 | async-start | bytes 17825792 | tf_op jit(solution)/shard_map/all_gather | solution.py:168
  265.3 257.0 %all-gather.25.cloned.1.call-start = ((), (), s32[]{:S(2)}) async-start(), calls=%async_computation.20 | async-start | bytes 4456448 | tf_op jit(solution)/shard_map/all_gather | solution.py:18
  279.7 116.7 %copy-start.12 = (bf16[1,64,4096]{2,1,0:T(8,128)(2,1)}, bf16[1,64,4096]{2,1,0:T(8,128)(2,1)S(1)}, u32[]{:S(2)}) copy-start(bf16[1,64,4096]{2,1,0:T(8,128)(2,1)S(1)} %all-gather.3) | copy-start | bytes 1572868
  457.8 126.1 %all-gather.27.cloned.1.call-start = ((), (), s32[]{:S(2)}) async-start(), calls=%async_computation.21 | async-start | bytes 4456448 | tf_op jit(solution)/shard_map/all_gather | solution.py:18
  532.5 179.9 %all-gather.29.cloned.1.call-start = ((), (), s32[]{:S(2)}) async-start(), calls=%async_computation.22 | async-start | bytes 4456448 | tf_op jit(solution)/shard_map/all_gather | solution.py:18
  649.3 193.1 %all-gather.31.cloned.1.call-start = ((), (), s32[]{:S(2)}) async-start(), calls=%async_computation.23 | async-start | bytes 17825792 | tf_op jit(solution)/shard_map/all_gather | solution.py:168
  722.4 395.3 %reduce-scatter.33.cloned.1.call-start = ((), (), s32[]{:S(2)}) async-start(), calls=%async_computation.24 | async-start | bytes 17825792 | tf_op jit(solution)/shard_map/reduce_scatter | solution.py:219
  842.4 71.6 %copy-start.16 = (bf16[64,2048]{1,0:T(8,128)(2,1)S(1)}, bf16[64,2048]{1,0:T(8,128)(2,1)}, u32[]{:S(2)}) copy-start(bf16[64,2048]{1,0:T(8,128)(2,1)} %param.35) | copy-start | bytes 786436
  982.2 220.1 %reduce-scatter.35.cloned.1.call-start = ((), (), s32[]{:S(2)}) async-start(), calls=%async_computation.25 | async-start | bytes 4456448 | tf_op jit(solution)/shard_map/reduce_scatter | solution.py:22
  1126.3 235.1 %reduce-scatter.49.cloned.1.call-start = ((), (), s32[]{:S(2)}) async-start(), calls=%async_computation.32 | async-start | bytes 4456448
  1272.9 185.1 %reduce-scatter.37.cloned.1.call-start = ((), (), s32[]{:S(2)}) async-start(), calls=%async_computation.26 | async-start | bytes 4456448 | tf_op jit(solution)/shard_map/reduce_scatter | solution.py:22
  1380.8 137.5 %copy-start.13 = (bf16[1,64,4096]{2,1,0:T(8,128)(2,1)S(1)}, bf16[1,64,4096]{2,1,0:T(8,128)(2,1)}, u32[]{:S(2)}) copy-start(bf16[1,64,4096]{2,1,0:T(8,128)(2,1)} %copy-done.12) | copy-start | bytes 1572868
  1380.8 268.3 %reduce-scatter.39.cloned.1.call-start = ((), (), s32[]{:S(2)}) async-start(), calls=%async_computation.27 | async-start | bytes 17825792 | tf_op jit(solution)/shard_map/reduce_scatter | solution.py:219
  1526.5 206.6 %reduce-scatter.41.cloned.1.call-start = ((), (), s32[]{:S(2)}) async-start(), calls=%async_computation.28 | async-start | bytes 4456448 | tf_op jit(solution)/shard_map/reduce_scatter | solution.py:22
  1657.1 76.0 %copy-start.3 = (f32[64,2048]{1,0:T(8,128)S(1)}, f32[64,2048]{1,0:T(8,128)}, u32[]{:S(2)}) copy-start(f32[64,2048]{1,0:T(8,128)} %copy-done.2) | copy-start | bytes 1572868
  1657.1 76.0 %copy-start.28 = (f32[2048]{0:T(1024)S(1)}, f32[2048]{0:T(1024)}, u32[]{:S(2)}) copy-start(f32[2048]{0:T(1024)} %copy-done.27) | copy-start | bytes 24580
  1657.1 76.0 %copy-start.30 = (f32[2048]{0:T(1024)S(1)}, f32[2048]{0:T(1024)}, u32[]{:S(2)}) copy-start(f32[2048]{0:T(1024)} %copy-done.29) | copy-start | bytes 24580
  1657.1 76.0 %copy-start.36 = (f32[64]{0:T(128)S(1)}, f32[64]{0:T(128)}, u32[]{:S(2)}) copy-start(f32[64]{0:T(128)} %copy-done.35) | copy-start | bytes 772
  1657.1 137.6 %copy-start.25 = (bf16[1,64,1024]{2,1,0:T(8,128)(2,1)S(1)}, bf16[1,64,1024]{2,1,0:T(8,128)(2,1)}, u32[]{:S(2)}) copy-start(bf16[1,64,1024]{2,1,0:T(8,128)(2,1)} %copy-done.24) | copy-start | bytes 393220
  1657.1 235.7 %reduce-scatter.51.cloned.1.call-start = ((), (), s32[]{:S(2)}) async-start(), calls=%async_computation.33 | async-start | bytes 4456448
  1804.5 119.9 %reduce-scatter.63.cloned.1.call-start = ((), (), s32[]{:S(2)}) async-start(), calls=%async_computation.39 | async-start | bytes 589824
  1810.2 146.3 %reduce-scatter.59.cloned.1.call-start = ((), (), s32[]{:S(2)}) async-start(), calls=%async_computation.37 | async-start | bytes 294912
  1814.8 174.4 %reduce-scatter.55.cloned.1.call-start = ((), (), s32[]{:S(2)}) async-start(), calls=%async_computation.35 | async-start | bytes 589824
  1820.7 200.7 %reduce-scatter.47.cloned.1.call-start = ((), (), s32[]{:S(2)}) async-start(), calls=%async_computation.31 | async-start | bytes 589824 | tf_op jit(solution)/shard_map/reduce_scatter | solution.py:278
  1830.4 223.1 %reduce-scatter.45.cloned.1.call-start = ((), (), s32[]{:S(2)}) async-start(), calls=%async_computation.30 | async-start | bytes 589824 | tf_op jit(solution)/shard_map/reduce_scatter | solution.py:278
  1840.5 245.2 %reduce-scatter.61.cloned.1.call-start = ((), (), s32[]{:S(2)}) async-start(), calls=%async_computation.38 | async-start | bytes 589824
  1845.2 272.4 %reduce-scatter.57.cloned.1.call-start = ((), (), s32[]{:S(2)}) async-start(), calls=%async_computation.36 | async-start | bytes 294912
  1849.9 300.1 %reduce-scatter.53.cloned.1.call-start = ((), (), s32[]{:S(2)}) async-start(), calls=%async_computation.34 | async-start | bytes 589824
  1913.5 317.8 %reduce-scatter.43.cloned.1.call-start = ((), (), s32[]{:S(2)}) async-start(), calls=%async_computation.29 | async-start | bytes 4456448 | tf_op jit(solution)/shard_map/reduce_scatter | solution.py:22
  1917.7 72.5 %copy-start.47 = (f32[64]{0:T(128)S(1)}, f32[64]{0:T(128)}, u32[]{:S(2)}) copy-start(f32[64]{0:T(128)} %get-tuple-element.126) | copy-start | bytes 772
  1917.7 72.5 %copy-start.48 = (f32[64]{0:T(128)S(1)}, f32[64]{0:T(128)}, u32[]{:S(2)}) copy-start(f32[64]{0:T(128)} %get-tuple-element.141) | copy-start | bytes 772
  1917.7 137.4 %copy-start.38 = (f32[256]{0:T(256)S(1)}, f32[256]{0:T(256)}, u32[]{:S(2)}) copy-start(f32[256]{0:T(256)} %get-tuple-element.198) | copy-start | bytes 3076
  1917.8 169.7 %copy-start.39 = (f32[64]{0:T(128)S(1)}, f32[64]{0:T(128)}, u32[]{:S(2)}) copy-start(f32[64]{0:T(128)} %get-tuple-element.194) | copy-start | bytes 772
  1917.8 169.7 %copy-start.41 = (f32[64]{0:T(128)S(1)}, f32[64]{0:T(128)}, u32[]{:S(2)}) copy-start(f32[64]{0:T(128)} %get-tuple-element.139) | copy-start | bytes 772
  1917.8 169.7 %copy-start.43 = (f32[64]{0:T(128)S(1)}, f32[64]{0:T(128)}, u32[]{:S(2)}) copy-start(f32[64]{0:T(128)} %get-tuple-element.131) | copy-start | bytes 772
  1917.8 169.7 %copy-start.44 = (f32[64]{0:T(128)S(1)}, f32[64]{0:T(128)}, u32[]{:S(2)}) copy-start(f32[64]{0:T(128)} %get-tuple-element.138) | copy-start | bytes 772
  1917.8 169.7 %copy-start.40 = (f32[64]{0:T(128)S(1)}, f32[64]{0:T(128)}, u32[]{:S(2)}) copy-start(f32[64]{0:T(128)} %get-tuple-element.124) | copy-start | bytes 772
  1917.8 169.7 %copy-start.42 = (f32[64]{0:T(128)S(1)}, f32[64]{0:T(128)}, u32[]{:S(2)}) copy-start(f32[64]{0:T(128)} %get-tuple-element.122) | copy-start | bytes 772
  1917.8 169.7 %copy-start.45 = (f32[64]{0:T(128)S(1)}, f32[64]{0:T(128)}, u32[]{:S(2)}) copy-start(f32[64]{0:T(128)} %get-tuple-element.200) | copy-start | bytes 772
  (31 other events, 651.8 us)
Sparse Core Ops, SparseCore 0:
  10.2 54.8 all-gather.16
  75.4 51.2 all-gather.18
  192.0 63.1 all-gather.20
  265.5 119.8 all-gather.22
  457.9 64.4 all-gather.24
  532.6 51.2 all-gather.26
  649.5 62.8 all-gather.28
  722.5 119.8 all-gather.30
  982.3 135.3 reduce-scatter.32
  1126.4 75.8 reduce-scatter.34
  1273.0 88.3 reduce-scatter.48
  1380.9 76.9 reduce-scatter.36
  1526.6 122.4 reduce-scatter.38
  1657.2 75.8 reduce-scatter.40
  1804.6 88.1 reduce-scatter.50
  1895.1 29.1 reduce-scatter.62
  1927.1 29.3 reduce-scatter.58
  1959.4 29.7 reduce-scatter.54
  1991.6 29.7 reduce-scatter.46
  2023.7 29.8 reduce-scatter.44
  2056.0 29.7 reduce-scatter.60
  2088.2 29.3 reduce-scatter.56
  2120.0 29.8 reduce-scatter.52
  2153.5 77.7 reduce-scatter.42
where the time goes:
time: 2250 us; the launch traced here: 2240 us
  waiting for transfers between devices  1330 us (59%)
  blocking collectives  660 us (29%)
  matrix products  156 us (7%)
  local copies, waits for them, and re-layouts  45.8 us (2%)
  other arithmetic  34.8 us (2%)
    reduce_scatter x4, waiting for transfers between devices, collect(): lax.psum_scatter(values.astype(jnp.bfloat16), 'col', scatter_dimension=0,...  309 us
    unnamed x32, waiting for transfers between devices  269 us
    reduce_scatter x2, waiting for transfers between devices, on_device(): lax.psum_scatter(jnp.einsum('df,dt->ft', weights[3], grad_lower, preferre...  258 us
    psum x4, blocking collectives, norm_backward(): lax.psum((jnp.sum(grad_norm, axis=0), jnp.sum(grad_norm * normed, axis=0)...  231 us
    all_gather x6, waiting for transfers between devices, spread(): return lax.all_gather(values, 'col', axis=0, tiled=True)  215 us
    all_gather x2, waiting for transfers between devices, on_device(): lax.all_gather(activated.astype(jnp.bfloat16), 'col', axis=0, tiled=True)  212 us
    psum x4, blocking collectives, norm_forward(): centre = lax.psum(jnp.sum(summed, axis=0), 'col') / D  127 us
    psum x4, blocking collectives, norm_forward(): variance = lax.psum(jnp.sum(centred * centred, axis=0), 'col') / D  116 us
  transfers between devices with their start and end apart: 24, of which 24 were waited for; matrix products, arithmetic and copies ran while one was open for 4% of the time, Pallas kernels for 0%

commit v1 on v0

v1 whole, which is shorter than its diff:
```python
import jax
import jax.numpy as jnp
from jax import lax
from jax.sharding import Mesh, PartitionSpec as P

HEAD = 64
D = 1024
LAYERS = 2
SEQ_LEN = 1024
epsilon = 1e-05

CORE = "k"
Y = ("y",)
X = ("xh", "xl")
Z = ("zh", "zl")
COL = X + Z
CHIPS = Y + COL
SEQ = ("xl", "zh", "zl")
bf16 = jnp.bfloat16
f32 = jnp.float32


def dot(a, b, ca, cb):
    return lax.dot_general(a, b, (((ca,), (cb,)), ((), ())), preferred_element_type=f32)


def core_gather(values):
    return lax.all_gather(values, CORE, axis=1, tiled=True)


def core_reduce(part):
    me = lax.axis_index(CORE)
    halves = part.reshape(part.shape[0], 2, part.shape[1] // 2)
    keep = jnp.where(me == 0, halves[:, 0], halves[:, 1])
    send = jnp.where(me == 0, halves[:, 1], halves[:, 0]).astype(bf16)
    return keep + lax.ppermute(send, CORE, [(0, 1), (1, 0)]).astype(f32)


def trade(values):
    return lax.ppermute(values, (CORE, "zh"), [(0, 0), (1, 2), (2, 1), (3, 3)])


def pick(values, index, dim):
    return lax.dynamic_index_in_dim(values, index, dim, keepdims=False)


def scatter_axis(chunk_of, axes):
    me = lax.axis_index(axes)
    total = chunk_of(me).astype(f32)
    for shift in (1, 3, 2):
        sent = chunk_of((me + shift) % 4)
        total += lax.ppermute(sent, axes, [(i, (i + shift) % 4) for i in range(4)]).astype(f32)
    return total


def sum_axis(values, axes):
    total = values
    for shift in (1, 3, 2):
        total += lax.ppermute(values, axes, [(i, (i + shift) % 4) for i in range(4)])
    return total


def reduce_down(g):
    g = g.reshape(4, 4, 64, 4, 512)
    g = scatter_axis(lambda i: pick(g, i, 3), Y).astype(bf16)
    h = scatter_axis(lambda i: pick(g, i, 1), Z).astype(bf16)
    return scatter_axis(lambda i: pick(h, i, 0), X)


def reduce_up(g):
    g = g.reshape(4, 512, 1024)
    h = scatter_axis(lambda i: pick(g, i, 0), X).astype(bf16)
    h = h.reshape(512, 4, 256)
    q = scatter_axis(lambda i: pick(h, i, 1), Y).astype(bf16)
    q = q.reshape(2, 256, 2, 128).transpose(2, 0, 1, 3).reshape(4, 256, 128)
    return scatter_axis(lambda i: pick(q, i, 0), Z)


def reduce_qo(g_qkv, g_out):
    g_qkv = g_qkv.reshape(3, 4, 2, 64, 4, 2, 128)
    g_out = g_out.reshape(4, 4, 64, 4, 128)

    def chunk(i):
        a = pick(pick(g_qkv, i // 2, 5), i % 2, 2)
        b = pick(g_out, i, 1)
        return jnp.concatenate([a, b[None]], axis=0)

    h = scatter_axis(chunk, Z).astype(bf16)
    h2 = scatter_axis(lambda i: pick(h, i, 1), X).astype(bf16)
    return scatter_axis(lambda i: pick(h2, i, 2), Y)


def norm_forward(summed, gain, shift):
    centre = jnp.mean(summed, axis=0, keepdims=True)
    centred = summed - centre
    variance = jnp.mean(centred * centred, axis=0, keepdims=True)
    scaled = lax.rsqrt(variance + epsilon)
    normed = centred * scaled
    return normed * gain[:, None] + shift[:, None], normed, scaled


def norm_backward(incoming, normed, scaled, gain):
    grad_norm = incoming * gain[:, None]
    plain = jnp.mean(grad_norm, axis=0, keepdims=True)
    cross = jnp.mean(grad_norm * normed, axis=0, keepdims=True)
    return scaled * (grad_norm - plain - normed * cross)


def to_heads(values, kinds):
    v = values.reshape(kinds, 4, 128, 2, 128).transpose(3, 1, 0, 2, 4)
    v = v.reshape(8, kinds * 128, 128)
    v = lax.all_to_all(v, SEQ, 0, 2, tiled=True)
    return v.reshape(kinds, 2, HEAD, SEQ_LEN)


def to_tokens(values, kinds):
    v = values.reshape(kinds * 128, 8, 128).transpose(1, 0, 2)
    v = lax.all_to_all(v, SEQ, 0, 0, tiled=True)
    v = v.reshape(2, 4, kinds, 128, 128).transpose(2, 1, 3, 0, 4)
    return v.reshape(kinds * 512, 256)


def attend_forward(packed):
    factor = HEAD ** (-0.5)
    scores = jnp.einsum("hcq,hck->hqk", packed[0], packed[1], preferred_element_type=f32) * factor
    highest = jnp.max(scores, axis=-1, keepdims=True)
    exps = jnp.exp(scores - highest)
    total = jnp.sum(exps, axis=-1, keepdims=True)
    low = (exps / total).astype(bf16)
    blended = jnp.einsum("hqk,hck->hcq", low, packed[2], preferred_element_type=f32)
    return blended.astype(bf16).reshape(128, SEQ_LEN), (highest + jnp.log(total))[..., 0]


def attend_backward(packed, logsum, grad):
    factor = HEAD ** (-0.5)
    queries, keys, values = packed[0], packed[1], packed[2]
    scores = jnp.einsum("hcq,hck->hqk", queries, keys, preferred_element_type=f32) * factor
    probs = jnp.exp(scores - logsum[..., None])
    grad_probs = jnp.einsum("hcq,hck->hqk", grad, values, preferred_element_type=f32)
    grad_values = jnp.einsum("hqk,hcq->hck", probs.astype(bf16), grad, preferred_element_type=f32)
    grad_scores = probs * (grad_probs - jnp.sum(probs * grad_probs, axis=-1, keepdims=True))
    grad_scores = grad_scores.astype(bf16)
    grad_queries = jnp.einsum("hqk,hck->hcq", grad_scores, keys, preferred_element_type=f32) * factor
    grad_keys = jnp.einsum("hqk,hcq->hck", grad_scores, queries, preferred_element_type=f32) * factor
    return jnp.stack([grad_queries, grad_keys, grad_values]).astype(bf16)


def on_device(
    tokens,
    w_qkv,
    bias_qv,
    w_out,
    bias_out,
    gain_attn,
    shift_attn,
    w_up,
    bias_up,
    w_down,
    bias_down,
    gain_ffn,
    shift_ffn,
    cotangent,
):
    core = lax.axis_index(CORE)
    traded = trade(
        jnp.concatenate([w_qkv.reshape(LAYERS, 192, 128), w_up.reshape(LAYERS, 256, 128)], axis=1)
    )
    pack = jnp.concatenate(
        [
            traded,
            w_out,
            w_down.reshape(LAYERS, 64, 4, 128).transpose(0, 2, 1, 3).reshape(LAYERS, 256, 128),
        ],
        axis=1,
    )
    every = lax.all_gather(pack, CHIPS, axis=0, tiled=False).reshape(4, 4, 2, 2, LAYERS, 768, 128)
    weights = []
    for l in range(LAYERS):
        e = every[:, :, :, :, l]
        wq = e[..., :192, :].reshape(4, 4, 2, 2, 3, 64, 128)
        wq = wq.transpose(4, 1, 3, 5, 0, 2, 6).reshape(1536, 1024)
        wu = e[..., 192:448, :].transpose(1, 3, 4, 0, 2, 5).reshape(2048, 1024)
        wo = e[..., 448:512, :].transpose(1, 2, 3, 4, 0, 5).reshape(1024, 512)
        wd = e[..., 512:, :].reshape(4, 4, 2, 2, 4, 64, 128)
        wd = wd.transpose(1, 2, 3, 5, 0, 4, 6).reshape(1024, 2048)
        weights.append((wq, wo, wu, wd))

    small = jnp.concatenate(
        [
            v.reshape(-1)
            for v in (bias_qv, bias_out, gain_attn, shift_attn, bias_down, gain_ffn, shift_ffn, bias_up)
        ]
    )
    small = lax.all_to_all(
        jnp.broadcast_to(small[None], (16, small.shape[0])), COL, 0, 0, tiled=True
    )
    b_qv = small[:, :256].reshape(4, 2, 2, LAYERS, 2, 64)
    b_qv = pick(b_qv, core, 1).transpose(2, 3, 0, 1, 4).reshape(LAYERS, 2, 512)
    features = small[:, 256:1024].reshape(16, 6, LAYERS, 64).transpose(1, 2, 0, 3).reshape(6, LAYERS, D)
    b_out, g_attn, s_attn, b_down, g_ffn, s_ffn = features
    b_up = small[:, 1024:].reshape(4, 2, 2, LAYERS, 256)
    b_up = pick(b_up, core, 1).transpose(2, 0, 1, 3).reshape(LAYERS, 2048)

    stream = lax.all_to_all(tokens, COL, 1, 0, tiled=True).astype(f32)
    back = lax.all_to_all(cotangent, COL, 1, 0, tiled=True).astype(f32)
    stored = []
    for l in range(LAYERS):
        wq, wo, wu, wd = weights[l]
        seen = core_gather(stream.astype(bf16))
        bias = jnp.concatenate([b_qv[l, 0], jnp.zeros((512,), f32), b_qv[l, 1]])
        qkv = (dot(wq, seen, 1, 0) + bias[:, None]).astype(bf16)
        packed = to_heads(qkv, 3)
        blended, logsum = attend_forward(packed)
        blended = to_tokens(blended, 1)
        attn_out = core_reduce(dot(wo, blended, 1, 0)) + b_out[l][:, None]
        first, n_attn, i_attn = norm_forward(stream + attn_out, g_attn[l], s_attn[l])
        first_seen = core_gather(first.astype(bf16))
        upper = dot(wu, first_seen, 1, 0) + b_up[l][:, None]
        active = jax.nn.gelu(upper, approximate=False).astype(bf16)
        lower = core_reduce(dot(wd, active, 1, 0)) + b_down[l][:, None]
        stream, n_ffn, i_ffn = norm_forward(first + lower, g_ffn[l], s_ffn[l])
        stored.append(
            (seen, packed, logsum, blended, n_attn, i_attn, first_seen, upper, active, n_ffn, i_ffn)
        )
    result = lax.all_to_all(stream.astype(bf16), COL, 0, 1, tiled=True)

    big = [None] * LAYERS
    minor = [None] * LAYERS
    for l in reversed(range(LAYERS)):
        wq, wo, wu, wd = weights[l]
        (seen, packed, logsum, blended, n_attn, i_attn, first_seen, upper, active, n_ffn, i_ffn) = stored[l]
        grad_sum = norm_backward(back, n_ffn, i_ffn, g_ffn[l])
        p_gain_ffn = jnp.sum(back * n_ffn, axis=1)
        p_shift_ffn = jnp.sum(back, axis=1)
        low = grad_sum.astype(bf16)
        p_down = jnp.sum(low.astype(f32), axis=1)
        low = core_gather(low)
        gw_down = reduce_down(dot(low, active, 1, 1).astype(bf16))
        grad_active = dot(wd, low, 0, 0)
        _, gelu_back = jax.vjp(lambda v: jax.nn.gelu(v, approximate=False), upper)
        grad_upper = gelu_back(grad_active)[0].astype(bf16)
        p_up = jnp.sum(grad_upper.astype(f32), axis=1)
        gw_up = reduce_up(dot(grad_upper, first_seen, 1, 1).astype(bf16))
        grad_first = core_reduce(dot(wu, grad_upper, 0, 0)) + grad_sum
        p_gain_attn = jnp.sum(grad_first * n_attn, axis=1)
        p_shift_attn = jnp.sum(grad_first, axis=1)
        grad_total = norm_backward(grad_first, n_attn, i_attn, g_attn[l])
        low = grad_total.astype(bf16)
        p_out = jnp.sum(low.astype(f32), axis=1)
        low = core_gather(low)
        g_out = dot(low, blended, 1, 1).astype(bf16)
        grad_blended = to_heads(dot(wo, low, 0, 0).astype(bf16), 1)[0]
        grad_qkv = attend_backward(packed, logsum, grad_blended)
        grad_qkv = to_tokens(grad_qkv.reshape(384, SEQ_LEN), 3)
        p_qkv = jnp.sum(grad_qkv.astype(f32).reshape(3, 512, 256), axis=2)
        g_qkv = dot(grad_qkv, seen, 1, 1).astype(bf16)
        gw_qo = reduce_qo(g_qkv, g_out)
        back = core_reduce(dot(wq, grad_qkv, 0, 0)) + grad_total
        swapped = trade(jnp.concatenate([gw_qo[:3].reshape(192, 128), gw_up], axis=0).astype(bf16))
        swapped = swapped.astype(f32)
        big[l] = (swapped[:192].reshape(3, 64, 128), gw_qo[3], swapped[192:], gw_down)
        minor[l] = (p_qkv, p_out, p_gain_attn, p_shift_attn, p_down, p_gain_ffn, p_shift_ffn, p_up)
    grad_tokens = lax.all_to_all(back.astype(bf16), COL, 0, 1, tiled=True).astype(f32)

    mine = (jnp.arange(2) == core).astype(f32)
    qv = jnp.stack([jnp.stack([m[0][0], m[0][2]]) for m in minor])
    qv = qv.reshape(LAYERS, 2, 4, 2, 64).transpose(2, 3, 0, 1, 4)
    qv = (qv[:, None] * mine[None, :, None, None, None, None]).reshape(16, 256)
    up = jnp.stack([m[7] for m in minor]).reshape(LAYERS, 4, 2, 256).transpose(1, 2, 0, 3)
    up = (up[:, None] * mine[None, :, None, None, None]).reshape(16, 512)
    feats = jnp.stack([jnp.stack([m[i] for m in minor]) for i in range(1, 7)])
    feats = feats.reshape(6, LAYERS, 16, 64).transpose(2, 0, 1, 3).reshape(16, 768)
    sums = jnp.concatenate([qv, feats, up], axis=1).reshape(4, 4, 12, 128)
    sums = scatter_axis(lambda i: pick(sums, i, 0), X)
    sums2 = scatter_axis(lambda i: pick(sums, i, 0), Z)
    sums2 = sum_axis(sums2, Y)
    sums2 = sums2 + lax.ppermute(sums2, CORE, [(0, 1), (1, 0)])
    flat = sums2.reshape(1536)
    o_qv = flat[:256].reshape(LAYERS, 2, 64)
    o_out, o_gain_attn, o_shift_attn, o_down, o_gain_ffn, o_shift_ffn = flat[256:1024].reshape(6, LAYERS, 64)
    o_up = flat[1024:].reshape(LAYERS, 256)
    gw_qkv, gw_out, gw_up, gw_down = [jnp.stack([b[i] for b in big]) for i in range(4)]
    return (
        result,
        grad_tokens,
        gw_qkv,
        o_qv,
        gw_out,
        o_out,
        o_gain_attn,
        o_shift_attn,
        gw_up,
        o_up,
        gw_down,
        o_down,
        o_gain_ffn,
        o_shift_ffn,
    )


def solution(mesh):
    fine = Mesh(mesh.devices.reshape(4, 2, 2, 2, 2, 2), ("y", "k", "xh", "xl", "zh", "zl"))
    row = ("y", "k")
    col = COL
    in_specs = (
        P(col, row),
        P(None, None, col, row),
        P(None, None, col),
        P(None, col, row),
        P(None, col),
        P(None, col),
        P(None, col),
        P(None, col, row),
        P(None, col),
        P(None, col, row),
        P(None, col),
        P(None, col),
        P(None, col),
        P(col, row),
    )
    out_specs = (
        P(col, row),
        P(col, row),
        P(None, None, col, row),
        P(None, None, col),
        P(None, col, row),
        P(None, col),
        P(None, col),
        P(None, col),
        P(None, col, row),
        P(None, col),
        P(None, col, row),
        P(None, col),
        P(None, col),
        P(None, col),
    )
    return jax.shard_map(
        on_device, mesh=fine, in_specs=in_specs, out_specs=out_specs, check_vma=False
    )
```

time: 2250 us -> 1010 us (0.45)
  waiting for transfers between devices: 1330 us -> 260 us
  blocking collectives: 660 us -> 28.1 us
  local copies, waits for them, and re-layouts: 45.8 us -> 342 us
  starting transfers between devices: 1.79 us -> 184 us
  matrix products: 156 us -> 78.2 us
  other arithmetic: 34.8 us -> 87.4 us
    reduce_scatter x8 -> x0, waiting for transfers between devices: 630 us -> none  [the longest x4 309 us: collect(): lax.psum_scatter(values.astype(jnp.bfloat16), 'col', scatter_dimension=0,...]
    psum x13 -> x0, blocking collectives: 498 us -> none  [the longest x4 231 us: norm_backward(): lax.psum((jnp.sum(grad_norm, axis=0), jnp.sum(grad_norm * normed, axis=0)...]
    all_gather x8 -> x1, waiting for transfers between devices: 427 us -> 97 us  [on_device(): lax.all_gather(pack, CHIPS, axis=0, tiled=False)]
    unnamed x32 -> x1, waiting for transfers between devices: 269 us -> 0.02 us
    all_gather x8, blocking collectives: 162 us -> 28.1 us  [core_gather(): return lax.all_gather(values, CORE, axis=1, tiled=True)]
    reshape x6 -> x46, local copies, waits for them, and re-layouts: 1.94 us -> 132 us  [the longest x4 31.3 us: on_device(): wd = wd.transpose(1, 2, 3, 5, 0, 4, 6).reshape(1024, 2048)]
    ppermute x0 -> x75, starting transfers between devices: none -> 126 us  [the longest x60 75.6 us: scatter_axis(): lax.ppermute(sent, axes, [(i, (i + shift) % 4) for i in range(4)])]
    ppermute x0 -> x75, waiting for transfers between devices: none -> 114 us  [the longest x60 108 us: scatter_axis(): lax.ppermute(sent, axes, [(i, (i + shift) % 4) for i in range(4)])]
  transfers between devices with their start and end apart: 24 -> 89, of which waited for: 24 -> 26; matrix products, arithmetic and copies ran while one was open for 4% -> 42% of each run, Pallas kernels for 0% -> 0%
where the time goes in v1:
time: 1010 us; the launch traced here: 997 us
  local copies, waits for them, and re-layouts  342 us (34%)
  waiting for transfers between devices  260 us (26%)
  starting transfers between devices  184 us (18%)
  other arithmetic  87.4 us (9%)
  matrix products  78.2 us (8%)
  blocking collectives  28.1 us (3%)
  between operations  17.5 us (2%)
    ppermute x60, waiting for transfers between devices, scatter_axis(): lax.ppermute(sent, axes, [(i, (i + shift) % 4) for i in range(4)])  108 us
    all_gather x1, waiting for transfers between devices, on_device(): lax.all_gather(pack, CHIPS, axis=0, tiled=False)  97 us
    dynamic_slice x38, local copies, waits for them, and re-layouts, pick(): return lax.dynamic_index_in_dim(values, index, dim, keepdims=False)  82.6 us
    ppermute x60, starting transfers between devices, scatter_axis(): lax.ppermute(sent, axes, [(i, (i + shift) % 4) for i in range(4)])  75.6 us
    dot_general x24, matrix products, dot(): lax.dot_general(a, b, (((ca,), (cb,)), ((), ())), preferred_element_type=...  54.1 us
    transpose x3, local copies, waits for them, and re-layouts, on_device(): wu = e[..., 192:448, :].transpose(1, 3, 4, 0, 2, 5).reshape(2048, 1024)  34.6 us
    reshape x4, local copies, waits for them, and re-layouts, on_device(): wd = wd.transpose(1, 2, 3, 5, 0, 4, 6).reshape(1024, 2048)  31.3 us
    reshape x4, local copies, waits for them, and re-layouts, on_device(): wu = e[..., 192:448, :].transpose(1, 3, 4, 0, 2, 5).reshape(2048, 1024)  31.2 us
  transfers between devices with their start and end apart: 89, of which 26 were waited for; matrix products, arithmetic and copies ran while one was open for 42% of the time, Pallas kernels for 0%

profile of v1, /device:TPU:1, one launch (start us, length us, event | category | flops | bytes accessed | tf_op | source)
XLA Modules:
  0.0 997.0 jit_solution(5857764311229294167)
XLA Ops:
  8.3 6.9 collective-permute-start
  32.6 5.9 all-to-all-done.1
  42.3 7.4 all-to-all-done
  49.6 7.0 all_gather.32
  56.6 97.0 %all-gather.3.cloned.1.call-done = bf16[128,768,128]{2,1,0:T(8,128)(2,1)} async-done(((bf16[2,768,128]{2,1,0:T(8,128)(2,1)}), bf16[128,768,128]{2,1,0:T(8,128)(2,1)}) %all-gather.3.cloned.1.call-update) | async-done | bytes 25165840 | tf_op jit(solution)/shard_map/all_gather | solution.py:176
  153.6 15.2 %slice_bitcast_fusion.1 = (bf16[4,4,2,2,768,128]{5,4,3,2,1,0:T(8,128)(2,1)S(1)}, bf16[4,4,2,2,768,128]{5,4,3,2,1,0:T(8,128)(2,1)}) fusion(bf16[4,4,2,2,2,768,128]{6,5,4,3,2,1,0:T(8,128)(2,1)} %bitcast.839), kind=kLoop, calls=%fused_computation.1 | loop fusion | bytes 50331648 | tf_op jit(solution)/shard_map/squeeze | solution.py:179
  185.0 5.4 all-to-all-start.2
  191.1 10.7 %all-to-all-done.2 = bf16[8,384,128]{2,1,0:T(8,128)(2,1)S(1)} async-done(((bf16[8,384,128]{2,1,0:T(8,128)(2,1)}), bf16[8,384,128]{2,1,0:T(8,128)(2,1)S(1)}, u32[]{:S(2)}, u32[]{:S(2)}) %all-to-all-start.2) | async-done | bytes 786464 | tf_op jit(solution)/shard_map/all_to_all | solution.py:112
  223.6 12.2 %slice_bitcast_fusion.2 = (bf16[4,2,256,4,2,128]{5,2,1,4,0,3:T(8,128)(2,1)}, bf16[4,4,2,2,256,128]{5,4,3,2,1,0:T(8,128)(2,1)}, bf16[4,4,2,2,256,128]{5,4,3,2,1,0:T(8,128)(2,1)}, bf16[4,2,256,4,2,128]{5,2,1,4,0,3:T(8,128)(2,1)}) fusion(bf16[4,4,2,2,768,128]{5,4,3,2,1,0:T(8,128)(2,1)} %get-tuple-element.78, bf16[4,4,2,2,768,128]{5,4,3,2,1,0:T(8,128)(2,1)} %copy-done.4), kind=kLoop, calls=%fused_computation.18 | loop fusion | bytes 33554432 | tf_op jit(solution)/shard_map/transpose | solution.py:182
  235.8 11.2 %copy.720 = bf16[4,2,256,4,2,128]{2,1,0,5,4,3:T(2,128)(2,1)} copy(bf16[4,2,256,4,2,128]{5,2,1,4,0,3:T(8,128)(2,1)} %get-tuple-element.192) | data formatting | bytes 8388608 | tf_op jit(solution)/shard_map/transpose | solution.py:182
  247.1 7.8 reshape.672
  254.8 7.8 copy.928
  262.6 7.8 reshape.733
  273.5 7.1 fusion.49
  284.7 4.9 copy.722
  289.6 6.1 reshape.676
  306.9 11.2 %all-to-all-done.4 = bf16[8,384,128]{2,1,0:T(8,128)(2,1)S(1)} async-done(((bf16[8,384,128]{2,1,0:T(8,128)(2,1)}), bf16[8,384,128]{2,1,0:T(8,128)(2,1)S(1)}, u32[]{:S(2)}, u32[]{:S(2)}) %all-to-all-start.4) | async-done | bytes 786464 | tf_op jit(solution)/shard_map/all_to_all | solution.py:112
  349.1 7.7 copy.927
  356.8 7.8 reshape.735
  364.6 7.8 reshape.682
  372.4 11.2 %copy.731 = bf16[4,2,256,4,2,128]{2,1,0,5,4,3:T(2,128)(2,1)} copy(bf16[4,2,256,4,2,128]{5,2,1,4,0,3:T(8,128)(2,1)} %get-tuple-element.81) | data formatting | bytes 8388608 | tf_op jit(solution)/shard_map/transpose | solution.py:182
  383.6 7.8 reshape.683
  391.4 7.8 reshape.736
  399.2 7.8 reshape.671
  407.0 7.8 reshape.738
  420.6 6.3 fusion.47
  438.4 5.8 convert_reduce_fusion
  447.6 7.9 reshape.711
  455.5 14.9 %constant_dynamic-slice_fusion.3 = (bf16[4,4,64,1,512]{4,3,2,1,0:T(2,128)(2,1)S(1)}, bf16[4,4,64,1,512]{4,3,2,1,0:T(2,128)(2,1)S(1)}, bf16[4,4,64,1,512]{4,3,2,1,0:T(2,128)(2,1)S(1)}, bf16[4,4,64,1,512]{4,3,2,1,0:T(2,128)(2,1)S(1)}) fusion(bf16[4,4,64,4,512]{4,3,2,1,0:T(4,128)(2,1)} %reshape.711, s32[]{:T(128)S(6)} %select_n.516, s32[]{:T(128)S(6)} %select_n.522, ...), kind=kLoop, calls=%fused_computation.424 | loop fusion | bytes 8388624 | tf_op jit(solution)/shard_map/jit(dynamic_index_in_dim)/dynamic_slice | solution.py:44
  517.5 5.4 all-to-all-start.6
  524.2 5.2 multiply_reduce_fusion.1
  553.5 8.4 collective-permute-done.39
  582.7 7.3 constant_dynamic-slice_fusion.23
  601.2 8.1 collective-permute-start.6
  616.3 21.6 %collective-permute-done.43 = bf16[256,128]{1,0:T(8,128)(2,1)S(1)} collective-permute-done((bf16[256,128]{1,0:T(8,128)(2,1)S(1)}, bf16[256,128]{1,0:T(8,128)(2,1)S(1)}, u32[]{:S(2)}, u32[]{:S(2)}) %collective-permute-start.43) | collective-permute-done | bytes 65568 | tf_op jit(solution)/shard_map/ppermute | solution.py:52
  658.5 5.8 convert_reduce_fusion.1
  667.6 7.8 reshape.710
  675.4 15.2 %constant_dynamic-slice_fusion.7 = (bf16[4,4,64,1,512]{4,3,2,1,0:T(2,128)(2,1)S(1)}, bf16[4,4,64,1,512]{4,3,2,1,0:T(2,128)(2,1)S(1)}, bf16[4,4,64,1,512]{4,3,2,1,0:T(2,128)(2,1)S(1)}, bf16[4,4,64,1,512]{4,3,2,1,0:T(2,128)(2,1)S(1)}) fusion(bf16[4,4,64,4,512]{4,3,2,1,0:T(4,128)(2,1)} %reshape.710, s32[]{:T(128)S(6)} %select_n.516, s32[]{:T(128)S(6)} %select_n.522, ...), kind=kLoop, calls=%fused_computation.428 | loop fusion | bytes 8388624 | tf_op jit(solution)/shard_map/jit(dynamic_index_in_dim)/dynamic_slice | solution.py:44
  747.3 5.0 multiply_reduce_fusion
  771.0 5.0 all-to-all-start.11
  776.1 9.2 collective-permute-done.59
  787.1 27.1 %collective-permute-done.31 = bf16[4,64,4,128]{3,1,0,2:T(8,128)(2,1)} collective-permute-done((bf16[4,64,4,128]{3,1,0,2:T(8,128)(2,1)}, bf16[4,64,4,128]{3,1,0,2:T(8,128)(2,1)}, u32[]{:S(2)}, u32[]{:S(2)}) %collective-permute-start.31) | collective-permute-done | bytes 262176 | tf_op jit(solution)/shard_map/ppermute | solution.py:52
  823.2 5.2 collective-permute-done.33
  850.3 8.5 constant_dynamic-slice_fusion.35
  881.8 11.4 %collective-permute-start.46 = (bf16[448,128]{1,0:T(8,128)(2,1)S(1)}, bf16[448,128]{1,0:T(8,128)(2,1)S(1)}, u32[]{:S(2)}, u32[]{:S(2)}) collective-permute-start(bf16[448,128]{1,0:T(8,128)(2,1)S(1)} %copy-done.101), channel_id=1, source_target_pairs={{0,0},{2,16},{16,2},{18,18},{1,1},{3,17},{17,3},{19,19},{4,4},{6,2... | collective-permute-start | bytes 344072 | tf_op jit(solution)/shard_map/ppermute | solution.py:40
  928.4 19.8 %collective-permute-done.9 = bf16[4,4,64,4,128]{4,2,0,3,1:T(8,128)(2,1)S(1)} collective-permute-done((bf16[4,4,64,4,128]{4,2,0,3,1:T(8,128)(2,1)}, bf16[4,4,64,4,128]{4,2,0,3,1:T(8,128)(2,1)S(1)}, u32[]{:S(2)}, u32[]{:S(2)}) %collective-permute-start.9) | collective-permute-done | bytes 1048608 | tf_op jit(solution)/shard_map/ppermute | solution.py:52
  969.1 5.5 all-to-all-start.12
  974.7 10.2 %collective-permute-start.27 = (bf16[448,128]{1,0:T(8,128)(2,1)S(1)}, bf16[448,128]{1,0:T(8,128)(2,1)S(1)}, u32[]{:S(2)}, u32[]{:S(2)}) collective-permute-start(bf16[448,128]{1,0:T(8,128)(2,1)S(1)} %pad_maximum_fusion.13), channel_id=1, source_target_pairs={{0,0},{2,16},{16,2},{18,18},{1,1},{3,17},{17,3},{19,19},{4,4},{6,2... | collective-permute-start | bytes 344072 | tf_op jit(solution)/shard_map/ppermute | solution.py:40
  (776 shorter events, 455.8 us)
Async XLA Ops:
  7.2 146.4 %all-gather.3.cloned.1.call-start = ((), (), s32[]{:S(2)}) async-start(), calls=%async_computation.13 | async-start | bytes 25559040 | tf_op jit(solution)/shard_map/all_gather | solution.py:176
  185.0 16.8 %all-to-all-start.2 = ((bf16[8,384,128]{2,1,0:T(8,128)(2,1)}), bf16[8,384,128]{2,1,0:T(8,128)(2,1)S(1)}, u32[]{:S(2)}, u32[]{:S(2)}) async-start(bf16[8,384,128]{2,1,0:T(8,128)(2,1)} %bitcast.16), calls=%async_computation.2 | async-start | bytes 1572864 | tf_op jit(solution)/shard_map/all_to_all | solution.py:112
  221.4 49.1 %collective-permute-start.1 = (bf16[1024,128]{1,0:T(8,128)(2,1)S(1)}, bf16[1024,128]{1,0:T(8,128)(2,1)S(1)}, u32[]{:S(2)}, u32[]{:S(2)}) collective-permute-start(bf16[1024,128]{1,0:T(8,128)(2,1)S(1)} %fusion.159), channel_id=1, source_target_pairs={{0,16},{16,0},{1,17},{17,1},{2,18},{18,2},{3,19},{19,3},{4,20},{20... | collective-permute-start | bytes 786440 | tf_op jit(solution)/shard_map/ppermute | solution.py:36
  302.1 15.9 %all-to-all-start.4 = ((bf16[8,384,128]{2,1,0:T(8,128)(2,1)}), bf16[8,384,128]{2,1,0:T(8,128)(2,1)S(1)}, u32[]{:S(2)}, u32[]{:S(2)}) async-start(bf16[8,384,128]{2,1,0:T(8,128)(2,1)} %bitcast.46), calls=%async_computation.4 | async-start | bytes 1572864 | tf_op jit(solution)/shard_map/all_to_all | solution.py:112
  341.7 73.1 %collective-permute-start.3 = (bf16[1024,128]{1,0:T(8,128)(2,1)S(1)}, bf16[1024,128]{1,0:T(8,128)(2,1)S(1)}, u32[]{:S(2)}, u32[]{:S(2)}) collective-permute-start(bf16[1024,128]{1,0:T(8,128)(2,1)S(1)} %fusion.161), channel_id=1, source_target_pairs={{0,16},{16,0},{1,17},{17,1},{2,18},{18,2},{3,19},{19,3},{4,20},{20... | collective-permute-start | bytes 786440 | tf_op jit(solution)/shard_map/ppermute | solution.py:36
  438.0 52.8 %collective-permute-start.5 = (bf16[1024,128]{1,0:T(8,128)(2,1)}, bf16[1024,128]{1,0:T(8,128)(2,1)}, u32[]{:S(2)}, u32[]{:S(2)}) collective-permute-start(bf16[1024,128]{1,0:T(8,128)(2,1)} %fusion.163), channel_id=1, source_target_pairs={{0,16},{16,0},{1,17},{17,1},{2,18},{18,2},{3,19},{19,3},{4,20},{20... | collective-permute-start | bytes 786440 | tf_op jit(solution)/shard_map/ppermute | solution.py:36
  471.6 66.6 %collective-permute-start.66 = (bf16[4,4,64,512]{3,2,0,1:T(8,128)(2,1)}, bf16[4,4,64,512]{3,2,0,1:T(8,128)(2,1)}, u32[]{:S(2)}, u32[]{:S(2)}) collective-permute-start(bf16[4,4,64,512]{3,2,0,1:T(8,128)(2,1)} %bitcast.797), channel_id=1, source_target_pairs={{0,32},{32,64},{64,96},{96,0},{1,33},{33,65},{65,97},{97,1},{2,34}... | collective-permute-start | bytes 3145736 | tf_op jit(solution)/shard_map/ppermute | solution.py:52
  473.1 74.2 %collective-permute-start.67 = (bf16[4,4,64,512]{3,2,0,1:T(8,128)(2,1)}, bf16[4,4,64,512]{3,2,0,1:T(8,128)(2,1)}, u32[]{:S(2)}, u32[]{:S(2)}) collective-permute-start(bf16[4,4,64,512]{3,2,0,1:T(8,128)(2,1)} %bitcast.796), channel_id=1, source_target_pairs={{0,96},{32,0},{64,32},{96,64},{1,97},{33,1},{65,33},{97,65},{2,98}... | collective-permute-start | bytes 3145736 | tf_op jit(solution)/shard_map/ppermute | solution.py:52
  476.9 70.4 %collective-permute-start.68 = (bf16[4,4,64,512]{3,2,0,1:T(8,128)(2,1)}, bf16[4,4,64,512]{3,2,0,1:T(8,128)(2,1)}, u32[]{:S(2)}, u32[]{:S(2)}) collective-permute-start(bf16[4,4,64,512]{3,2,0,1:T(8,128)(2,1)} %bitcast.795), channel_id=1, source_target_pairs={{0,64},{32,96},{64,0},{96,32},{1,65},{33,97},{65,1},{97,33},{2,66}... | collective-permute-start | bytes 3145736 | tf_op jit(solution)/shard_map/ppermute | solution.py:52
  483.2 70.2 %collective-permute-start.37 = (bf16[512,1024]{0,1:T(8,128)(2,1)}, bf16[512,1024]{0,1:T(8,128)(2,1)}, u32[]{:S(2)}, u32[]{:S(2)}) collective-permute-start(bf16[512,1024]{0,1:T(8,128)(2,1)} %bitcast.890), channel_id=1, source_target_pairs={{0,4},{4,8},{8,12},{12,0},{1,5},{5,9},{9,13},{13,1},{2,6},{6,10},{... | collective-permute-start | bytes 3145736 | tf_op jit(solution)/shard_map/ppermute | solution.py:52
  490.9 62.6 %collective-permute-start.38 = (bf16[512,1024]{0,1:T(8,128)(2,1)}, bf16[512,1024]{0,1:T(8,128)(2,1)}, u32[]{:S(2)}, u32[]{:S(2)}) collective-permute-start(bf16[512,1024]{0,1:T(8,128)(2,1)} %bitcast.891), channel_id=1, source_target_pairs={{0,12},{4,0},{8,4},{12,8},{1,13},{5,1},{9,5},{13,9},{2,14},{6,2},{... | collective-permute-start | bytes 3145736 | tf_op jit(solution)/shard_map/ppermute | solution.py:52
  501.7 15.7 %all-to-all-start.8 = ((bf16[8,128,128]{2,1,0:T(8,128)(2,1)}), bf16[8,128,128]{2,1,0:T(8,128)(2,1)}, u32[]{:S(2)}, u32[]{:S(2)}) async-start(bf16[8,128,128]{2,1,0:T(8,128)(2,1)} %bitcast.79), calls=%async_computation.8 | async-start | bytes 524288 | tf_op jit(solution)/shard_map/all_to_all | solution.py:112
  517.5 25.1 %all-to-all-start.6 = ((bf16[16,64,128]{2,1,0:T(8,128)(2,1)}), bf16[16,64,128]{2,1,0:T(8,128)(2,1)S(1)}, u32[]{:S(2)}, u32[]{:S(2)}) async-start(bf16[16,64,128]{2,1,0:T(8,128)(2,1)} %bitcast.67), calls=%async_computation.6 | async-start | bytes 524288 | tf_op jit(solution)/shard_map/all_to_all | solution.py:225
  538.2 23.7 %collective-permute-start.39 = (bf16[512,1024]{0,1:T(8,128)(2,1)}, bf16[512,1024]{0,1:T(8,128)(2,1)}, u32[]{:S(2)}, u32[]{:S(2)}) collective-permute-start(bf16[512,1024]{0,1:T(8,128)(2,1)} %bitcast.170), channel_id=1, source_target_pairs={{0,8},{4,12},{8,0},{12,4},{1,9},{5,13},{9,1},{13,5},{2,10},{6,14},... | collective-permute-start | bytes 3145736 | tf_op jit(solution)/shard_map/ppermute | solution.py:52
  542.6 27.6 %all-to-all-start.9 = ((bf16[8,384,128]{2,1,0:T(8,128)(2,1)}), bf16[8,384,128]{2,1,0:T(8,128)(2,1)S(1)}, u32[]{:S(2)}, u32[]{:S(2)}) async-start(bf16[8,384,128]{2,1,0:T(8,128)(2,1)} %bitcast.862), calls=%async_computation.9 | async-start | bytes 1572864 | tf_op jit(solution)/shard_map/all_to_all | solution.py:118
  550.8 60.4 %collective-permute-start.69 = (bf16[4,64,512]{2,1,0:T(8,128)(2,1)}, bf16[4,64,512]{2,1,0:T(8,128)(2,1)}, u32[]{:S(2)}, u32[]{:S(2)}) collective-permute-start(bf16[4,64,512]{2,1,0:T(8,128)(2,1)} %get-tuple-element.110), channel_id=1, source_target_pairs={{0,1},{1,2},{2,3},{3,0},{4,5},{5,6},{6,7},{7,4},{8,9},{9,10},{10,1... | collective-permute-start | bytes 786440 | tf_op jit(solution)/shard_map/ppermute | solution.py:52
  552.2 59.0 %collective-permute-start.70 = (bf16[4,64,512]{2,1,0:T(8,128)(2,1)}, bf16[4,64,512]{2,1,0:T(8,128)(2,1)}, u32[]{:S(2)}, u32[]{:S(2)}) collective-permute-start(bf16[4,64,512]{2,1,0:T(8,128)(2,1)} %get-tuple-element.112), channel_id=1, source_target_pairs={{0,3},{1,0},{2,1},{3,2},{4,7},{5,4},{6,5},{7,6},{8,11},{9,8},{10,9... | collective-permute-start | bytes 786440 | tf_op jit(solution)/shard_map/ppermute | solution.py:52
  565.2 33.3 %collective-permute-start.40 = (bf16[512,256]{0,1:T(8,128)(2,1)}, bf16[512,256]{0,1:T(8,128)(2,1)}, u32[]{:S(2)}, u32[]{:S(2)}) collective-permute-start(bf16[512,256]{0,1:T(8,128)(2,1)} %get-tuple-element.130), channel_id=1, source_target_pairs={{0,32},{32,64},{64,96},{96,0},{1,33},{33,65},{65,97},{97,1},{2,34}... | collective-permute-start | bytes 786440 | tf_op jit(solution)/shard_map/ppermute | solution.py:52
  565.5 35.7 %collective-permute-start.41 = (bf16[512,256]{0,1:T(8,128)(2,1)}, bf16[512,256]{0,1:T(8,128)(2,1)}, u32[]{:S(2)}, u32[]{:S(2)}) collective-permute-start(bf16[512,256]{0,1:T(8,128)(2,1)} %get-tuple-element.132), channel_id=1, source_target_pairs={{0,96},{32,0},{64,32},{96,64},{1,97},{33,1},{65,33},{97,65},{2,98}... | collective-permute-start | bytes 786440 | tf_op jit(solution)/shard_map/ppermute | solution.py:52
  567.9 41.3 %collective-permute-start.42 = (bf16[512,256]{0,1:T(8,128)(2,1)}, bf16[512,256]{0,1:T(8,128)(2,1)}, u32[]{:S(2)}, u32[]{:S(2)}) collective-permute-start(bf16[512,256]{0,1:T(8,128)(2,1)} %get-tuple-element.131), channel_id=1, source_target_pairs={{0,64},{32,96},{64,0},{96,32},{1,65},{33,97},{65,1},{97,33},{2,66}... | collective-permute-start | bytes 786440 | tf_op jit(solution)/shard_map/ppermute | solution.py:52
  601.2 45.8 %collective-permute-start.6 = (bf16[1024,128]{1,0:T(8,128)(2,1)}, bf16[1024,128]{1,0:T(8,128)(2,1)}, u32[]{:S(2)}, u32[]{:S(2)}) collective-permute-start(bf16[1024,128]{1,0:T(8,128)(2,1)} %fusion.164), channel_id=1, source_target_pairs={{0,16},{16,0},{1,17},{17,1},{2,18},{18,2},{3,19},{19,3},{4,20},{20... | collective-permute-start | bytes 786440 | tf_op jit(solution)/shard_map/ppermute | solution.py:36
  609.2 149.5 %collective-permute-start.28 = (bf16[4,4,64,4,128]{4,2,0,3,1:T(8,128)(2,1)}, bf16[4,4,64,4,128]{4,2,0,3,1:T(8,128)(2,1)}, u32[]{:S(2)}, u32[]{:S(2)}) collective-permute-start(bf16[4,4,64,4,128]{4,2,0,3,1:T(8,128)(2,1)} %pad_maximum_fusion.3), channel_id=1, source_target_pairs={{0,1},{1,2},{2,3},{3,0},{4,5},{5,6},{6,7},{7,4},{8,9},{9,10},{10,1... | collective-permute-start | bytes 3145736 | tf_op jit(solution)/shard_map/ppermute | solution.py:52
  611.2 26.7 %collective-permute-start.43 = (bf16[256,128]{1,0:T(8,128)(2,1)S(1)}, bf16[256,128]{1,0:T(8,128)(2,1)S(1)}, u32[]{:S(2)}, u32[]{:S(2)}) collective-permute-start(bf16[256,128]{1,0:T(8,128)(2,1)S(1)} %get-tuple-element.155), channel_id=1, source_target_pairs={{0,1},{1,2},{2,3},{3,0},{4,5},{5,6},{6,7},{7,4},{8,9},{9,10},{10,1... | collective-permute-start | bytes 196616 | tf_op jit(solution)/shard_map/ppermute | solution.py:52
  611.3 28.4 %collective-permute-start.44 = (bf16[256,128]{1,0:T(8,128)(2,1)S(1)}, bf16[256,128]{1,0:T(8,128)(2,1)S(1)}, u32[]{:S(2)}, u32[]{:S(2)}) collective-permute-start(bf16[256,128]{1,0:T(8,128)(2,1)S(1)} %get-tuple-element.157), channel_id=1, source_target_pairs={{0,3},{1,0},{2,1},{3,2},{4,7},{5,4},{6,5},{7,6},{8,11},{9,8},{10,9... | collective-permute-start | bytes 196616 | tf_op jit(solution)/shard_map/ppermute | solution.py:52
  613.9 27.0 %collective-permute-start.45 = (bf16[256,128]{1,0:T(8,128)(2,1)S(1)}, bf16[256,128]{1,0:T(8,128)(2,1)S(1)}, u32[]{:S(2)}, u32[]{:S(2)}) collective-permute-start(bf16[256,128]{1,0:T(8,128)(2,1)S(1)} %get-tuple-element.156), channel_id=1, source_target_pairs={{0,2},{1,3},{2,0},{3,1},{4,6},{5,7},{6,4},{7,5},{8,10},{9,11},{10,... | collective-permute-start | bytes 196616 | tf_op jit(solution)/shard_map/ppermute | solution.py:52
  642.7 117.6 %collective-permute-start.29 = (bf16[4,4,64,4,128]{4,2,0,3,1:T(8,128)(2,1)}, bf16[4,4,64,4,128]{4,2,0,3,1:T(8,128)(2,1)}, u32[]{:S(2)}, u32[]{:S(2)}) collective-permute-start(bf16[4,4,64,4,128]{4,2,0,3,1:T(8,128)(2,1)} %pad_maximum_fusion.4), channel_id=1, source_target_pairs={{0,3},{1,0},{2,1},{3,2},{4,7},{5,4},{6,5},{7,6},{8,11},{9,8},{10,9... | collective-permute-start | bytes 3145736 | tf_op jit(solution)/shard_map/ppermute | solution.py:52
  642.8 118.9 %collective-permute-start.30 = (bf16[4,4,64,4,128]{4,2,0,3,1:T(8,128)(2,1)}, bf16[4,4,64,4,128]{4,2,0,3,1:T(8,128)(2,1)}, u32[]{:S(2)}, u32[]{:S(2)}) collective-permute-start(bf16[4,4,64,4,128]{4,2,0,3,1:T(8,128)(2,1)} %pad_maximum_fusion.5), channel_id=1, source_target_pairs={{0,2},{1,3},{2,0},{3,1},{4,6},{5,7},{6,4},{7,5},{8,10},{9,11},{10,... | collective-permute-start | bytes 3145736 | tf_op jit(solution)/shard_map/ppermute | solution.py:52
  691.9 74.9 %collective-permute-start.57 = (bf16[4,4,64,512]{3,2,0,1:T(8,128)(2,1)}, bf16[4,4,64,512]{3,2,0,1:T(8,128)(2,1)}, u32[]{:S(2)}, u32[]{:S(2)}) collective-permute-start(bf16[4,4,64,512]{3,2,0,1:T(8,128)(2,1)} %bitcast.800), channel_id=1, source_target_pairs={{0,32},{32,64},{64,96},{96,0},{1,33},{33,65},{65,97},{97,1},{2,34}... | collective-permute-start | bytes 3145736 | tf_op jit(solution)/shard_map/ppermute | solution.py:52
  694.1 19.4 %collective-permute-start.7 = (bf16[1024,128]{1,0:T(8,128)(2,1)}, bf16[1024,128]{1,0:T(8,128)(2,1)S(1)}, u32[]{:S(2)}, u32[]{:S(2)}) collective-permute-start(bf16[1024,128]{1,0:T(8,128)(2,1)} %fusion.165), channel_id=1, source_target_pairs={{0,16},{16,0},{1,17},{17,1},{2,18},{18,2},{3,19},{19,3},{4,20},{20... | collective-permute-start | bytes 786440 | tf_op jit(solution)/shard_map/ppermute | solution.py:36
  714.3 53.3 %collective-permute-start.58 = (bf16[4,4,64,512]{3,2,0,1:T(8,128)(2,1)}, bf16[4,4,64,512]{3,2,0,1:T(8,128)(2,1)}, u32[]{:S(2)}, u32[]{:S(2)}) collective-permute-start(bf16[4,4,64,512]{3,2,0,1:T(8,128)(2,1)} %bitcast.881), channel_id=1, source_target_pairs={{0,96},{32,0},{64,32},{96,64},{1,97},{33,1},{65,33},{97,65},{2,98}... | collective-permute-start | bytes 3145736 | tf_op jit(solution)/shard_map/ppermute | solution.py:52
  727.4 18.7 %all-to-all-start.10 = ((bf16[8,128,128]{2,1,0:T(8,128)(2,1)}), bf16[8,128,128]{2,1,0:T(8,128)(2,1)}, u32[]{:S(2)}, u32[]{:S(2)}) async-start(bf16[8,128,128]{2,1,0:T(8,128)(2,1)} %bitcast.98), calls=%async_computation.10 | async-start | bytes 524288 | tf_op jit(solution)/shard_map/all_to_all | solution.py:112
  758.8 26.5 %collective-permute-start.59 = (bf16[4,4,64,512]{3,2,0,1:T(8,128)(2,1)}, bf16[4,4,64,512]{3,2,0,1:T(8,128)(2,1)}, u32[]{:S(2)}, u32[]{:S(2)}) collective-permute-start(bf16[4,4,64,512]{3,2,0,1:T(8,128)(2,1)} %bitcast.798), channel_id=1, source_target_pairs={{0,64},{32,96},{64,0},{96,32},{1,65},{33,97},{65,1},{97,33},{2,66}... | collective-permute-start | bytes 3145736 | tf_op jit(solution)/shard_map/ppermute | solution.py:52
  760.3 71.7 %collective-permute-start.18 = (bf16[512,1024]{0,1:T(8,128)(2,1)}, bf16[512,1024]{0,1:T(8,128)(2,1)}, u32[]{:S(2)}, u32[]{:S(2)}) collective-permute-start(bf16[512,1024]{0,1:T(8,128)(2,1)} %bitcast.133), channel_id=1, source_target_pairs={{0,4},{4,8},{8,12},{12,0},{1,5},{5,9},{9,13},{13,1},{2,6},{6,10},{... | collective-permute-start | bytes 3145736 | tf_op jit(solution)/shard_map/ppermute | solution.py:52
  761.7 70.7 %collective-permute-start.19 = (bf16[512,1024]{0,1:T(8,128)(2,1)}, bf16[512,1024]{0,1:T(8,128)(2,1)}, u32[]{:S(2)}, u32[]{:S(2)}) collective-permute-start(bf16[512,1024]{0,1:T(8,128)(2,1)} %bitcast.134), channel_id=1, source_target_pairs={{0,12},{4,0},{8,4},{12,8},{1,13},{5,1},{9,5},{13,9},{2,14},{6,2},{... | collective-permute-start | bytes 3145736 | tf_op jit(solution)/shard_map/ppermute | solution.py:52
  766.9 67.9 %collective-permute-start.20 = (bf16[512,1024]{0,1:T(8,128)(2,1)}, bf16[512,1024]{0,1:T(8,128)(2,1)}, u32[]{:S(2)}, u32[]{:S(2)}) collective-permute-start(bf16[512,1024]{0,1:T(8,128)(2,1)} %bitcast.135), channel_id=1, source_target_pairs={{0,8},{4,12},{8,0},{12,4},{1,9},{5,13},{9,1},{13,5},{2,10},{6,14},... | collective-permute-start | bytes 3145736 | tf_op jit(solution)/shard_map/ppermute | solution.py:52
  767.6 46.6 %collective-permute-start.31 = (bf16[4,64,4,128]{3,1,0,2:T(8,128)(2,1)}, bf16[4,64,4,128]{3,1,0,2:T(8,128)(2,1)}, u32[]{:S(2)}, u32[]{:S(2)}) collective-permute-start(bf16[4,64,4,128]{3,1,0,2:T(8,128)(2,1)} %get-tuple-element.123), channel_id=1, source_target_pairs={{0,4},{4,8},{8,12},{12,0},{1,5},{5,9},{9,13},{13,1},{2,6},{6,10},{... | collective-permute-start | bytes 786440 | tf_op jit(solution)/shard_map/ppermute | solution.py:52
  771.0 70.0 %all-to-all-start.11 = ((bf16[8,384,128]{2,1,0:T(8,128)(2,1)}), bf16[8,384,128]{2,1,0:T(8,128)(2,1)S(1)}, u32[]{:S(2)}, u32[]{:S(2)}) async-start(bf16[8,384,128]{2,1,0:T(8,128)(2,1)} %bitcast.861), calls=%async_computation.11 | async-start | bytes 1572864 | tf_op jit(solution)/shard_map/all_to_all | solution.py:118
  785.3 36.7 %collective-permute-start.32 = (bf16[4,64,4,128]{3,1,0,2:T(8,128)(2,1)S(1)}, bf16[4,64,4,128]{3,1,0,2:T(8,128)(2,1)S(1)}, u32[]{:S(2)}, u32[]{:S(2)}) collective-permute-start(bf16[4,64,4,128]{3,1,0,2:T(8,128)(2,1)S(1)} %copy-done.94), channel_id=1, source_target_pairs={{0,12},{4,0},{8,4},{12,8},{1,13},{5,1},{9,5},{13,9},{2,14},{6,2},{... | collective-permute-start | bytes 786440 | tf_op jit(solution)/shard_map/ppermute | solution.py:52
  822.0 78.4 %collective-permute-start.60 = (bf16[4,64,512]{2,1,0:T(8,128)(2,1)}, bf16[4,64,512]{2,1,0:T(8,128)(2,1)}, u32[]{:S(2)}, u32[]{:S(2)}) collective-permute-start(bf16[4,64,512]{2,1,0:T(8,128)(2,1)} %get-tuple-element.107), channel_id=1, source_target_pairs={{0,1},{1,2},{2,3},{3,0},{4,5},{5,6},{6,7},{7,4},{8,9},{9,10},{10,1... | collective-permute-start | bytes 786440 | tf_op jit(solution)/shard_map/ppermute | solution.py:52
  828.4 74.7 %collective-permute-start.61 = (bf16[4,64,512]{2,1,0:T(8,128)(2,1)}, bf16[4,64,512]{2,1,0:T(8,128)(2,1)}, u32[]{:S(2)}, u32[]{:S(2)}) collective-permute-start(bf16[4,64,512]{2,1,0:T(8,128)(2,1)} %get-tuple-element.109), channel_id=1, source_target_pairs={{0,3},{1,0},{2,1},{3,2},{4,7},{5,4},{6,5},{7,6},{8,11},{9,8},{10,9... | collective-permute-start | bytes 786440 | tf_op jit(solution)/shard_map/ppermute | solution.py:52
  881.4 22.4 %collective-permute-start.62 = (bf16[4,64,512]{2,1,0:T(8,128)(2,1)}, bf16[4,64,512]{2,1,0:T(8,128)(2,1)}, u32[]{:S(2)}, u32[]{:S(2)}) collective-permute-start(bf16[4,64,512]{2,1,0:T(8,128)(2,1)} %get-tuple-element.108), channel_id=1, source_target_pairs={{0,2},{1,3},{2,0},{3,1},{4,6},{5,7},{6,4},{7,5},{8,10},{9,11},{10,... | collective-permute-start | bytes 786440 | tf_op jit(solution)/shard_map/ppermute | solution.py:52
  881.8 18.5 %collective-permute-start.46 = (bf16[448,128]{1,0:T(8,128)(2,1)S(1)}, bf16[448,128]{1,0:T(8,128)(2,1)S(1)}, u32[]{:S(2)}, u32[]{:S(2)}) collective-permute-start(bf16[448,128]{1,0:T(8,128)(2,1)S(1)} %copy-done.101), channel_id=1, source_target_pairs={{0,0},{2,16},{16,2},{18,18},{1,1},{3,17},{17,3},{19,19},{4,4},{6,2... | collective-permute-start | bytes 344072 | tf_op jit(solution)/shard_map/ppermute | solution.py:40
  900.4 47.8 %collective-permute-start.9 = (bf16[4,4,64,4,128]{4,2,0,3,1:T(8,128)(2,1)}, bf16[4,4,64,4,128]{4,2,0,3,1:T(8,128)(2,1)S(1)}, u32[]{:S(2)}, u32[]{:S(2)}) collective-permute-start(bf16[4,4,64,4,128]{4,2,0,3,1:T(8,128)(2,1)} %pad_maximum_fusion), channel_id=1, source_target_pairs={{0,1},{1,2},{2,3},{3,0},{4,5},{5,6},{6,7},{7,4},{8,9},{9,10},{10,1... | collective-permute-start | bytes 3145736 | tf_op jit(solution)/shard_map/ppermute | solution.py:52
  900.4 47.8 %collective-permute-start.10 = (bf16[4,4,64,4,128]{4,2,0,3,1:T(8,128)(2,1)}, bf16[4,4,64,4,128]{4,2,0,3,1:T(8,128)(2,1)S(1)}, u32[]{:S(2)}, u32[]{:S(2)}) collective-permute-start(bf16[4,4,64,4,128]{4,2,0,3,1:T(8,128)(2,1)} %pad_maximum_fusion.1), channel_id=1, source_target_pairs={{0,3},{1,0},{2,1},{3,2},{4,7},{5,4},{6,5},{7,6},{8,11},{9,8},{10,9... | collective-permute-start | bytes 3145736 | tf_op jit(solution)/shard_map/ppermute | solution.py:52
  903.1 45.0 %collective-permute-start.11 = (bf16[4,4,64,4,128]{4,2,0,3,1:T(8,128)(2,1)}, bf16[4,4,64,4,128]{4,2,0,3,1:T(8,128)(2,1)}, u32[]{:S(2)}, u32[]{:S(2)}) collective-permute-start(bf16[4,4,64,4,128]{4,2,0,3,1:T(8,128)(2,1)} %pad_maximum_fusion.2), channel_id=1, source_target_pairs={{0,2},{1,3},{2,0},{3,1},{4,6},{5,7},{6,4},{7,5},{8,10},{9,11},{10,... | collective-permute-start | bytes 3145736 | tf_op jit(solution)/shard_map/ppermute | solution.py:52
  923.4 29.8 %collective-permute-start.24 = (bf16[256,128]{1,0:T(8,128)(2,1)S(1)}, bf16[256,128]{1,0:T(8,128)(2,1)S(1)}, u32[]{:S(2)}, u32[]{:S(2)}) collective-permute-start(bf16[256,128]{1,0:T(8,128)(2,1)S(1)} %get-tuple-element.149), channel_id=1, source_target_pairs={{0,1},{1,2},{2,3},{3,0},{4,5},{5,6},{6,7},{7,4},{8,9},{9,10},{10,1... | collective-permute-start | bytes 196616 | tf_op jit(solution)/shard_map/ppermute | solution.py:52
  926.7 28.9 %collective-permute-start.25 = (bf16[256,128]{1,0:T(8,128)(2,1)S(1)}, bf16[256,128]{1,0:T(8,128)(2,1)S(1)}, u32[]{:S(2)}, u32[]{:S(2)}) collective-permute-start(bf16[256,128]{1,0:T(8,128)(2,1)S(1)} %get-tuple-element.151), channel_id=1, source_target_pairs={{0,3},{1,0},{2,1},{3,2},{4,7},{5,4},{6,5},{7,6},{8,11},{9,8},{10,9... | collective-permute-start | bytes 196616 | tf_op jit(solution)/shard_map/ppermute | solution.py:52
  969.1 15.8 %all-to-all-start.12 = ((bf16[16,64,128]{2,1,0:T(8,128)(2,1)}), bf16[16,64,128]{2,1,0:T(8,128)(2,1)S(1)}, u32[]{:S(2)}, u32[]{:S(2)}) async-start(bf16[16,64,128]{2,1,0:T(8,128)(2,1)} %bitcast.112), calls=%async_computation.12 | async-start | bytes 524288 | tf_op jit(solution)/shard_map/all_to_all | solution.py:263
  (172 other events, 2654.4 us)
Sparse Core Ops, SparseCore 0:
  20.5 133.0 all-gather.2

commit v2 on v1

v2 whole, which is shorter than its diff:
```python
import jax
import jax.numpy as jnp
from jax import lax
from jax.experimental import pallas as pl
from jax.experimental.pallas import tpu as pltpu
from jax.sharding import Mesh, PartitionSpec as P

HEAD = 64
D = 1024
LAYERS = 2
SEQ_LEN = 1024
epsilon = 1e-05

CORE = "k"
Y = ("y",)
X = ("xh", "xl")
Z = ("zh", "zl")
COL = X + Z
CHIPS = Y + COL
SEQ = ("xl", "zh", "zl")
bf16 = jnp.bfloat16
f32 = jnp.float32


NT = ((1,), (1,))
TN = ((0,), (0,))
NN = ((1,), (0,))


def mm(a, b, dims):
    return lax.dot_general(a, b, (dims, ((), ())), preferred_element_type=f32)


def core_gather(values):
    return lax.all_gather(values, CORE, axis=1, tiled=True)


def core_add(pair):
    keep, send = pair
    return keep + lax.ppermute(send, CORE, [(0, 1), (1, 0)]).astype(f32)


def trade(values):
    return lax.ppermute(values, (CORE, "zh"), [(0, 0), (1, 2), (2, 1), (3, 3)])


def pick(values, index, dim):
    return lax.dynamic_index_in_dim(values, index, dim, keepdims=False)


def reduce_stage(g, axes):
    return jnp.sum(lax.all_to_all(g, axes, 0, 0, tiled=True).astype(f32), axis=0)


def reduce_both(g, first, second):
    h = reduce_stage(g, first).astype(bf16)
    return reduce_stage(h.reshape(16, 256, 128), second)


def sum_axis(values, axes):
    total = values
    for shift in (1, 3, 2):
        total += lax.ppermute(values, axes, [(i, (i + shift) % 4) for i in range(4)])
    return total


def call(kernel, grid, ins, outs, scratch=(), flops=0, moved=0):
    return pl.pallas_call(
        kernel,
        grid=grid,
        in_specs=[spec for spec, _ in ins],
        out_specs=[spec for spec, _ in outs],
        out_shape=[shape for _, shape in outs],
        scratch_shapes=list(scratch),
        compiler_params=pltpu.CompilerParams(vmem_limit_bytes=50 * 1024 * 1024),
        cost_estimate=pl.CostEstimate(flops=flops, bytes_accessed=moved, transcendentals=0),
    )(*[value for _, value in ins])


def whole(value):
    rank = value.ndim
    return (pl.BlockSpec(value.shape, lambda g: (0,) * rank), value)


def scalar(value):
    return (pl.BlockSpec(memory_space=pltpu.SMEM), value)


def out_whole(shape, dtype):
    rank = len(shape)
    return (pl.BlockSpec(shape, lambda g: (0,) * rank), jax.ShapeDtypeStruct(shape, dtype))


def split_cores(core_ref, acc, keep_ref, send_ref):
    first = core_ref[0] == 0
    low, high = acc[:, :128], acc[:, 128:]
    keep_ref[...] = jnp.where(first, low, high)
    send_ref[...] = jnp.where(first, high, low).astype(bf16)


PAIR = (out_whole((D, 128), f32), out_whole((D, 128), bf16))


def w_qkv_spec(l):
    return pl.BlockSpec((4, 1, 2, 2, 1, 192, 128), lambda g: (0, g, 0, 0, l, 0, 0))


def w_out_spec(l):
    return pl.BlockSpec((4, 4, 2, 2, 1, 64, 128), lambda g: (0, 0, 0, 0, l, 3, 0))


def w_up_spec(l):
    return pl.BlockSpec((4, 1, 2, 2, 1, 256, 128), lambda g: (0, g, 0, 0, l, 1, 0))


def w_down_spec(l):
    return pl.BlockSpec((1, 4, 2, 2, 1, 256, 128), lambda g: (g, 0, 0, 0, l, 2, 0))


def rows_by_inputs(w_ref, b):
    return jnp.concatenate([w_ref[y, 0, a, b, 0] for y in range(4) for a in range(2)], axis=1)


def down_block(w_ref):
    rows = []
    for x in range(4):
        for a in range(2):
            for b in range(2):
                blk = w_ref[0, x, a, b, 0]
                rows.append(jnp.concatenate([blk[j * 64 : (j + 1) * 64] for j in range(4)], axis=1))
    return jnp.concatenate(rows, axis=0)


def out_block(w_ref):
    rows = []
    for x in range(4):
        for a in range(2):
            for b in range(2):
                rows.append(jnp.concatenate([w_ref[y, x, a, b, 0] for y in range(4)], axis=1))
    return jnp.concatenate(rows, axis=0)


def qkv_kernel(w_ref, x_ref, bias_ref, o_ref):
    x = x_ref[...]
    for b in range(2):
        r = mm(rows_by_inputs(w_ref, b), x, NN)
        for s in range(2):
            v = (r[:, s * 128 : (s + 1) * 128] + bias_ref[0, b]).astype(bf16)
            for j in range(3):
                o_ref[s, 0, j * 128 + b * 64 : j * 128 + b * 64 + 64, :] = v[j * 64 : (j + 1) * 64]


def run_qkv(l, every, seen, bias):
    out = call(
        qkv_kernel,
        (4,),
        [
            (w_qkv_spec(l), every),
            whole(seen),
            (pl.BlockSpec((1, 2, 192, 128), lambda g: (g, 0, 0, 0)), bias),
        ],
        [
            (
                pl.BlockSpec((2, 1, 384, 128), lambda g: (0, g, 0, 0)),
                jax.ShapeDtypeStruct((2, 4, 384, 128), bf16),
            )
        ],
        flops=2 * 1536 * 1024 * 256,
        moved=5 << 20,
    )[0]
    return out.reshape(8, 384, 128)


def join_heads(ref, rows):
    return jnp.concatenate(
        [jnp.concatenate([ref[s * 4 + h] for h in range(4)], axis=0) for s in range(2)], axis=1
    )


def out_kernel(core_ref, w_ref, b_ref, keep_ref, send_ref, blended_ref):
    blended = join_heads(b_ref, 128)
    blended_ref[...] = blended
    split_cores(core_ref, mm(out_block(w_ref), blended, NN), keep_ref, send_ref)


def run_out(l, core, every, arrived):
    keep, send, blended = call(
        out_kernel,
        (1,),
        [scalar(core), (w_out_spec(l), every), whole(arrived)],
        [*PAIR, out_whole((512, 256), bf16)],
        flops=2 * 1024 * 512 * 256,
        moved=2 << 20,
    )
    return (keep, send), blended


def ffn_kernel(core_ref, up_ref, down_ref, x_ref, bias_ref, keep_ref, send_ref, act_ref, slope_ref, acc):
    g = pl.program_id(0)
    x = x_ref[...]
    acts = []
    for b in range(2):
        r = mm(rows_by_inputs(up_ref, b), x, NN)
        bias = bias_ref[0, b]
        r = r + jnp.concatenate([bias, bias], axis=1)
        half = 0.5 * (1.0 + lax.erf(r * (2.0**-0.5)))
        act = (r * half).astype(bf16)
        slope_ref[b * 256 : (b + 1) * 256, :] = half + r * jnp.exp(-0.5 * r * r) * 0.3989422804014327
        act_ref[b * 256 : (b + 1) * 256, :] = act
        acts.append(act)
    part = mm(down_block(down_ref), jnp.concatenate(acts, axis=0), NN)

    @pl.when(g == 0)
    def _():
        acc[...] = part

    @pl.when(g > 0)
    def _():
        acc[...] += part

    @pl.when(g == 3)
    def _():
        split_cores(core_ref, acc[...], keep_ref, send_ref)


def by_step(rows, columns):
    return pl.BlockSpec((rows, columns), lambda g: (g, 0))


def run_ffn(l, core, every, seen, bias):
    keep, send, act, slope = call(
        ffn_kernel,
        (4,),
        [
            scalar(core),
            (w_up_spec(l), every),
            (w_down_spec(l), every),
            whole(seen),
            (pl.BlockSpec((1, 2, 256, 128), lambda g: (g, 0, 0, 0)), bias),
        ],
        [
            *PAIR,
            (by_step(512, 256), jax.ShapeDtypeStruct((2048, 256), bf16)),
            (by_step(512, 256), jax.ShapeDtypeStruct((2048, 256), f32)),
        ],
        [pltpu.VMEM((D, 256), f32)],
        flops=4 * 2048 * 1024 * 256,
        moved=13 << 20,
    )
    return (keep, send), act, slope


def ffn_back_kernel(
    core_ref, up_ref, down_ref, low_ref, act_ref, slope_ref, x_ref, keep_ref, send_ref, gd_ref, gu_ref, bias_ref, acc
):
    g = pl.program_id(0)
    low = low_ref[...]
    grad_active = mm(down_block(down_ref), low, TN)
    wide = grad_active * slope_ref[...]
    gu = wide.astype(bf16)
    bias_ref[...] = jnp.sum(gu.astype(f32), axis=1, keepdims=True)
    gd = mm(low, act_ref[...], NT).astype(bf16)
    for c in range(16):
        for j in range(4):
            gd_ref[0, c, j * 64 : (j + 1) * 64, :] = gd[c * 64 : (c + 1) * 64, j * 128 : (j + 1) * 128]
    x = x_ref[...]
    part = None
    for b in range(2):
        gub = gu[b * 256 : (b + 1) * 256]
        gw = mm(gub, x, NT).astype(bf16)
        for y in range(4):
            for a in range(2):
                i = y * 2 + a
                gu_ref[0, y, a, b] = gw[:, i * 128 : (i + 1) * 128]
        term = mm(rows_by_inputs(up_ref, b), gub, TN)
        part = term if part is None else part + term

    @pl.when(g == 0)
    def _():
        acc[...] = part

    @pl.when(g > 0)
    def _():
        acc[...] += part

    @pl.when(g == 3)
    def _():
        split_cores(core_ref, acc[...], keep_ref, send_ref)


def run_ffn_back(l, core, every, low, act, slope, seen):
    keep, send, gd, gu, bias = call(
        ffn_back_kernel,
        (4,),
        [
            scalar(core),
            (w_up_spec(l), every),
            (w_down_spec(l), every),
            whole(low),
            (by_step(512, 256), act),
            (by_step(512, 256), slope),
            whole(seen),
        ],
        [
            *PAIR,
            (pl.BlockSpec((1, 16, 256, 128), lambda g: (g, 0, 0, 0)), jax.ShapeDtypeStruct((4, 16, 256, 128), bf16)),
            (
                pl.BlockSpec((1, 4, 2, 2, 256, 128), lambda g: (g, 0, 0, 0, 0, 0)),
                jax.ShapeDtypeStruct((4, 4, 2, 2, 256, 128), bf16),
            ),
            (by_step(512, 1), jax.ShapeDtypeStruct((2048, 1), f32)),
        ],
        [pltpu.VMEM((D, 256), f32)],
        flops=8 * 2048 * 1024 * 256,
        moved=22 << 20,
    )
    return (keep, send), gd, gu, bias


def out_back_kernel(w_ref, low_ref, o_ref):
    r = mm(out_block(w_ref), low_ref[...], TN).astype(bf16)
    for s in range(2):
        for h in range(4):
            o_ref[s * 4 + h] = r[h * 128 : (h + 1) * 128, s * 128 : (s + 1) * 128]


def run_out_back(l, every, low):
    return call(
        out_back_kernel,
        (1,),
        [(w_out_spec(l), every), whole(low)],
        [out_whole((8, 128, 128), bf16)],
        flops=2 * 1024 * 512 * 256,
        moved=2 << 20,
    )[0]


def qkv_back_kernel(core_ref, w_ref, gq_ref, x_ref, low_ref, bl_ref, keep_ref, send_ref, g_ref, bias_ref, acc):
    g = pl.program_id(0)
    x = x_ref[...]
    both = jnp.concatenate([gq_ref[0, 0], gq_ref[1, 0]], axis=1)
    part = None
    for b in range(2):
        gq = jnp.concatenate([both[j * 128 + b * 64 : j * 128 + b * 64 + 64] for j in range(3)], axis=0)
        bias_ref[0, b] = jnp.sum(gq.astype(f32), axis=1, keepdims=True)
        gw = mm(gq, x, NT).astype(bf16)
        for y in range(4):
            for a in range(2):
                i = y * 2 + a
                g_ref[a * 2 + b, y, 0, 0:192, :] = gw[:, i * 128 : (i + 1) * 128]
        term = mm(rows_by_inputs(w_ref, b), gq, TN)
        part = term if part is None else part + term
    go = mm(low_ref[...], bl_ref[...], NT).astype(bf16)
    for z in range(4):
        for y in range(4):
            g_ref[z, y, 0, 192:256, :] = go[z * 64 : (z + 1) * 64, y * 128 : (y + 1) * 128]

    @pl.when(g == 0)
    def _():
        acc[...] = part

    @pl.when(g > 0)
    def _():
        acc[...] += part

    @pl.when(g == 3)
    def _():
        split_cores(core_ref, acc[...], keep_ref, send_ref)


def run_qkv_back(l, core, every, arrived, seen, low, blended):
    keep, send, gqo, bias = call(
        qkv_back_kernel,
        (4,),
        [
            scalar(core),
            (w_qkv_spec(l), every),
            (pl.BlockSpec((2, 1, 384, 128), lambda g: (0, g, 0, 0)), arrived.reshape(2, 4, 384, 128)),
            whole(seen),
            (by_step(256, 256), low),
            whole(blended),
        ],
        [
            *PAIR,
            (
                pl.BlockSpec((4, 4, 1, 256, 128), lambda g: (0, 0, g, 0, 0)),
                jax.ShapeDtypeStruct((4, 4, 4, 256, 128), bf16),
            ),
            (pl.BlockSpec((1, 2, 192, 1), lambda g: (g, 0, 0, 0)), jax.ShapeDtypeStruct((4, 2, 192, 1), f32)),
        ],
        [pltpu.VMEM((D, 256), f32)],
        flops=6 * 2048 * 1024 * 256,
        moved=12 << 20,
    )
    return (keep, send), gqo, bias


FACTOR = HEAD ** (-0.5)
STEP = 256


def join_tokens(ref, top):
    return jnp.concatenate([ref[c, top : top + HEAD] for c in range(8)], axis=1)


def attend_kernel(p_ref, o_ref, log_ref):
    for h in range(2):
        q = join_tokens(p_ref, h * 64)
        k = join_tokens(p_ref, 128 + h * 64)
        v = join_tokens(p_ref, 256 + h * 64)
        for c in range(SEQ_LEN // STEP):
            scores = mm(k, q[:, c * STEP : (c + 1) * STEP], TN) * FACTOR
            highest = jnp.max(scores, axis=0, keepdims=True)
            exps = jnp.exp(scores - highest)
            total = jnp.sum(exps, axis=0, keepdims=True)
            low = (exps * (1.0 / total)).astype(bf16)
            out = mm(v, low, NN).astype(bf16)
            log_ref[h : h + 1, c * STEP : (c + 1) * STEP] = highest + jnp.log(total)
            for n in range(STEP // 128):
                o_ref[c * (STEP // 128) + n, h * 64 : h * 64 + 64, :] = out[:, n * 128 : (n + 1) * 128]


def run_attend(packed):
    return call(
        attend_kernel,
        (1,),
        [whole(packed)],
        [out_whole((8, 128, 128), bf16), out_whole((2, SEQ_LEN), f32)],
        flops=8 * 1024 * 1024 * 128,
        moved=1 << 20,
    )


def attend_back_kernel(p_ref, b_ref, log_ref, o_ref):
    for h in range(2):
        q = join_tokens(p_ref, h * 64)
        k = join_tokens(p_ref, 128 + h * 64)
        v = join_tokens(p_ref, 256 + h * 64)
        gb = join_tokens(b_ref, h * 64)
        gk = gv = None
        for c in range(SEQ_LEN // STEP):
            cols = slice(c * STEP, (c + 1) * STEP)
            qc, gc = q[:, cols], gb[:, cols]
            probs = jnp.exp(mm(k, qc, TN) * FACTOR - log_ref[h : h + 1, cols])
            gp = mm(v, gc, TN)
            row = jnp.sum(probs * gp, axis=0, keepdims=True)
            ds = (probs * (gp - row)).astype(bf16)
            tv = mm(gc, probs.astype(bf16), NT)
            tk = mm(qc, ds, NT)
            gv = tv if gv is None else gv + tv
            gk = tk if gk is None else gk + tk
            gq = (mm(k, ds, NN) * FACTOR).astype(bf16)
            for n in range(STEP // 128):
                o_ref[c * (STEP // 128) + n, h * 64 : h * 64 + 64, :] = gq[:, n * 128 : (n + 1) * 128]
        gk = (gk * FACTOR).astype(bf16)
        gv = gv.astype(bf16)
        for c in range(8):
            o_ref[c, 128 + h * 64 : 192 + h * 64, :] = gk[:, c * 128 : (c + 1) * 128]
            o_ref[c, 256 + h * 64 : 320 + h * 64, :] = gv[:, c * 128 : (c + 1) * 128]


def run_attend_back(packed, grad, log):
    return call(
        attend_back_kernel,
        (1,),
        [whole(packed), whole(grad), whole(log)],
        [out_whole((8, 384, 128), bf16)],
        flops=20 * 1024 * 1024 * 128,
        moved=2 << 20,
    )[0]


def seq_swap(values):
    return lax.all_to_all(values, SEQ, 0, 0, tiled=True)


def norm_forward(summed, gain, shift):
    centre = jnp.mean(summed, axis=0, keepdims=True)
    centred = summed - centre
    variance = jnp.mean(centred * centred, axis=0, keepdims=True)
    scaled = lax.rsqrt(variance + epsilon)
    normed = centred * scaled
    return normed * gain[:, None] + shift[:, None], normed, scaled


def norm_backward(incoming, normed, scaled, gain):
    grad_norm = incoming * gain[:, None]
    plain = jnp.mean(grad_norm, axis=0, keepdims=True)
    cross = jnp.mean(grad_norm * normed, axis=0, keepdims=True)
    return scaled * (grad_norm - plain - normed * cross)


def on_device(
    tokens,
    w_qkv,
    bias_qv,
    w_out,
    bias_out,
    gain_attn,
    shift_attn,
    w_up,
    bias_up,
    w_down,
    bias_down,
    gain_ffn,
    shift_ffn,
    cotangent,
):
    core = lax.axis_index(CORE)
    here = core.astype(jnp.int32).reshape(1)
    traded = trade(
        jnp.concatenate([w_qkv.reshape(LAYERS, 192, 128), w_up.reshape(LAYERS, 256, 128)], axis=1)
    )
    pack = jnp.concatenate(
        [
            traded[:, :192],
            w_out,
            traded[:, 192:],
            w_down.reshape(LAYERS, 64, 4, 128).transpose(0, 2, 1, 3).reshape(LAYERS, 256, 128),
        ],
        axis=1,
    )
    every = lax.all_gather(pack, CHIPS, axis=0, tiled=False).reshape(4, 4, 2, 2, LAYERS, 768, 128)

    small = jnp.concatenate(
        [
            v.reshape(-1)
            for v in (bias_qv, bias_out, gain_attn, shift_attn, bias_down, gain_ffn, shift_ffn, bias_up)
        ]
    )
    small = lax.all_to_all(
        jnp.broadcast_to(small[None], (16, small.shape[0])), COL, 0, 0, tiled=True
    )
    b_qv = small[:, :256].reshape(4, 2, 2, LAYERS, 2, 64)
    b_qv = pick(b_qv, core, 1).transpose(2, 0, 1, 3, 4)
    b_qkv = jnp.stack([b_qv[:, :, :, 0], jnp.zeros_like(b_qv[:, :, :, 0]), b_qv[:, :, :, 1]], axis=3)
    b_qkv = jnp.broadcast_to(b_qkv.reshape(LAYERS, 4, 2, 192, 1), (LAYERS, 4, 2, 192, 128))
    features = small[:, 256:1024].reshape(16, 6, LAYERS, 64).transpose(1, 2, 0, 3).reshape(6, LAYERS, D)
    b_out, g_attn, s_attn, b_down, g_ffn, s_ffn = features
    b_up = small[:, 1024:].reshape(4, 2, 2, LAYERS, 256)
    b_up = pick(b_up, core, 1).transpose(2, 0, 1, 3)
    b_up = jnp.broadcast_to(b_up[..., None], (LAYERS, 4, 2, 256, 128))

    stream = lax.all_to_all(tokens, COL, 1, 0, tiled=True).astype(f32)
    back = lax.all_to_all(cotangent, COL, 1, 0, tiled=True).astype(f32)
    stored = []
    for l in range(LAYERS):
        seen = core_gather(stream.astype(bf16))
        packed = seq_swap(run_qkv(l, every, seen, b_qkv[l]))
        mixed, log = run_attend(packed)
        pair, blended = run_out(l, here, every, seq_swap(mixed))
        attn_out = core_add(pair) + b_out[l][:, None]
        first, n_attn, i_attn = norm_forward(stream + attn_out, g_attn[l], s_attn[l])
        first_seen = core_gather(first.astype(bf16))
        pair, active, slope = run_ffn(l, here, every, first_seen, b_up[l])
        lower = core_add(pair) + b_down[l][:, None]
        stream, n_ffn, i_ffn = norm_forward(first + lower, g_ffn[l], s_ffn[l])
        stored.append((seen, packed, log, blended, n_attn, i_attn, first_seen, active, slope, n_ffn, i_ffn))
    result = lax.all_to_all(stream.astype(bf16), COL, 0, 1, tiled=True)

    big = [None] * LAYERS
    minor = [None] * LAYERS
    for l in reversed(range(LAYERS)):
        (seen, packed, log, blended, n_attn, i_attn, first_seen, active, slope, n_ffn, i_ffn) = stored[l]
        grad_sum = norm_backward(back, n_ffn, i_ffn, g_ffn[l])
        p_gain_ffn = jnp.sum(back * n_ffn, axis=1)
        p_shift_ffn = jnp.sum(back, axis=1)
        low = grad_sum.astype(bf16)
        p_down = jnp.sum(low.astype(f32), axis=1)
        pair, gd, gu, p_up = run_ffn_back(l, here, every, core_gather(low), active, slope, first_seen)
        gw_down = reduce_both(gd, Y, COL)
        gw_up = reduce_both(gu.reshape(4, 16, 256, 128), X, ("y",) + Z)
        grad_first = core_add(pair) + grad_sum
        p_gain_attn = jnp.sum(grad_first * n_attn, axis=1)
        p_shift_attn = jnp.sum(grad_first, axis=1)
        grad_total = norm_backward(grad_first, n_attn, i_attn, g_attn[l])
        low = grad_total.astype(bf16)
        p_out = jnp.sum(low.astype(f32), axis=1)
        low = core_gather(low)
        grad_blended = seq_swap(run_out_back(l, every, low))
        grad_qkv = seq_swap(run_attend_back(packed, grad_blended, log))
        pair, gqo, p_qkv = run_qkv_back(l, here, every, grad_qkv, seen, low, blended)
        gw_qo = reduce_both(gqo.reshape(4, 16, 256, 128), Z, ("y",) + X)
        back = core_add(pair) + grad_total
        swapped = trade(jnp.concatenate([gw_qo[:192], gw_up], axis=0).astype(bf16)).astype(f32)
        gw_down = gw_down.reshape(4, 64, 128).transpose(1, 0, 2).reshape(64, 512)
        big[l] = (swapped[:192].reshape(3, 64, 128), gw_qo[192:], swapped[192:], gw_down)
        minor[l] = (p_qkv, p_out, p_gain_attn, p_shift_attn, p_down, p_gain_ffn, p_shift_ffn, p_up)
    grad_tokens = lax.all_to_all(back.astype(bf16), COL, 0, 1, tiled=True).astype(f32)

    mine = (jnp.arange(2) == core).astype(f32)
    qv = jnp.stack([m[0].reshape(4, 2, 3, 64)[:, :, ::2] for m in minor])
    qv = qv.transpose(1, 2, 0, 3, 4)
    qv = (qv[:, None] * mine[None, :, None, None, None, None]).reshape(16, 256)
    up = jnp.stack([m[7] for m in minor]).reshape(LAYERS, 4, 2, 256).transpose(1, 2, 0, 3)
    up = (up[:, None] * mine[None, :, None, None, None]).reshape(16, 512)
    feats = jnp.stack([jnp.stack([m[i] for m in minor]) for i in range(1, 7)])
    feats = feats.reshape(6, LAYERS, 16, 64).transpose(2, 0, 1, 3).reshape(16, 768)
    sums = jnp.concatenate([qv, feats, up], axis=1).reshape(4, 4, 12, 128)
    sums2 = sum_axis(reduce_stage(sums.reshape(16, 12, 128), COL), Y)
    sums2 = sums2 + lax.ppermute(sums2, CORE, [(0, 1), (1, 0)])
    flat = sums2.reshape(1536)
    o_qv = flat[:256].reshape(LAYERS, 2, 64)
    o_out, o_gain_attn, o_shift_attn, o_down, o_gain_ffn, o_shift_ffn = flat[256:1024].reshape(6, LAYERS, 64)
    o_up = flat[1024:].reshape(LAYERS, 256)
    gw_qkv, gw_out, gw_up, gw_down = [jnp.stack([b[i] for b in big]) for i in range(4)]
    return (
        result,
        grad_tokens,
        gw_qkv,
        o_qv,
        gw_out,
        o_out,
        o_gain_attn,
        o_shift_attn,
        gw_up,
        o_up,
        gw_down,
        o_down,
        o_gain_ffn,
        o_shift_ffn,
    )


def solution(mesh):
    fine = Mesh(mesh.devices.reshape(4, 2, 2, 2, 2, 2), ("y", "k", "xh", "xl", "zh", "zl"))
    row = ("y", "k")
    col = COL
    in_specs = (
        P(col, row),
        P(None, None, col, row),
        P(None, None, col),
        P(None, col, row),
        P(None, col),
        P(None, col),
        P(None, col),
        P(None, col, row),
        P(None, col),
        P(None, col, row),
        P(None, col),
        P(None, col),
        P(None, col),
        P(col, row),
    )
    out_specs = (
        P(col, row),
        P(col, row),
        P(None, None, col, row),
        P(None, None, col),
        P(None, col, row),
        P(None, col),
        P(None, col),
        P(None, col),
        P(None, col, row),
        P(None, col),
        P(None, col, row),
        P(None, col),
        P(None, col),
        P(None, col),
    )
    return jax.shard_map(
        on_device, mesh=fine, in_specs=in_specs, out_specs=out_specs, check_vma=False
    )
```

time: 1010 us -> 878 us (0.87)
  local copies, waits for them, and re-layouts: 342 us -> 29.2 us
  blocking collectives: 28.1 us -> 275 us
  Pallas kernels: 0 us -> 93.9 us
  matrix products: 78.2 us -> 0 us
  starting transfers between devices: 184 us -> 136 us
  other arithmetic: 87.4 us -> 56.7 us
    all_to_all x0 -> x11, blocking collectives: none -> 252 us  [the longest x5 176 us: reduce_stage(): lax.all_to_all(g, axes, 0, 0, tiled=True).astype(f32)]
    reshape x32 -> x2, local copies, waits for them, and re-layouts: 123 us -> 0.18 us  [on_device(): qv = jnp.stack([m[0].reshape(4, 2, 3, 64)[:, :, ::2] for m in minor])]
    ppermute x68 -> x8, waiting for transfers between devices: 109 us -> 5.29 us  [core_add(): return keep + lax.ppermute(send, CORE, [(0, 1), (1, 0)]).astype(f32)]
    all_to_all x9 -> x11, waiting for transfers between devices: 31.8 us -> 133 us  [the longest x8 116 us: reduce_stage(): lax.all_to_all(g, axes, 0, 0, tiled=True).astype(f32)]
    pallas_call x0 -> x16, Pallas kernels: none -> 93.9 us  [call(): pl.pallas_call(kernel, grid=grid, in_specs=[spec for spec, _ in ins], out...]
    dynamic_slice x38 -> x0, local copies, waits for them, and re-layouts: 82.6 us -> none  [pick(): return lax.dynamic_index_in_dim(values, index, dim, keepdims=False)]
    ppermute x68 -> x8, starting transfers between devices: 93.7 us -> 11.1 us  [core_add(): return keep + lax.ppermute(send, CORE, [(0, 1), (1, 0)]).astype(f32)]
    dot_general x36 -> x0, matrix products: 78.2 us -> none  [the longest x24 54.1 us: dot(): lax.dot_general(a, b, (((ca,), (cb,)), ((), ())), preferred_element_type=...]
  transfers between devices with their start and end apart: 89 -> 31, of which waited for: 26 -> 23; matrix products, arithmetic and copies ran while one was open for 42% -> 7% of each run, Pallas kernels for 0% -> 2%
where the time goes in v2:
time: 878 us; the launch traced here: 866 us
  blocking collectives  275 us (31%)
  waiting for transfers between devices  260 us (30%)
  starting transfers between devices  136 us (15%)
  Pallas kernels  93.9 us (11%)
  other arithmetic  56.7 us (6%)
  local copies, waits for them, and re-layouts  29.2 us (3%)
  between operations  15.5 us (2%)
    all_to_all x5, blocking collectives, reduce_stage(): lax.all_to_all(g, axes, 0, 0, tiled=True).astype(f32)  176 us
    all_to_all x8, waiting for transfers between devices, reduce_stage(): lax.all_to_all(g, axes, 0, 0, tiled=True).astype(f32)  116 us
    all_gather x1, waiting for transfers between devices, on_device(): lax.all_gather(pack, CHIPS, axis=0, tiled=False)  97.1 us
    pallas_call x16, Pallas kernels, call(): pl.pallas_call(kernel, grid=grid, in_specs=[spec for spec, _ in ins], out...  93.9 us
    all_to_all x5, blocking collectives, seq_swap(): return lax.all_to_all(values, SEQ, 0, 0, tiled=True)  65.2 us
    all_to_all x8, starting transfers between devices, reduce_stage(): lax.all_to_all(g, axes, 0, 0, tiled=True).astype(f32)  42.5 us
    ppermute x3, starting transfers between devices, trade(): return lax.ppermute(values, (CORE, 'zh'), [(0, 0), (1, 2), (2, 1), (3, 3)])  34.2 us
    reduce_sum x13, other arithmetic, reduce_stage(): jnp.sum(lax.all_to_all(g, axes, 0, 0, tiled=True).astype(f32), axis=0)  29 us
  transfers between devices with their start and end apart: 31, of which 23 were waited for; matrix products, arithmetic and copies ran while one was open for 7% of the time, Pallas kernels for 2%

profile of v2, /device:TPU:1, one launch (start us, length us, event | category | flops | bytes accessed | tf_op | source)
XLA Modules:
  0.0 866.3 jit_solution(2167135930534028163)
XLA Ops:
  8.3 6.9 collective-permute-start
  27.2 4.6 all-to-all-start.1
  32.7 5.8 all-to-all-done.1
  42.3 7.3 all-to-all-done
  49.7 6.9 all_gather.32.x_ref
  56.5 97.1 %all-gather.3.cloned.1.call-done = bf16[128,768,128]{2,1,0:T(8,128)(2,1)} async-done(((bf16[2,768,128]{2,1,0:T(8,128)(2,1)}), bf16[128,768,128]{2,1,0:T(8,128)(2,1)}) %all-gather.3.cloned.1.call-update) | async-done | bytes 25165840 | tf_op jit(solution)/shard_map/all_gather | solution.py:523
  157.5 16.1 %all_to_all.178.p_ref = bf16[8,384,128]{2,1,0:T(8,128)(2,1)S(1)} all-to-all(bf16[8,384,128]{2,1,0:T(8,128)(2,1)S(1)} %bitcast.133), channel_id=1, replica_groups=mesh['y'=4,'k'=2,'xh'=2,'xl'=2,'zh'=2,'zl'=2] {'xl','zh','zl'}, dimensions={0} | all-to-all | bytes 1572864 | tf_op jit(solution)/shard_map/all_to_all | solution.py:474
  173.6 7.2 shard_map.246
  185.2 5.9 all-to-all-done.3.b_ref
  200.9 7.7 shard_map.248
  218.4 13.9 %all_to_all.179.p_ref = bf16[8,384,128]{2,1,0:T(8,128)(2,1)S(1)} all-to-all(bf16[8,384,128]{2,1,0:T(8,128)(2,1)S(1)} %bitcast.134), channel_id=1, replica_groups=mesh['y'=4,'k'=2,'xh'=2,'xl'=2,'zh'=2,'zl'=2] {'xl','zh','zl'}, dimensions={0} | all-to-all | bytes 1572864 | tf_op jit(solution)/shard_map/all_to_all | solution.py:474
  232.4 6.5 shard_map.250
  238.9 10.0 %all_to_all.180.b_ref = bf16[8,128,128]{2,1,0:T(8,128)(2,1)S(1)} all-to-all(bf16[8,128,128]{2,1,0:T(8,128)(2,1)S(1)} %get-tuple-element.55), channel_id=1, replica_groups=mesh['y'=4,'k'=2,'xh'=2,'xl'=2,'zh'=2,'zl'=2] {'xl','zh','zl'}, dimensions={0} | all-to-all | bytes 524288 | tf_op jit(solution)/shard_map/all_to_all | solution.py:474
  264.1 7.8 shard_map.252
  282.9 10.1 %shard_map.253 = (f32[1024,128]{1,0:T(8,128)S(1)}, bf16[1024,128]{1,0:T(8,128)(2,1)}, bf16[4,16,256,128]{3,2,1,0:T(8,128)(2,1)}, bf16[4,4,2,2,256,128]{5,4,3,2,1,0:T(8,128)(2,1)}, f32[2048,1]{1,0:T(8,128)S(1)}) custom-call(s32[1]{0:T(128)} %bitcast.2.core_ref, bf16[4,4,2,2,2,768,128]{6,5,4,3,2,1,0:T(8,128)(2,1)} %bitcast.143, ...), custom_call_target="tpu_custom_call" | custom-call | flops 4294967296 | bytes 23068672 | tf_op jit(solution)/shard_map/pallas_call | solution.py:68
  304.6 11.2 %all_to_all.181.b_ref = bf16[8,128,128]{2,1,0:T(8,128)(2,1)S(1)} all-to-all(bf16[8,128,128]{2,1,0:T(8,128)(2,1)S(1)} %shard_map.254), channel_id=1, replica_groups=mesh['y'=4,'k'=2,'xh'=2,'xl'=2,'zh'=2,'zl'=2] {'xl','zh','zl'}, dimensions={0} | all-to-all | bytes 524288 | tf_op jit(solution)/shard_map/all_to_all | solution.py:474
  315.8 6.8 shard_map.255
  322.6 14.0 %all_to_all.182 = bf16[8,384,128]{2,1,0:T(8,128)(2,1)S(1)} all-to-all(bf16[8,384,128]{2,1,0:T(8,128)(2,1)S(1)} %shard_map.255), channel_id=1, replica_groups=mesh['y'=4,'k'=2,'xh'=2,'xl'=2,'zh'=2,'zl'=2] {'xl','zh','zl'}, dimensions={0} | all-to-all | bytes 1572864 | tf_op jit(solution)/shard_map/all_to_all | solution.py:474
  336.6 6.8 shard_map.256
  351.0 10.1 %shard_map.257 = (f32[1024,128]{1,0:T(8,128)S(1)}, bf16[1024,128]{1,0:T(8,128)(2,1)S(1)}, bf16[4,16,256,128]{3,2,1,0:T(8,128)(2,1)}, bf16[4,4,2,2,256,128]{5,4,3,2,1,0:T(8,128)(2,1)}, f32[2048,1]{1,0:T(8,128)S(1)}) custom-call(s32[1]{0:T(128)} %bitcast.2.core_ref, bf16[4,4,2,2,2,768,128]{6,5,4,3,2,1,0:T(8,128)(2,1)} %bitcast.147, ...), custom_call_target="tpu_custom_call" | custom-call | flops 4294967296 | bytes 23068672 | tf_op jit(solution)/shard_map/pallas_call | solution.py:68
  380.2 8.6 shard_map.259
  393.7 8.6 all-to-all-done.11
  402.3 7.9 all-to-all-start.6
  410.2 6.7 shard_map.260
  420.2 7.0 all-to-all-start.21
  428.7 5.3 all-to-all-done.21
  434.0 10.7 %all_to_all.183 = bf16[16,64,128]{2,1,0:T(8,128)(2,1)S(1)} all-to-all(bf16[16,64,128]{2,1,0:T(8,128)(2,1)S(1)} %bitcast.156), channel_id=1, replica_groups=mesh['y'=4,'k'=2,'xh'=2,'xl'=2,'zh'=2,'zl'=2] {'xh','xl','zh','zl'}, dimensions={0} | all-to-all | bytes 524288 | tf_op jit(solution)/shard_map/all_to_all | solution.py:589
  444.7 51.9 %all_to_all.184 = bf16[4,16,256,128]{3,2,1,0:T(8,128)(2,1)} all-to-all(bf16[4,16,256,128]{3,2,1,0:T(8,128)(2,1)} %bitcast.151), channel_id=1, replica_groups=mesh['y'=4,'k'=2,'xh'=2,'xl'=2,'zh'=2,'zl'=2] {'xh','xl'}, dimensions={0} | all-to-all | bytes 8388608 | tf_op jit(solution)/shard_map/all_to_all | solution.py:52
  496.6 4.9 all-to-all-start.24
  505.7 41.1 %all-to-all-done.24 = bf16[4,16,256,128]{3,2,1,0:T(8,128)(2,1)} async-done(((bf16[4,16,256,128]{3,2,1,0:T(8,128)(2,1)}), bf16[4,16,256,128]{3,2,1,0:T(8,128)(2,1)}, u32[]{:S(2)}, u32[]{:S(2)}) %all-to-all-start.24) | async-done | bytes 4194336 | tf_op jit(solution)/shard_map/all_to_all | solution.py:52
  554.0 9.0 %all-to-all-done.20 = bf16[16,256,128]{2,1,0:T(8,128)(2,1)S(1)} async-done(((bf16[16,256,128]{2,1,0:T(8,128)(2,1)}), bf16[16,256,128]{2,1,0:T(8,128)(2,1)S(1)}, u32[]{:S(2)}, u32[]{:S(2)}) %all-to-all-start.20) | async-done | bytes 1048608 | tf_op jit(solution)/shard_map/all_to_all | solution.py:52
  563.0 15.1 %all_to_all.185 = bf16[16,256,128]{2,1,0:T(8,128)(2,1)} all-to-all(bf16[16,256,128]{2,1,0:T(8,128)(2,1)S(1)} %reduce_sum.426), channel_id=1, replica_groups=mesh['y'=4,'k'=2,'xh'=2,'xl'=2,'zh'=2,'zl'=2] {'xh','xl','zh','zl'}, dimensions={0} | all-to-all | bytes 2097152 | tf_op jit(solution)/shard_map/all_to_all | solution.py:52
  578.1 47.5 %all_to_all.186 = bf16[4,16,256,128]{3,2,1,0:T(8,128)(2,1)} all-to-all(bf16[4,16,256,128]{3,2,1,0:T(8,128)(2,1)} %bitcast.152), channel_id=1, replica_groups=mesh['y'=4,'k'=2,'xh'=2,'xl'=2,'zh'=2,'zl'=2] {'zh','zl'}, dimensions={0} | all-to-all | bytes 8388608 | tf_op jit(solution)/shard_map/all_to_all | solution.py:52
  625.6 44.0 %all_to_all.187 = bf16[4,16,256,128]{3,2,1,0:T(8,128)(2,1)} all-to-all(bf16[4,16,256,128]{3,2,1,0:T(8,128)(2,1)S(1)} %bitcast.153), channel_id=1, replica_groups=mesh['y'=4,'k'=2,'xh'=2,'xl'=2,'zh'=2,'zl'=2] {'xh','xl'}, dimensions={0} | all-to-all | bytes 8388608 | tf_op jit(solution)/shard_map/all_to_all | solution.py:52
  669.6 5.5 all-to-all-start.22
  679.4 36.2 %all-to-all-done.22 = bf16[4,16,256,128]{3,2,1,0:T(8,128)(2,1)} async-done(((bf16[4,16,256,128]{3,2,1,0:T(8,128)(2,1)}), bf16[4,16,256,128]{3,2,1,0:T(8,128)(2,1)}, u32[]{:S(2)}, u32[]{:S(2)}) %all-to-all-start.22) | async-done | bytes 4194336 | tf_op jit(solution)/shard_map/all_to_all | solution.py:52
  715.7 5.4 all-to-all-start.18
  721.1 4.3 reduce_sum.405
  725.4 8.0 all-to-all-done.18
  733.4 17.2 %all_to_all.188 = bf16[16,256,128]{2,1,0:T(8,128)(2,1)S(1)} all-to-all(bf16[16,256,128]{2,1,0:T(8,128)(2,1)} %reduce_sum.405), channel_id=1, replica_groups=mesh['y'=4,'k'=2,'xh'=2,'xl'=2,'zh'=2,'zl'=2] {'y','zh','zl'}, dimensions={0} | all-to-all | bytes 2097152 | tf_op jit(solution)/shard_map/all_to_all | solution.py:52
  750.5 4.8 all-to-all-start.13
  762.6 13.8 %collective-permute-start.14 = (f32[12,128]{1,0:T(8,128)S(1)}, f32[12,128]{1,0:T(8,128)S(1)}, u32[]{:S(2)}, u32[]{:S(2)}) collective-permute-start(f32[12,128]{1,0:T(8,128)S(1)} %add_add_fusion.7), channel_id=1, source_target_pairs={{0,16},{16,0},{1,17},{17,1},{2,18},{18,2},{3,19},{19,3},{4,20},{20... | collective-permute-start | bytes 18440 | tf_op jit(solution)/shard_map/ppermute | solution.py:601
  776.3 4.3 reduce_sum.424
  780.6 16.0 %all-to-all-done.13 = bf16[4,16,256,128]{3,2,1,0:T(8,128)(2,1)} async-done(((bf16[4,16,256,128]{3,2,1,0:T(8,128)(2,1)}), bf16[4,16,256,128]{3,2,1,0:T(8,128)(2,1)}, u32[]{:S(2)}, u32[]{:S(2)}) %all-to-all-start.13) | async-done | bytes 4194336 | tf_op jit(solution)/shard_map/all_to_all | solution.py:52
  796.6 4.6 all-to-all-start.23
  814.8 6.1 all-to-all-start.14
  822.4 20.7 %collective-permute-start.10 = (bf16[448,128]{1,0:T(8,128)(2,1)S(1)}, bf16[448,128]{1,0:T(8,128)(2,1)S(1)}, u32[]{:S(2)}, u32[]{:S(2)}) collective-permute-start(bf16[448,128]{1,0:T(8,128)(2,1)S(1)} %pad_maximum_fusion.6), channel_id=1, source_target_pairs={{0,0},{2,16},{16,2},{18,18},{1,1},{3,17},{17,3},{19,19},{4,4},{6,2... | collective-permute-start | bytes 344072 | tf_op jit(solution)/shard_map/ppermute | solution.py:44
  848.5 6.6 collective-permute-start.9
  (301 shorter events, 166.2 us)
Async XLA Ops:
  7.2 24.6 %copy-start = (bf16[64,2048]{1,0:T(8,128)(2,1)S(1)}, bf16[64,2048]{1,0:T(8,128)(2,1)}, u32[]{:S(2)}) copy-start(bf16[64,2048]{1,0:T(8,128)(2,1)} %param.14) | copy-start | bytes 786436
  7.2 146.4 %all-gather.3.cloned.1.call-start = ((), (), s32[]{:S(2)}) async-start(), calls=%async_computation.26 | async-start | bytes 25559040 | tf_op jit(solution)/shard_map/all_gather | solution.py:523
  8.3 10.6 %collective-permute-start = (bf16[2,448,128]{2,1,0:T(8,128)(2,1)S(1)}, bf16[2,448,128]{2,1,0:T(8,128)(2,1)S(1)}, u32[]{:S(2)}, u32[]{:S(2)}) collective-permute-start(bf16[2,448,128]{2,1,0:T(8,128)(2,1)S(1)} %pad_maximum_fusion.3), channel_id=1, source_target_pairs={{0,0},{2,16},{16,2},{18,18},{1,1},{3,17},{17,3},{19,19},{4,4},{6,2... | collective-permute-start | bytes 688136 | tf_op jit(solution)/shard_map/ppermute | solution.py:44
  27.2 11.2 %all-to-all-start.1 = ((f32[16,1,1536]{2,1,0:T(1,128)}), f32[16,1,1536]{2,1,0:T(1,128)S(1)}, u32[]{:S(2)}, u32[]{:S(2)}) async-start(f32[16,1,1536]{2,1,0:T(1,128)} %broadcast_in_dim.18), calls=%async_computation.1 | async-start | bytes 196608 | tf_op jit(solution)/shard_map/all_to_all | solution.py:531
  38.5 11.2 %all-to-all-start = ((bf16[64,16,128]{2,0,1:T(8,128)(2,1)}), bf16[64,16,128]{2,0,1:T(8,128)(2,1)S(1)}, u32[]{:S(2)}, u32[]{:S(2)}) async-start(bf16[64,16,128]{2,0,1:T(8,128)(2,1)} %copy_bitcast_fusion.3), calls=%async_computation | async-start | bytes 524288 | tf_op jit(solution)/shard_map/all_to_all | solution.py:544
  181.7 9.4 %all-to-all-start.3 = ((bf16[8,128,128]{2,1,0:T(8,128)(2,1)}), bf16[8,128,128]{2,1,0:T(8,128)(2,1)S(1)}, u32[]{:S(2)}, u32[]{:S(2)}) async-start(bf16[8,128,128]{2,1,0:T(8,128)(2,1)} %get-tuple-element.50), calls=%async_computation.3 | async-start | bytes 524288 | tf_op jit(solution)/shard_map/all_to_all | solution.py:474
  192.8 4.8 collective-permute-start.1
  198.0 12.1 %copy-start.26 = (f32[128]{0:T(128)}, f32[128]{0:T(128)S(1)}, u32[]{:S(2)}) copy-start(f32[128]{0:T(128)S(1)} %add_rsqrt_fusion.3) | copy-start | bytes 1540
  208.6 1.5 collective-permute-start.2
  211.9 136.3 %copy-start.28 = (f32[128]{0:T(128)}, f32[128]{0:T(128)S(1)}, u32[]{:S(2)}) copy-start(f32[128]{0:T(128)S(1)} %add_rsqrt_fusion.2) | copy-start | bytes 1540
  232.4 6.5 copy-start.8
  252.0 7.4 collective-permute-start.3
  254.9 19.2 %all-to-all-start.7 = ((bf16[64,16,128]{2,0,1:T(8,128)(2,1)}), bf16[64,16,128]{2,0,1:T(8,128)(2,1)}, u32[]{:S(2)}, u32[]{:S(2)}) async-start(bf16[64,16,128]{2,0,1:T(8,128)(2,1)} %copy_bitcast_fusion.2), calls=%async_computation.7 | async-start | bytes 524288 | tf_op jit(solution)/shard_map/all_to_all | solution.py:545
  273.8 1.9 collective-permute-start.4
  274.1 8.8 %copy-start.3 = (bf16[2048,256]{1,0:T(8,128)(2,1)S(1)}, bf16[2048,256]{1,0:T(8,128)(2,1)}, u32[]{:S(2)}) copy-start(bf16[2048,256]{1,0:T(8,128)(2,1)} %copy-done.2) | copy-start | bytes 3145732
  294.9 1.7 collective-permute-start.5
  302.8 13.0 %copy-start.9 = (bf16[8,384,128]{2,1,0:T(8,128)(2,1)S(1)}, bf16[8,384,128]{2,1,0:T(8,128)(2,1)}, u32[]{:S(2)}) copy-start(bf16[8,384,128]{2,1,0:T(8,128)(2,1)} %copy-done.8) | copy-start | bytes 2359300
  315.8 20.8 %copy-start.14 = (bf16[512,256]{1,0:T(8,128)(2,1)S(1)}, bf16[512,256]{1,0:T(8,128)(2,1)}, u32[]{:S(2)}) copy-start(bf16[512,256]{1,0:T(8,128)(2,1)} %copy-done.13) | copy-start | bytes 786436
  336.6 10.9 %copy-start.19 = (f32[1024,128]{1,0:T(8,128)S(1)}, f32[1024,128]{1,0:T(8,128)}, u32[]{:S(2)}) copy-start(f32[1024,128]{1,0:T(8,128)} %copy-done.18) | copy-start | bytes 1572868
  336.6 10.9 %copy-start.21 = (f32[1024,128]{1,0:T(8,128)S(1)}, f32[1024,128]{1,0:T(8,128)}, u32[]{:S(2)}) copy-start(f32[1024,128]{1,0:T(8,128)} %copy-done.20) | copy-start | bytes 1572868
  343.4 7.6 copy-start.10
  343.4 4.1 collective-permute-start.6
  351.0 11.7 %copy-start.17 = (f32[1024,128]{1,0:T(8,128)S(1)}, f32[1024,128]{1,0:T(8,128)}, u32[]{:S(2)}) copy-start(f32[1024,128]{1,0:T(8,128)} %copy-done.16) | copy-start | bytes 1572868
  351.0 11.7 %copy-start.27 = (f32[128]{0:T(128)S(1)}, f32[128]{0:T(128)}, u32[]{:S(2)}) copy-start(f32[128]{0:T(128)} %copy-done.26) | copy-start | bytes 1540
  351.0 11.7 %copy-start.29 = (f32[128]{0:T(128)S(1)}, f32[128]{0:T(128)}, u32[]{:S(2)}) copy-start(f32[128]{0:T(128)} %copy-done.28) | copy-start | bytes 1540
  361.1 1.5 collective-permute-start.7
  366.3 6.9 copy-start.5
  368.8 10.2 %all-to-all-start.10 = ((bf16[8,128,128]{2,1,0:T(8,128)(2,1)}), bf16[8,128,128]{2,1,0:T(8,128)(2,1)}, u32[]{:S(2)}, u32[]{:S(2)}) async-start(bf16[8,128,128]{2,1,0:T(8,128)(2,1)} %shard_map.258), calls=%async_computation.10 | async-start | bytes 524288 | tf_op jit(solution)/shard_map/all_to_all | solution.py:474
  388.8 13.5 %all-to-all-start.11 = ((bf16[8,384,128]{2,1,0:T(8,128)(2,1)}), bf16[8,384,128]{2,1,0:T(8,128)(2,1)S(1)}, u32[]{:S(2)}, u32[]{:S(2)}) async-start(bf16[8,384,128]{2,1,0:T(8,128)(2,1)} %shard_map.259), calls=%async_computation.11 | async-start | bytes 1572864 | tf_op jit(solution)/shard_map/all_to_all | solution.py:474
  402.3 18.0 %all-to-all-start.6 = ((bf16[16,64,128]{2,1,0:T(8,128)(2,1)}), bf16[16,64,128]{2,1,0:T(8,128)(2,1)}, u32[]{:S(2)}, u32[]{:S(2)}) async-start(bf16[16,64,128]{2,1,0:T(8,128)(2,1)} %bitcast.17), calls=%async_computation.6 | async-start | bytes 524288 | tf_op jit(solution)/shard_map/all_to_all | solution.py:559
  410.2 17.1 %copy-start.31 = (f32[128]{0:T(128)S(1)}, f32[128]{0:T(128)}, u32[]{:S(2)}) copy-start(f32[128]{0:T(128)} %copy-done.30) | copy-start | bytes 1540
  418.3 8.9 %collective-permute-start.8 = (bf16[1024,128]{1,0:T(8,128)(2,1)}, bf16[1024,128]{1,0:T(8,128)(2,1)S(1)}, u32[]{:S(2)}, u32[]{:S(2)}) collective-permute-start(bf16[1024,128]{1,0:T(8,128)(2,1)} %copy-done.15), channel_id=1, source_target_pairs={{0,16},{16,0},{1,17},{17,1},{2,18},{18,2},{3,19},{19,3},{4,20},{20... | collective-permute-start | bytes 786440 | tf_op jit(solution)/shard_map/ppermute | solution.py:40
  420.2 13.8 %all-to-all-start.21 = ((f32[16,12,128]{2,1,0:T(8,128)}), f32[16,12,128]{2,1,0:T(8,128)S(1)}, u32[]{:S(2)}, u32[]{:S(2)}) async-start(f32[16,12,128]{2,1,0:T(8,128)} %reshape_reshape.3), calls=%async_computation.21 | async-start | bytes 262144 | tf_op jit(solution)/shard_map/all_to_all | solution.py:52
  496.6 50.2 %all-to-all-start.24 = ((bf16[4,16,256,128]{3,2,1,0:T(8,128)(2,1)}), bf16[4,16,256,128]{3,2,1,0:T(8,128)(2,1)}, u32[]{:S(2)}, u32[]{:S(2)}) async-start(bf16[4,16,256,128]{3,2,1,0:T(8,128)(2,1)} %get-tuple-element.85), calls=%async_computation.24 | async-start | bytes 8388608 | tf_op jit(solution)/shard_map/all_to_all | solution.py:52
  546.8 16.2 %all-to-all-start.20 = ((bf16[16,256,128]{2,1,0:T(8,128)(2,1)}), bf16[16,256,128]{2,1,0:T(8,128)(2,1)S(1)}, u32[]{:S(2)}, u32[]{:S(2)}) async-start(bf16[16,256,128]{2,1,0:T(8,128)(2,1)} %reduce_sum.409), calls=%async_computation.20 | async-start | bytes 2097152 | tf_op jit(solution)/shard_map/all_to_all | solution.py:52
  578.1 47.5 %copy-start.24 = (bf16[4,4,2,2,256,128]{5,4,3,2,1,0:T(8,128)(2,1)S(1)}, bf16[4,4,2,2,256,128]{5,4,3,2,1,0:T(8,128)(2,1)}, u32[]{:S(2)}) copy-start(bf16[4,4,2,2,256,128]{5,4,3,2,1,0:T(8,128)(2,1)} %get-tuple-element.77) | copy-start | bytes 12582916
  669.6 46.0 %all-to-all-start.22 = ((bf16[4,16,256,128]{3,2,1,0:T(8,128)(2,1)}), bf16[4,16,256,128]{3,2,1,0:T(8,128)(2,1)}, u32[]{:S(2)}, u32[]{:S(2)}) async-start(bf16[4,16,256,128]{3,2,1,0:T(8,128)(2,1)} %get-tuple-element.84), calls=%async_computation.22 | async-start | bytes 8388608 | tf_op jit(solution)/shard_map/all_to_all | solution.py:52
  715.7 17.7 %all-to-all-start.18 = ((bf16[16,256,128]{2,1,0:T(8,128)(2,1)}), bf16[16,256,128]{2,1,0:T(8,128)(2,1)}, u32[]{:S(2)}, u32[]{:S(2)}) async-start(bf16[16,256,128]{2,1,0:T(8,128)(2,1)} %reduce_sum.407), calls=%async_computation.18 | async-start | bytes 2097152 | tf_op jit(solution)/shard_map/all_to_all | solution.py:52
  750.5 46.1 %all-to-all-start.13 = ((bf16[4,16,256,128]{3,2,1,0:T(8,128)(2,1)}), bf16[4,16,256,128]{3,2,1,0:T(8,128)(2,1)}, u32[]{:S(2)}, u32[]{:S(2)}) async-start(bf16[4,16,256,128]{3,2,1,0:T(8,128)(2,1)} %bitcast.154), calls=%async_computation.13 | async-start | bytes 8388608 | tf_op jit(solution)/shard_map/all_to_all | solution.py:52
  755.4 4.5 collective-permute-start.13
  756.8 3.2 collective-permute-start.12
  758.5 4.0 collective-permute-start.11
  762.6 40.3 %collective-permute-start.14 = (f32[12,128]{1,0:T(8,128)S(1)}, f32[12,128]{1,0:T(8,128)S(1)}, u32[]{:S(2)}, u32[]{:S(2)}) collective-permute-start(f32[12,128]{1,0:T(8,128)S(1)} %add_add_fusion.7), channel_id=1, source_target_pairs={{0,16},{16,0},{1,17},{17,1},{2,18},{18,2},{3,19},{19,3},{4,20},{20... | collective-permute-start | bytes 18440 | tf_op jit(solution)/shard_map/ppermute | solution.py:601
  796.6 18.2 %all-to-all-start.23 = ((bf16[16,256,128]{2,1,0:T(8,128)(2,1)}), bf16[16,256,128]{2,1,0:T(8,128)(2,1)}, u32[]{:S(2)}, u32[]{:S(2)}) async-start(bf16[16,256,128]{2,1,0:T(8,128)(2,1)} %reduce_sum.424), calls=%async_computation.23 | async-start | bytes 2097152 | tf_op jit(solution)/shard_map/all_to_all | solution.py:52
  814.8 33.5 %all-to-all-start.14 = ((bf16[16,256,128]{2,1,0:T(8,128)(2,1)}), bf16[16,256,128]{2,1,0:T(8,128)(2,1)S(1)}, u32[]{:S(2)}, u32[]{:S(2)}) async-start(bf16[16,256,128]{2,1,0:T(8,128)(2,1)} %reduce_sum.403), calls=%async_computation.14 | async-start | bytes 2097152 | tf_op jit(solution)/shard_map/all_to_all | solution.py:52
  820.9 38.1 %copy-start.1 = (bf16[64,2048]{1,0:T(8,128)(2,1)S(1)}, bf16[64,2048]{1,0:T(8,128)(2,1)}, u32[]{:S(2)}) copy-start(bf16[64,2048]{1,0:T(8,128)(2,1)} %param.14) | copy-start | bytes 786436
  822.4 23.5 %collective-permute-start.10 = (bf16[448,128]{1,0:T(8,128)(2,1)S(1)}, bf16[448,128]{1,0:T(8,128)(2,1)S(1)}, u32[]{:S(2)}, u32[]{:S(2)}) collective-permute-start(bf16[448,128]{1,0:T(8,128)(2,1)S(1)} %pad_maximum_fusion.6), channel_id=1, source_target_pairs={{0,0},{2,16},{16,2},{18,18},{1,1},{3,17},{17,3},{19,19},{4,4},{6,2... | collective-permute-start | bytes 344072 | tf_op jit(solution)/shard_map/ppermute | solution.py:44
  848.5 9.1 %collective-permute-start.9 = (bf16[448,128]{1,0:T(8,128)(2,1)S(1)}, bf16[448,128]{1,0:T(8,128)(2,1)S(1)}, u32[]{:S(2)}, u32[]{:S(2)}) collective-permute-start(bf16[448,128]{1,0:T(8,128)(2,1)S(1)} %pad_maximum_fusion.5), channel_id=1, source_target_pairs={{0,0},{2,16},{16,2},{18,18},{1,1},{3,17},{17,3},{19,19},{4,4},{6,2... | collective-permute-start | bytes 344072 | tf_op jit(solution)/shard_map/ppermute | solution.py:44
  (15 other events, 27.3 us)
Sparse Core Ops, SparseCore 0:
  20.6 133.0 all-gather.2

commit v3 on v2

--- a/solution.py
+++ b/solution.py
@@ -1,3 +1,6 @@
+from functools import partial
+from typing import NamedTuple
+
 import jax
 import jax.numpy as jnp
 from jax import lax
@@ -52,9 +55,16 @@
     return jnp.sum(lax.all_to_all(g, axes, 0, 0, tiled=True).astype(f32), axis=0)
 
 
-def reduce_both(g, first, second):
-    h = reduce_stage(g, first).astype(bf16)
-    return reduce_stage(h.reshape(16, 256, 128), second)
+def after(values, *others):
+    return lax.optimization_barrier((values, *others))[0]
+
+
+class Weights(NamedTuple):
+    qo: jax.Array
+    up: jax.Array
+    down: jax.Array
+    up_at: int
+    down_at: int
 
 
 def sum_axis(values, axes):
@@ -101,24 +111,24 @@
 PAIR = (out_whole((D, 128), f32), out_whole((D, 128), bf16))
 
 
-def w_qkv_spec(l):
-    return pl.BlockSpec((4, 1, 2, 2, 1, 192, 128), lambda g: (0, g, 0, 0, l, 0, 0))
-
-
-def w_out_spec(l):
-    return pl.BlockSpec((4, 4, 2, 2, 1, 64, 128), lambda g: (0, 0, 0, 0, l, 3, 0))
-
-
-def w_up_spec(l):
-    return pl.BlockSpec((4, 1, 2, 2, 1, 256, 128), lambda g: (0, g, 0, 0, l, 1, 0))
-
-
-def w_down_spec(l):
-    return pl.BlockSpec((1, 4, 2, 2, 1, 256, 128), lambda g: (g, 0, 0, 0, l, 2, 0))
+def w_qkv_spec():
+    return pl.BlockSpec((4, 1, 2, 2, 192, 128), lambda g: (0, g, 0, 0, 0, 0))
+
+
+def w_out_spec():
+    return pl.BlockSpec((4, 4, 2, 2, 64, 128), lambda g: (0, 0, 0, 0, 3, 0))
+
+
+def w_up_spec(i):
+    return pl.BlockSpec((4, 1, 2, 2, 256, 128), lambda g: (0, g, 0, 0, i, 0))
+
+
+def w_down_spec(i):
+    return pl.BlockSpec((1, 4, 2, 2, 256, 128), lambda g: (g, 0, 0, 0, i, 0))
 
 
 def rows_by_inputs(w_ref, b):
-    return jnp.concatenate([w_ref[y, 0, a, b, 0] for y in range(4) for a in range(2)], axis=1)
+    return jnp.concatenate([w_ref[y, 0, a, b] for y in range(4) for a in range(2)], axis=1)
 
 
 def down_block(w_ref):
@@ -126,7 +136,7 @@
     for x in range(4):
         for a in range(2):
             for b in range(2):
-                blk = w_ref[0, x, a, b, 0]
+                blk = w_ref[0, x, a, b]
                 rows.append(jnp.concatenate([blk[j * 64 : (j + 1) * 64] for j in range(4)], axis=1))
     return jnp.concatenate(rows, axis=0)
 
@@ -136,7 +146,7 @@
     for x in range(4):
         for a in range(2):
             for b in range(2):
-                rows.append(jnp.concatenate([w_ref[y, x, a, b, 0] for y in range(4)], axis=1))
+                rows.append(jnp.concatenate([w_ref[y, x, a, b] for y in range(4)], axis=1))
     return jnp.concatenate(rows, axis=0)
 
 
@@ -150,12 +160,12 @@
                 o_ref[s, 0, j * 128 + b * 64 : j * 128 + b * 64 + 64, :] = v[j * 64 : (j + 1) * 64]
 
 
-def run_qkv(l, every, seen, bias):
+def run_qkv(w, seen, bias):
     out = call(
         qkv_kernel,
         (4,),
         [
-            (w_qkv_spec(l), every),
+            (w_qkv_spec(), w.qo),
             whole(seen),
             (pl.BlockSpec((1, 2, 192, 128), lambda g: (g, 0, 0, 0)), bias),
         ],
@@ -183,11 +193,11 @@
     split_cores(core_ref, mm(out_block(w_ref), blended, NN), keep_ref, send_ref)
 
 
-def run_out(l, core, every, arrived):
+def run_out(w, core, arrived):
     keep, send, blended = call(
         out_kernel,
         (1,),
-        [scalar(core), (w_out_spec(l), every), whole(arrived)],
+        [scalar(core), (w_out_spec(), w.qo), whole(arrived)],
         [*PAIR, out_whole((512, 256), bf16)],
         flops=2 * 1024 * 512 * 256,
         moved=2 << 20,
@@ -227,14 +237,14 @@
     return pl.BlockSpec((rows, columns), lambda g: (g, 0))
 
 
-def run_ffn(l, core, every, seen, bias):
+def run_ffn(w, core, seen, bias):
     keep, send, act, slope = call(
         ffn_kernel,
         (4,),
         [
             scalar(core),
-            (w_up_spec(l), every),
-            (w_down_spec(l), every),
+            (w_up_spec(w.up_at), w.up),
+            (w_down_spec(w.down_at), w.down),
             whole(seen),
             (pl.BlockSpec((1, 2, 256, 128), lambda g: (g, 0, 0, 0)), bias),
         ],
@@ -250,30 +260,15 @@
     return (keep, send), act, slope
 
 
-def ffn_back_kernel(
-    core_ref, up_ref, down_ref, low_ref, act_ref, slope_ref, x_ref, keep_ref, send_ref, gd_ref, gu_ref, bias_ref, acc
-):
+def ffn_back_kernel(core_ref, up_ref, down_ref, low_ref, slope_ref, keep_ref, send_ref, bias_ref, g_ref, acc):
     g = pl.program_id(0)
     low = low_ref[...]
-    grad_active = mm(down_block(down_ref), low, TN)
-    wide = grad_active * slope_ref[...]
-    gu = wide.astype(bf16)
+    gu = (mm(down_block(down_ref), low, TN) * slope_ref[...]).astype(bf16)
     bias_ref[...] = jnp.sum(gu.astype(f32), axis=1, keepdims=True)
-    gd = mm(low, act_ref[...], NT).astype(bf16)
-    for c in range(16):
-        for j in range(4):
-            gd_ref[0, c, j * 64 : (j + 1) * 64, :] = gd[c * 64 : (c + 1) * 64, j * 128 : (j + 1) * 128]
-    x = x_ref[...]
-    part = None
-    for b in range(2):
-        gub = gu[b * 256 : (b + 1) * 256]
-        gw = mm(gub, x, NT).astype(bf16)
-        for y in range(4):
-            for a in range(2):
-                i = y * 2 + a
-                gu_ref[0, y, a, b] = gw[:, i * 128 : (i + 1) * 128]
-        term = mm(rows_by_inputs(up_ref, b), gub, TN)
-        part = term if part is None else part + term
+    g_ref[0, 0:256] = low_ref[pl.ds(pl.multiple_of(g * 256, 256), 256), :]
+    g_ref[0, 256:768] = gu
+    up = jnp.concatenate([rows_by_inputs(up_ref, b) for b in range(2)], axis=0)
+    part = mm(up, gu, TN)
 
     @pl.when(g == 0)
     def _():
@@ -288,33 +283,80 @@
         split_cores(core_ref, acc[...], keep_ref, send_ref)
 
 
-def run_ffn_back(l, core, every, low, act, slope, seen):
-    keep, send, gd, gu, bias = call(
+def run_ffn_back(w, core, low, slope):
+    keep, send, bias, grads = call(
         ffn_back_kernel,
         (4,),
         [
             scalar(core),
-            (w_up_spec(l), every),
-            (w_down_spec(l), every),
+            (w_up_spec(w.up_at), w.up),
+            (w_down_spec(w.down_at), w.down),
             whole(low),
-            (by_step(512, 256), act),
             (by_step(512, 256), slope),
-            whole(seen),
         ],
         [
             *PAIR,
-            (pl.BlockSpec((1, 16, 256, 128), lambda g: (g, 0, 0, 0)), jax.ShapeDtypeStruct((4, 16, 256, 128), bf16)),
-            (
-                pl.BlockSpec((1, 4, 2, 2, 256, 128), lambda g: (g, 0, 0, 0, 0, 0)),
-                jax.ShapeDtypeStruct((4, 4, 2, 2, 256, 128), bf16),
-            ),
             (by_step(512, 1), jax.ShapeDtypeStruct((2048, 1), f32)),
+            (pl.BlockSpec((1, 768, 256), lambda g: (g, 0, 0)), jax.ShapeDtypeStruct((4, 768, 256), bf16)),
         ],
         [pltpu.VMEM((D, 256), f32)],
-        flops=8 * 2048 * 1024 * 256,
-        moved=22 << 20,
-    )
-    return (keep, send), gd, gu, bias
+        flops=4 * 2048 * 1024 * 256,
+        moved=14 << 20,
+    )
+    return (keep, send), grads, bias
+
+
+def wide(ref, top, rows):
+    return jnp.concatenate([ref[i, top : top + rows] for i in range(4)], axis=1)
+
+
+def ffn_grad_kernel(g_ref, act_ref, seen_ref, o_ref):
+    gd = mm(wide(g_ref, 0, 256), wide(act_ref, 0, 512), NT).astype(bf16)
+    gu = mm(wide(g_ref, 256, 512), wide(seen_ref, 0, 256), NT).astype(bf16)
+    for a in range(2):
+        for b in range(2):
+            z = a * 2 + b
+            o_ref[0, z, 0:256, :] = gu[b * 256 : (b + 1) * 256, a * 128 : (a + 1) * 128]
+            for j in range(4):
+                o_ref[0, z, 256 + j * 64 : 320 + j * 64, :] = gd[z * 64 : (z + 1) * 64, j * 128 : (j + 1) * 128]
+
+
+def inputs_spec(rows, base):
+    return pl.BlockSpec((4, rows, 256), lambda g: (0, base + g, 0))
+
+
+def run_ffn_grad(arrived, inputs):
+    return call(
+        ffn_grad_kernel,
+        (4,),
+        [whole(arrived), (inputs_spec(512, 0), inputs), (inputs_spec(256, 8), inputs)],
+        [(pl.BlockSpec((1, 4, 512, 128), lambda g: (g, 0, 0, 0)), jax.ShapeDtypeStruct((4, 4, 512, 128), bf16))],
+        flops=4 * 2048 * 1024 * 256,
+        moved=14 << 20,
+    )[0]
+
+
+def attend_grad_kernel(g_ref, bl_ref, seen_ref, o_ref):
+    go = mm(wide(g_ref, 0, 256), wide(bl_ref, 0, 128), NT).astype(bf16)
+    gq = mm(wide(g_ref, 256, 384), wide(seen_ref, 0, 256), NT).astype(bf16)
+    for a in range(2):
+        for b in range(2):
+            z = a * 2 + b
+            for j in range(3):
+                top = j * 128 + b * 64
+                o_ref[0, z, j * 64 : (j + 1) * 64, :] = gq[top : top + 64, a * 128 : (a + 1) * 128]
+            o_ref[0, z, 192:256, :] = go[z * 64 : (z + 1) * 64]
+
+
+def run_attend_grad(arrived, inputs):
+    return call(
+        attend_grad_kernel,
+        (4,),
+        [whole(arrived), (inputs_spec(128, 24), inputs), (inputs_spec(256, 14), inputs)],
+        [(pl.BlockSpec((1, 4, 256, 128), lambda g: (g, 0, 0, 0)), jax.ShapeDtypeStruct((4, 4, 256, 128), bf16))],
+        flops=2 * 2048 * 1024 * 256,
+        moved=7 << 20,
+    )[0]
 
 
 def out_back_kernel(w_ref, low_ref, o_ref):
@@ -324,36 +366,28 @@
             o_ref[s * 4 + h] = r[h * 128 : (h + 1) * 128, s * 128 : (s + 1) * 128]
 
 
-def run_out_back(l, every, low):
+def run_out_back(w, low):
     return call(
         out_back_kernel,
         (1,),
-        [(w_out_spec(l), every), whole(low)],
+        [(w_out_spec(), w.qo), whole(low)],
         [out_whole((8, 128, 128), bf16)],
         flops=2 * 1024 * 512 * 256,
         moved=2 << 20,
     )[0]
 
 
-def qkv_back_kernel(core_ref, w_ref, gq_ref, x_ref, low_ref, bl_ref, keep_ref, send_ref, g_ref, bias_ref, acc):
+def qkv_back_kernel(core_ref, w_ref, gq_ref, low_ref, keep_ref, send_ref, g_ref, bias_ref, acc):
     g = pl.program_id(0)
-    x = x_ref[...]
     both = jnp.concatenate([gq_ref[0, 0], gq_ref[1, 0]], axis=1)
+    g_ref[0, 0:256] = low_ref[...]
+    g_ref[0, 256:640] = both
     part = None
     for b in range(2):
         gq = jnp.concatenate([both[j * 128 + b * 64 : j * 128 + b * 64 + 64] for j in range(3)], axis=0)
         bias_ref[0, b] = jnp.sum(gq.astype(f32), axis=1, keepdims=True)
-        gw = mm(gq, x, NT).astype(bf16)
-        for y in range(4):
-            for a in range(2):
-                i = y * 2 + a
-                g_ref[a * 2 + b, y, 0, 0:192, :] = gw[:, i * 128 : (i + 1) * 128]
         term = mm(rows_by_inputs(w_ref, b), gq, TN)
         part = term if part is None else part + term
-    go = mm(low_ref[...], bl_ref[...], NT).astype(bf16)
-    for z in range(4):
-        for y in range(4):
-            g_ref[z, y, 0, 192:256, :] = go[z * 64 : (z + 1) * 64, y * 128 : (y + 1) * 128]
 
     @pl.when(g == 0)
     def _():
@@ -368,31 +402,26 @@
         split_cores(core_ref, acc[...], keep_ref, send_ref)
 
 
-def run_qkv_back(l, core, every, arrived, seen, low, blended):
-    keep, send, gqo, bias = call(
+def run_qkv_back(w, core, arrived, low):
+    keep, send, grads, bias = call(
         qkv_back_kernel,
         (4,),
         [
             scalar(core),
-            (w_qkv_spec(l), every),
+            (w_qkv_spec(), w.qo),
             (pl.BlockSpec((2, 1, 384, 128), lambda g: (0, g, 0, 0)), arrived.reshape(2, 4, 384, 128)),
-            whole(seen),
             (by_step(256, 256), low),
-            whole(blended),
         ],
         [
             *PAIR,
-            (
-                pl.BlockSpec((4, 4, 1, 256, 128), lambda g: (0, 0, g, 0, 0)),
-                jax.ShapeDtypeStruct((4, 4, 4, 256, 128), bf16),
-            ),
+            (pl.BlockSpec((1, 640, 256), lambda g: (g, 0, 0)), jax.ShapeDtypeStruct((4, 640, 256), bf16)),
             (pl.BlockSpec((1, 2, 192, 1), lambda g: (g, 0, 0, 0)), jax.ShapeDtypeStruct((4, 2, 192, 1), f32)),
         ],
         [pltpu.VMEM((D, 256), f32)],
-        flops=6 * 2048 * 1024 * 256,
-        moved=12 << 20,
-    )
-    return (keep, send), gqo, bias
+        flops=2 * 1536 * 1024 * 256,
+        moved=7 << 20,
+    )
+    return (keep, send), grads, bias
 
 
 FACTOR = HEAD ** (-0.5)
@@ -520,7 +549,10 @@
         ],
         axis=1,
     )
-    every = lax.all_gather(pack, CHIPS, axis=0, tiled=False).reshape(4, 4, 2, 2, LAYERS, 768, 128)
+    weights = []
+    for l in range(LAYERS):
+        every = lax.all_gather(pack[l], CHIPS, axis=0, tiled=False).reshape(4, 4, 2, 2, 768, 128)
+        weights.append(Weights(every, every, every, 1, 2))
 
     small = jnp.concatenate(
         [
@@ -546,30 +578,37 @@
     stored = []
     for l in range(LAYERS):
         seen = core_gather(stream.astype(bf16))
-        packed = seq_swap(run_qkv(l, every, seen, b_qkv[l]))
+        packed = seq_swap(run_qkv(weights[l], seen, b_qkv[l]))
         mixed, log = run_attend(packed)
-        pair, blended = run_out(l, here, every, seq_swap(mixed))
+        pair, blended = run_out(weights[l], here, seq_swap(mixed))
         attn_out = core_add(pair) + b_out[l][:, None]
         first, n_attn, i_attn = norm_forward(stream + attn_out, g_attn[l], s_attn[l])
         first_seen = core_gather(first.astype(bf16))
-        pair, active, slope = run_ffn(l, here, every, first_seen, b_up[l])
+        pair, active, slope = run_ffn(weights[l], here, first_seen, b_up[l])
         lower = core_add(pair) + b_down[l][:, None]
         stream, n_ffn, i_ffn = norm_forward(first + lower, g_ffn[l], s_ffn[l])
-        stored.append((seen, packed, log, blended, n_attn, i_attn, first_seen, active, slope, n_ffn, i_ffn))
+        inputs = jnp.concatenate([active, first_seen, blended, seen], axis=0)
+        inputs = lax.all_gather(inputs, X, axis=0, tiled=False)
+        stored.append((inputs, packed, log, n_attn, i_attn, slope, n_ffn, i_ffn))
     result = lax.all_to_all(stream.astype(bf16), COL, 0, 1, tiled=True)
 
-    big = [None] * LAYERS
     minor = [None] * LAYERS
     for l in reversed(range(LAYERS)):
-        (seen, packed, log, blended, n_attn, i_attn, first_seen, active, slope, n_ffn, i_ffn) = stored[l]
+        (inputs, packed, log, n_attn, i_attn, slope, n_ffn, i_ffn) = stored[l]
         grad_sum = norm_backward(back, n_ffn, i_ffn, g_ffn[l])
         p_gain_ffn = jnp.sum(back * n_ffn, axis=1)
         p_shift_ffn = jnp.sum(back, axis=1)
         low = grad_sum.astype(bf16)
         p_down = jnp.sum(low.astype(f32), axis=1)
-        pair, gd, gu, p_up = run_ffn_back(l, here, every, core_gather(low), active, slope, first_seen)
-        gw_down = reduce_both(gd, Y, COL)
-        gw_up = reduce_both(gu.reshape(4, 16, 256, 128), X, ("y",) + Z)
+        pair, send_ud, p_up = run_ffn_back(weights[l], here, core_gather(low), slope)
+        g_ud = lax.all_to_all(send_ud, X, 0, 0, tiled=True)
+        if l == 0:
+            rest = jnp.concatenate(
+                [run_ffn_grad(after(late[0], send_ud), late[2]), run_attend_grad(after(late[1], send_ud), late[2])],
+                axis=2,
+            )
+            rest = lax.psum_scatter(rest.reshape(16, 768, 128), ("y",) + Z, scatter_dimension=0)
+            ud = reduce_stage(run_ffn_grad(g_ud, inputs).reshape(16, 512, 128), ("y",) + Z)
         grad_first = core_add(pair) + grad_sum
         p_gain_attn = jnp.sum(grad_first * n_attn, axis=1)
         p_shift_attn = jnp.sum(grad_first, axis=1)
@@ -577,15 +616,30 @@
         low = grad_total.astype(bf16)
         p_out = jnp.sum(low.astype(f32), axis=1)
         low = core_gather(low)
-        grad_blended = seq_swap(run_out_back(l, every, low))
+        grad_blended = seq_swap(run_out_back(weights[l], low))
         grad_qkv = seq_swap(run_attend_back(packed, grad_blended, log))
-        pair, gqo, p_qkv = run_qkv_back(l, here, every, grad_qkv, seen, low, blended)
-        gw_qo = reduce_both(gqo.reshape(4, 16, 256, 128), Z, ("y",) + X)
+        pair, send_qo, p_qkv = run_qkv_back(weights[l], here, grad_qkv, low)
+        g_qo = lax.all_to_all(send_qo, X, 0, 0, tiled=True)
+        if l == 1:
+            late = (g_ud, g_qo, inputs)
+        else:
+            qo = reduce_stage(run_attend_grad(g_qo, inputs).reshape(16, 256, 128), ("y",) + Z)
         back = core_add(pair) + grad_total
-        swapped = trade(jnp.concatenate([gw_qo[:192], gw_up], axis=0).astype(bf16)).astype(f32)
-        gw_down = gw_down.reshape(4, 64, 128).transpose(1, 0, 2).reshape(64, 512)
-        big[l] = (swapped[:192].reshape(3, 64, 128), gw_qo[192:], swapped[192:], gw_down)
         minor[l] = (p_qkv, p_out, p_gain_attn, p_shift_attn, p_down, p_gain_ffn, p_shift_ffn, p_up)
+    rest = after(rest, send_qo).astype(f32)
+    sums = ((ud[256:], ud[:256], qo), (rest[256:512], rest[:256], rest[512:]))
+    swapped = trade(
+        jnp.stack([jnp.concatenate([q[:192], u], axis=0) for _, u, q in sums]).astype(bf16)
+    ).astype(f32)
+    big = [
+        (
+            swapped[l, :192].reshape(3, 64, 128),
+            sums[l][2][192:],
+            swapped[l, 192:],
+            sums[l][0].reshape(4, 64, 128).transpose(1, 0, 2).reshape(64, 512),
+        )
+        for l in range(LAYERS)
+    ]
     grad_tokens = lax.all_to_all(back.astype(bf16), COL, 0, 1, tiled=True).astype(f32)
 
     mine = (jnp.arange(2) == core).astype(f32)

time: 878 us -> 644 us (0.73)
  blocking collectives: 275 us -> 121 us
  waiting for transfers between devices: 260 us -> 217 us
  starting transfers between devices: 136 us -> 101 us
  other arithmetic: 56.7 us -> 34.1 us
  local copies, waits for them, and re-layouts: 29.2 us -> 40.6 us
  Pallas kernels: 93.9 us -> 103 us
    all_to_all x5 -> x1, blocking collectives: 176 us -> 9.26 us  [reduce_stage(): lax.all_to_all(g, axes, 0, 0, tiled=True).astype(f32)]
    all_to_all x8 -> x2, waiting for transfers between devices: 116 us -> 5.69 us  [reduce_stage(): lax.all_to_all(g, axes, 0, 0, tiled=True).astype(f32)]
    all_to_all x0 -> x5, waiting for transfers between devices: none -> 56.9 us  [the longest x2 33.2 us: on_device(): g_ud = lax.all_to_all(send_ud, X, 0, 0, tiled=True)]
    all_to_all x8 -> x2, starting transfers between devices: 42.5 us -> 9.73 us  [reduce_stage(): lax.all_to_all(g, axes, 0, 0, tiled=True).astype(f32)]
    reduce_sum x13 -> x3, other arithmetic: 29 us -> 0.46 us  [reduce_stage(): jnp.sum(lax.all_to_all(g, axes, 0, 0, tiled=True).astype(f32), axis=0)]
    ppermute x3 -> x2, starting transfers between devices: 34.2 us -> 11 us  [trade(): return lax.ppermute(values, (CORE, 'zh'), [(0, 0), (1, 2), (2, 1), (3, 3)])]
    all_to_all x5 -> x6, blocking collectives: 65.2 us -> 86.8 us  [seq_swap(): return lax.all_to_all(values, SEQ, 0, 0, tiled=True)]
    all_to_all x0 -> x5, starting transfers between devices: none -> 19.6 us  [the longest x2 7.26 us: on_device(): g_ud = lax.all_to_all(send_ud, X, 0, 0, tiled=True)]
  transfers between devices with their start and end apart: 31 -> 32, of which waited for: 23 -> 22; matrix products, arithmetic and copies ran while one was open for 7% -> 7% of each run, Pallas kernels for 2% -> 13%
where the time goes in v3:
time: 644 us; the launch traced here: 633 us
  waiting for transfers between devices  217 us (34%)
  blocking collectives  121 us (19%)
  Pallas kernels  103 us (16%)
  starting transfers between devices  101 us (16%)
  local copies, waits for them, and re-layouts  40.6 us (6%)
  other arithmetic  34.1 us (5%)
  between operations  15.4 us (2%)
    pallas_call x20, Pallas kernels, call(): pl.pallas_call(kernel, grid=grid, in_specs=[spec for spec, _ in ins], out...  103 us
    all_gather x2, waiting for transfers between devices, on_device(): lax.all_gather(pack[l], CHIPS, axis=0, tiled=False)  92.4 us
    all_to_all x6, blocking collectives, seq_swap(): return lax.all_to_all(values, SEQ, 0, 0, tiled=True)  86.8 us
    all_to_all x2, waiting for transfers between devices, on_device(): g_ud = lax.all_to_all(send_ud, X, 0, 0, tiled=True)  33.2 us
    all_gather x8, blocking collectives, core_gather(): return lax.all_gather(values, CORE, axis=1, tiled=True)  25.1 us
    ppermute x8, starting transfers between devices, core_add(): return keep + lax.ppermute(send, CORE, [(0, 1), (1, 0)]).astype(f32)  21.5 us
    all_to_all x2, waiting for transfers between devices, on_device(): g_qo = lax.all_to_all(send_qo, X, 0, 0, tiled=True)  21.4 us
    unnamed x118, local copies, waits for them, and re-layouts  18.1 us
  transfers between devices with their start and end apart: 32, of which 22 were waited for; matrix products, arithmetic and copies ran while one was open for 7% of the time, Pallas kernels for 13%

profile of v3, /device:TPU:1, one launch (start us, length us, event | category | flops | bytes accessed | tf_op | source)
XLA Modules:
  0.0 632.9 jit_solution(8216217201896137011)
XLA Ops:
  8.3 6.9 %collective-permute-start = (bf16[2,448,128]{2,1,0:T(8,128)(2,1)S(1)}, bf16[2,448,128]{2,1,0:T(8,128)(2,1)S(1)}, u32[]{:S(2)}, u32[]{:S(2)}) collective-permute-start(bf16[2,448,128]{2,1,0:T(8,128)(2,1)S(1)} %pad_maximum_fusion.5), channel_id=1, source_target_pairs={{0,0},{2,16},{16,2},{18,18},{1,1},{3,17},{17,3},{19,19},{4,4},{6,2... | collective-permute-start | bytes 688136 | tf_op jit(solution)/shard_map/ppermute | solution.py:47
  22.7 4.6 all-to-all-start.1
  28.2 5.7 all-to-all-done.1
  37.8 7.2 %all-to-all-done = bf16[64,16,128]{2,0,1:T(8,128)(2,1)S(1)} async-done(((bf16[64,16,128]{2,0,1:T(8,128)(2,1)}), bf16[64,16,128]{2,0,1:T(8,128)(2,1)S(1)}, u32[]{:S(2)}, u32[]{:S(2)}) %all-to-all-start) | async-done | bytes 262176 | tf_op jit(solution)/shard_map/all_to_all | solution.py:576
  45.0 6.9 %all_gather.43.x_ref = bf16[1024,256]{1,0:T(8,128)(2,1)S(1)} all-gather(bf16[1024,128]{1,0:T(8,128)(2,1)S(1)} %bitcast.165), channel_id=1, replica_groups=mesh['y'=4,'k'=2,'xh'=2,'xl'=2,'zh'=2,'zl'=2] {'k'}, dimensions={1}, use_global_device_ids=true | all-gather | bytes 786432 | tf_op jit(solution)/shard_map/all_gather | solution.py:38
  51.9 61.6 %all-gather.7.cloned.1.call-done = bf16[64,768,128]{2,1,0:T(8,128)(2,1)} async-done(((bf16[1,768,128]{2,1,0:T(8,128)(2,1)}), bf16[64,768,128]{2,1,0:T(8,128)(2,1)}) %all-gather.7.cloned.1.call-update) | async-done | bytes 12582928 | tf_op jit(solution)/shard_map/all_gather | solution.py:554
  117.4 16.7 %all_to_all.148.p_ref = bf16[8,384,128]{2,1,0:T(8,128)(2,1)S(1)} all-to-all(bf16[8,384,128]{2,1,0:T(8,128)(2,1)S(1)} %bitcast.136), channel_id=1, replica_groups=mesh['y'=4,'k'=2,'xh'=2,'xl'=2,'zh'=2,'zl'=2] {'xl','zh','zl'}, dimensions={0} | all-to-all | bytes 1572864 | tf_op jit(solution)/shard_map/all_to_all | solution.py:503
  134.0 7.2 %shard_map.246 = (bf16[8,128,128]{2,1,0:T(8,128)(2,1)}, f32[2,1024]{1,0:T(2,128)S(1)}) custom-call(bf16[8,384,128]{2,1,0:T(8,128)(2,1)S(1)} %all_to_all.148.p_ref), custom_call_target="tpu_custom_call" | custom-call | flops 1073741824 | bytes 1048576 | tf_op jit(solution)/shard_map/pallas_call | solution.py:78
  146.1 5.5 all-to-all-done.3.b_ref
  154.0 5.1 collective-permute-start.1
  163.5 7.7 %shard_map.248 = (f32[1024,128]{1,0:T(8,128)S(1)}, bf16[1024,128]{1,0:T(8,128)(2,1)S(1)}, bf16[2048,256]{1,0:T(8,128)(2,1)S(1)}, f32[2048,256]{1,0:T(8,128)}) custom-call(s32[1]{0:T(128)} %bitcast.2.core_ref, bf16[4,4,2,2,768,128]{5,4,3,2,1,0:T(8,128)(2,1)} %bitcast.142, bf16[4,4,2,2,768,128]{5,4,3,2,1,0:T(8,128)(2,1)} %bitcast.143, ...), custom_call_target="tpu_custom_call" | custom-call | flops 2147483648 | bytes 13631488 | tf_op jit(solution)/shard_map/pallas_call | solution.py:78
  178.2 30.7 %all-gather.9.cloned.1.call-done = bf16[64,768,128]{2,1,0:T(8,128)(2,1)} async-done(((bf16[1,768,128]{2,1,0:T(8,128)(2,1)}), bf16[64,768,128]{2,1,0:T(8,128)(2,1)}) %all-gather.9.cloned.1.call-update) | async-done | bytes 12582928 | tf_op jit(solution)/shard_map/all_gather | solution.py:554
  212.7 16.1 %all_to_all.149.p_ref = bf16[8,384,128]{2,1,0:T(8,128)(2,1)S(1)} all-to-all(bf16[8,384,128]{2,1,0:T(8,128)(2,1)S(1)} %bitcast.137), channel_id=1, replica_groups=mesh['y'=4,'k'=2,'xh'=2,'xl'=2,'zh'=2,'zl'=2] {'xl','zh','zl'}, dimensions={0} | all-to-all | bytes 1572864 | tf_op jit(solution)/shard_map/all_to_all | solution.py:503
  228.8 6.5 %shard_map.250 = (bf16[8,128,128]{2,1,0:T(8,128)(2,1)S(1)}, f32[2,1024]{1,0:T(2,128)S(1)}) custom-call(bf16[8,384,128]{2,1,0:T(8,128)(2,1)S(1)} %all_to_all.149.p_ref), custom_call_target="tpu_custom_call" | custom-call | flops 1073741824 | bytes 1048576 | tf_op jit(solution)/shard_map/pallas_call | solution.py:78
  235.4 8.8 %all_to_all.150.b_ref = bf16[8,128,128]{2,1,0:T(8,128)(2,1)S(1)} all-to-all(bf16[8,128,128]{2,1,0:T(8,128)(2,1)S(1)} %get-tuple-element.56), channel_id=1, replica_groups=mesh['y'=4,'k'=2,'xh'=2,'xl'=2,'zh'=2,'zl'=2] {'xl','zh','zl'}, dimensions={0} | all-to-all | bytes 524288 | tf_op jit(solution)/shard_map/all_to_all | solution.py:503
  257.7 7.8 %shard_map.252 = (f32[1024,128]{1,0:T(8,128)S(1)}, bf16[1024,128]{1,0:T(8,128)(2,1)S(1)}, bf16[2048,256]{1,0:T(8,128)(2,1)S(1)}, f32[2048,256]{1,0:T(8,128)}) custom-call(s32[1]{0:T(128)} %bitcast.2.core_ref, bf16[4,4,2,2,768,128]{5,4,3,2,1,0:T(8,128)(2,1)} %bitcast.150, bf16[4,4,2,2,768,128]{5,4,3,2,1,0:T(8,128)(2,1)} %bitcast.151, ...), custom_call_target="tpu_custom_call" | custom-call | flops 2147483648 | bytes 13631488 | tf_op jit(solution)/shard_map/pallas_call | solution.py:78
  272.8 4.2 all-to-all-start.7
  277.9 7.1 %all-to-all-done.7 = bf16[64,16,128]{2,0,1:T(8,128)(2,1)S(1)} async-done(((bf16[64,16,128]{2,0,1:T(8,128)(2,1)}), bf16[64,16,128]{2,0,1:T(8,128)(2,1)S(1)}, u32[]{:S(2)}, u32[]{:S(2)}) %all-to-all-start.7) | async-done | bytes 262176 | tf_op jit(solution)/shard_map/all_to_all | solution.py:577
  286.9 5.1 all_gather.48.low_ref
  292.0 8.8 %shard_map.253 = (f32[1024,128]{1,0:T(8,128)S(1)}, bf16[1024,128]{1,0:T(8,128)(2,1)S(1)}, f32[2048,1]{1,0:T(8,128)S(1)}, bf16[4,768,256]{2,1,0:T(8,128)(2,1)}) custom-call(s32[1]{0:T(128)} %bitcast.2.core_ref, bf16[4,4,2,2,768,128]{5,4,3,2,1,0:T(8,128)(2,1)} %bitcast.152, bf16[4,4,2,2,768,128]{5,4,3,2,1,0:T(8,128)(2,1)} %bitcast.153, ...), custom_call_target="tpu_custom_call" | custom-call | flops 2147483648 | bytes 14680064 | tf_op jit(solution)/shard_map/pallas_call | solution.py:78
  310.4 11.6 %all_to_all.151.b_ref = bf16[8,128,128]{2,1,0:T(8,128)(2,1)S(1)} all-to-all(bf16[8,128,128]{2,1,0:T(8,128)(2,1)S(1)} %shard_map.254), channel_id=1, replica_groups=mesh['y'=4,'k'=2,'xh'=2,'xl'=2,'zh'=2,'zl'=2] {'xl','zh','zl'}, dimensions={0} | all-to-all | bytes 524288 | tf_op jit(solution)/shard_map/all_to_all | solution.py:503
  322.0 6.8 %shard_map.255 = bf16[8,384,128]{2,1,0:T(8,128)(2,1)S(1)} custom-call(bf16[8,384,128]{2,1,0:T(8,128)(2,1)S(1)} %all_to_all.149.p_ref, bf16[8,128,128]{2,1,0:T(8,128)(2,1)S(1)} %all_to_all.151.b_ref, f32[2,1024]{1,0:T(2,128)S(1)} %get-tuple-element.64.log_ref), custom_call_target="tpu_custom_call" | custom-call | flops 2684354560 | bytes 2097152 | tf_op jit(solution)/shard_map/pallas_call | solution.py:78
  328.8 22.6 %all_to_all.152 = bf16[8,384,128]{2,1,0:T(8,128)(2,1)S(1)} all-to-all(bf16[8,384,128]{2,1,0:T(8,128)(2,1)S(1)} %shard_map.255), channel_id=1, replica_groups=mesh['y'=4,'k'=2,'xh'=2,'xl'=2,'zh'=2,'zl'=2] {'xl','zh','zl'}, dimensions={0} | all-to-all | bytes 1572864 | tf_op jit(solution)/shard_map/all_to_all | solution.py:503
  351.4 5.1 shard_map.256
  364.3 7.8 %shard_map.257 = (f32[1024,128]{1,0:T(8,128)S(1)}, bf16[1024,128]{1,0:T(8,128)(2,1)S(1)}, f32[2048,1]{1,0:T(8,128)S(1)}, bf16[4,768,256]{2,1,0:T(8,128)(2,1)S(1)}) custom-call(s32[1]{0:T(128)} %bitcast.2.core_ref, bf16[4,4,2,2,768,128]{5,4,3,2,1,0:T(8,128)(2,1)} %bitcast.144, bf16[4,4,2,2,768,128]{5,4,3,2,1,0:T(8,128)(2,1)} %bitcast.145, ...), custom_call_target="tpu_custom_call" | custom-call | flops 2147483648 | bytes 14680064 | tf_op jit(solution)/shard_map/pallas_call | solution.py:78
  385.6 24.1 %all-to-all-done.17.g_ref = bf16[4,768,256]{2,1,0:T(8,128)(2,1)S(1)} async-done(((bf16[4,768,256]{2,1,0:T(8,128)(2,1)}), bf16[4,768,256]{2,1,0:T(8,128)(2,1)S(1)}, u32[]{:S(2)}, u32[]{:S(2)}) %all-to-all-start.17) | async-done | bytes 1572896 | tf_op jit(solution)/shard_map/all_to_all | solution.py:604
  409.6 11.0 %all_to_all.153.b_ref = bf16[8,128,128]{2,1,0:T(8,128)(2,1)} all-to-all(bf16[8,128,128]{2,1,0:T(8,128)(2,1)S(1)} %shard_map.258), channel_id=1, replica_groups=mesh['y'=4,'k'=2,'xh'=2,'xl'=2,'zh'=2,'zl'=2] {'xl','zh','zl'}, dimensions={0} | all-to-all | bytes 524288 | tf_op jit(solution)/shard_map/all_to_all | solution.py:503
  426.3 6.8 %shard_map.259 = bf16[8,384,128]{2,1,0:T(8,128)(2,1)S(1)} custom-call(bf16[8,384,128]{2,1,0:T(8,128)(2,1)S(1)} %copy-done.12, bf16[8,128,128]{2,1,0:T(8,128)(2,1)S(1)} %copy-done.24, f32[2,1024]{1,0:T(2,128)S(1)} %get-tuple-element.70.log_ref), custom_call_target="tpu_custom_call" | custom-call | flops 2684354560 | bytes 2097152 | tf_op jit(solution)/shard_map/pallas_call | solution.py:78
  433.9 21.2 %all-to-all-done.18.g_ref = bf16[4,640,256]{2,1,0:T(8,128)(2,1)S(1)} async-done(((bf16[4,640,256]{2,1,0:T(8,128)(2,1)}), bf16[4,640,256]{2,1,0:T(8,128)(2,1)S(1)}, u32[]{:S(2)}, u32[]{:S(2)}) %all-to-all-start.18) | async-done | bytes 1310752 | tf_op jit(solution)/shard_map/all_to_all | solution.py:622
  455.1 4.5 all-to-all-start.6
  459.7 4.0 shard_map.264
  464.8 5.2 shard_map.263
  469.9 5.0 all-to-all-start.11
  486.4 6.6 %all-to-all-done.11 = bf16[8,384,128]{2,1,0:T(8,128)(2,1)S(1)} async-done(((bf16[8,384,128]{2,1,0:T(8,128)(2,1)}), bf16[8,384,128]{2,1,0:T(8,128)(2,1)S(1)}, u32[]{:S(2)}, u32[]{:S(2)}) %all-to-all-start.11) | async-done | bytes 786464 | tf_op jit(solution)/shard_map/all_to_all | solution.py:503
  493.0 3.7 all-to-all-start.15
  497.7 5.0 shard_map.260
  506.5 9.1 %all-to-all-done.15.g_ref = bf16[4,768,256]{2,1,0:T(8,128)(2,1)S(1)} async-done(((bf16[4,768,256]{2,1,0:T(8,128)(2,1)}), bf16[4,768,256]{2,1,0:T(8,128)(2,1)S(1)}, u32[]{:S(2)}, u32[]{:S(2)}) %all-to-all-start.15) | async-done | bytes 1572896 | tf_op jit(solution)/shard_map/all_to_all | solution.py:604
  515.6 9.3 %all_to_all.154 = f32[16,12,128]{2,1,0:T(8,128)S(1)} all-to-all(f32[16,12,128]{2,1,0:T(8,128)S(1)} %reshape_reshape.3), channel_id=1, replica_groups=mesh['y'=4,'k'=2,'xh'=2,'xl'=2,'zh'=2,'zl'=2] {'xh','xl','zh','zl'}, dimensions={0} | all-to-all | bytes 196608 | tf_op jit(solution)/shard_map/all_to_all | solution.py:55
  528.4 7.4 %collective-permute-start.8 = (bf16[1024,128]{1,0:T(8,128)(2,1)S(1)}, bf16[1024,128]{1,0:T(8,128)(2,1)S(1)}, u32[]{:S(2)}, u32[]{:S(2)}) collective-permute-start(bf16[1024,128]{1,0:T(8,128)(2,1)S(1)} %copy-done.28), channel_id=1, source_target_pairs={{0,16},{16,0},{1,17},{17,1},{2,18},{18,2},{3,19},{19,3},{4,20},{20... | collective-permute-start | bytes 786440 | tf_op jit(solution)/shard_map/ppermute | solution.py:43
  539.5 5.2 all-to-all-start.12
  544.8 3.9 shard_map.261
  552.1 6.0 all-to-all-start.14
  558.1 6.1 shard_map.262
  564.2 5.7 all-to-all-done.14
  569.9 3.7 all-to-all-start.16
  578.0 16.3 %collective-permute-done.12 = f32[12,128]{1,0:T(8,128)S(1)} collective-permute-done((f32[12,128]{1,0:T(8,128)S(1)}, f32[12,128]{1,0:T(8,128)S(1)}, u32[]{:S(2)}, u32[]{:S(2)}) %collective-permute-start.12) | collective-permute-done | bytes 6176 | tf_op jit(solution)/shard_map/ppermute | solution.py:73
  594.3 9.4 %collective-permute-start.13 = (f32[12,128]{1,0:T(8,128)S(1)}, f32[12,128]{1,0:T(8,128)S(1)}, u32[]{:S(2)}, u32[]{:S(2)}) collective-permute-start(f32[12,128]{1,0:T(8,128)S(1)} %add_add_fusion.7), channel_id=1, source_target_pairs={{0,16},{16,0},{1,17},{17,1},{2,18},{18,2},{3,19},{19,3},{4,20},{20... | collective-permute-start | bytes 18440 | tf_op jit(solution)/shard_map/ppermute | solution.py:655
  615.6 4.1 collective-permute-start.9
  (344 shorter events, 149.9 us)
Async XLA Ops:
  7.2 20.1 %copy-start = (bf16[64,2048]{1,0:T(8,128)(2,1)S(1)}, bf16[64,2048]{1,0:T(8,128)(2,1)}, u32[]{:S(2)}) copy-start(bf16[64,2048]{1,0:T(8,128)(2,1)} %param.14) | copy-start | bytes 786436
  7.2 14.1 %copy-start.45 = (f32[2,2,64]{2,1,0:T(2,128)S(1)}, f32[2,2,64]{2,1,0:T(2,128)}, u32[]{:S(2)}) copy-start(f32[2,2,64]{2,1,0:T(2,128)} %param.16) | copy-start | bytes 3076
  7.2 14.2 %copy-start.47 = (f32[2,64]{1,0:T(2,128)S(1)}, f32[2,64]{1,0:T(2,128)}, u32[]{:S(2)}) copy-start(f32[2,64]{1,0:T(2,128)} %param.18) | copy-start | bytes 1540
  7.2 14.3 %copy-start.48 = (f32[2,64]{1,0:T(2,128)S(1)}, f32[2,64]{1,0:T(2,128)}, u32[]{:S(2)}) copy-start(f32[2,64]{1,0:T(2,128)} %param.19) | copy-start | bytes 1540
  7.2 14.3 %copy-start.49 = (f32[2,64]{1,0:T(2,128)S(1)}, f32[2,64]{1,0:T(2,128)}, u32[]{:S(2)}) copy-start(f32[2,64]{1,0:T(2,128)} %param.20) | copy-start | bytes 1540
  7.2 14.4 %copy-start.50 = (f32[2,64]{1,0:T(2,128)S(1)}, f32[2,64]{1,0:T(2,128)}, u32[]{:S(2)}) copy-start(f32[2,64]{1,0:T(2,128)} %param.24) | copy-start | bytes 1540
  7.3 14.5 %copy-start.51 = (f32[2,64]{1,0:T(2,128)S(1)}, f32[2,64]{1,0:T(2,128)}, u32[]{:S(2)}) copy-start(f32[2,64]{1,0:T(2,128)} %param.25) | copy-start | bytes 1540
  7.3 14.6 %copy-start.52 = (f32[2,64]{1,0:T(2,128)S(1)}, f32[2,64]{1,0:T(2,128)}, u32[]{:S(2)}) copy-start(f32[2,64]{1,0:T(2,128)} %param.26) | copy-start | bytes 1540
  7.3 14.6 %copy-start.46 = (f32[2,256]{1,0:T(2,128)S(1)}, f32[2,256]{1,0:T(2,128)}, u32[]{:S(2)}) copy-start(f32[2,256]{1,0:T(2,128)} %param.22) | copy-start | bytes 6148
  7.3 106.3 %all-gather.7.cloned.1.call-start = ((), (), s32[]{:S(2)}) async-start(), calls=%async_computation.21 | async-start | bytes 12779520 | tf_op jit(solution)/shard_map/all_gather | solution.py:554
  8.3 10.6 %collective-permute-start = (bf16[2,448,128]{2,1,0:T(8,128)(2,1)S(1)}, bf16[2,448,128]{2,1,0:T(8,128)(2,1)S(1)}, u32[]{:S(2)}, u32[]{:S(2)}) collective-permute-start(bf16[2,448,128]{2,1,0:T(8,128)(2,1)S(1)} %pad_maximum_fusion.5), channel_id=1, source_target_pairs={{0,0},{2,16},{16,2},{18,18},{1,1},{3,17},{17,3},{19,19},{4,4},{6,2... | collective-permute-start | bytes 688136 | tf_op jit(solution)/shard_map/ppermute | solution.py:47
  20.6 188.4 %all-gather.9.cloned.1.call-start = ((), (), s32[]{:S(2)}) async-start(), calls=%async_computation.22 | async-start | bytes 12779520 | tf_op jit(solution)/shard_map/all_gather | solution.py:554
  22.7 11.2 %all-to-all-start.1 = ((f32[16,1,1536]{2,1,0:T(1,128)}), f32[16,1,1536]{2,1,0:T(1,128)S(1)}, u32[]{:S(2)}, u32[]{:S(2)}) async-start(f32[16,1,1536]{2,1,0:T(1,128)} %broadcast_in_dim.18), calls=%async_computation.1 | async-start | bytes 196608 | tf_op jit(solution)/shard_map/all_to_all | solution.py:563
  33.9 11.1 %all-to-all-start = ((bf16[64,16,128]{2,0,1:T(8,128)(2,1)}), bf16[64,16,128]{2,0,1:T(8,128)(2,1)S(1)}, u32[]{:S(2)}, u32[]{:S(2)}) async-start(bf16[64,16,128]{2,0,1:T(8,128)(2,1)} %copy_bitcast_fusion.3), calls=%async_computation | async-start | bytes 524288 | tf_op jit(solution)/shard_map/all_to_all | solution.py:576
  142.2 9.5 %all-to-all-start.3 = ((bf16[8,128,128]{2,1,0:T(8,128)(2,1)}), bf16[8,128,128]{2,1,0:T(8,128)(2,1)S(1)}, u32[]{:S(2)}, u32[]{:S(2)}) async-start(bf16[8,128,128]{2,1,0:T(8,128)(2,1)} %get-tuple-element.51), calls=%async_computation.3 | async-start | bytes 524288 | tf_op jit(solution)/shard_map/all_to_all | solution.py:503
  145.6 314.1 %all-gather.13.cloned.1.call-start = ((), (), s32[]{:S(2)}) async-start(), calls=%async_computation.24 | async-start | bytes 11796480 | tf_op jit(solution)/shard_map/all_gather | solution.py:591
  154.0 6.3 collective-permute-start.1
  171.3 2.1 collective-permute-start.2
  248.1 4.8 collective-permute-start.3
  268.6 276.2 %all-gather.11.cloned.1.call-start = ((), (), s32[]{:S(2)}) async-start(), calls=%async_computation.23 | async-start | bytes 11796480 | tf_op jit(solution)/shard_map/all_gather | solution.py:591
  271.1 14.3 %copy-start.18 = (f32[1024,128]{1,0:T(8,128)S(1)}, f32[1024,128]{1,0:T(8,128)}, u32[]{:S(2)}) copy-start(f32[1024,128]{1,0:T(8,128)} %copy-done.17) | copy-start | bytes 1572868
  271.1 14.3 %copy-start.34 = (f32[1024,128]{1,0:T(8,128)S(1)}, f32[1024,128]{1,0:T(8,128)}, u32[]{:S(2)}) copy-start(f32[1024,128]{1,0:T(8,128)} %copy-done.33) | copy-start | bytes 1572868
  272.8 12.2 %all-to-all-start.7 = ((bf16[64,16,128]{2,0,1:T(8,128)(2,1)}), bf16[64,16,128]{2,0,1:T(8,128)(2,1)S(1)}, u32[]{:S(2)}, u32[]{:S(2)}) async-start(bf16[64,16,128]{2,0,1:T(8,128)(2,1)} %copy_bitcast_fusion.2), calls=%async_computation.7 | async-start | bytes 524288 | tf_op jit(solution)/shard_map/all_to_all | solution.py:577
  277.1 8.3 %collective-permute-start.4 = (bf16[1024,128]{1,0:T(8,128)(2,1)S(1)}, bf16[1024,128]{1,0:T(8,128)(2,1)S(1)}, u32[]{:S(2)}, u32[]{:S(2)}) collective-permute-start(bf16[1024,128]{1,0:T(8,128)(2,1)S(1)} %copy-done.26), channel_id=1, source_target_pairs={{0,16},{16,0},{1,17},{17,1},{2,18},{18,2},{3,19},{19,3},{4,20},{20... | collective-permute-start | bytes 786440 | tf_op jit(solution)/shard_map/ppermute | solution.py:43
  301.8 1.5 collective-permute-start.5
  356.5 4.5 collective-permute-start.6
  374.2 3.9 collective-permute-start.7
  374.6 35.1 %all-to-all-start.17 = ((bf16[4,768,256]{2,1,0:T(8,128)(2,1)}), bf16[4,768,256]{2,1,0:T(8,128)(2,1)S(1)}, u32[]{:S(2)}, u32[]{:S(2)}) async-start(bf16[4,768,256]{2,1,0:T(8,128)(2,1)} %get-tuple-element.77), calls=%async_computation.17 | async-start | bytes 3145728 | tf_op jit(solution)/shard_map/all_to_all | solution.py:604
  409.6 23.4 %copy-start.2 = (bf16[4,768,256]{2,1,0:T(8,128)(2,1)}, bf16[4,768,256]{2,1,0:T(8,128)(2,1)S(1)}, u32[]{:S(2)}) copy-start(bf16[4,768,256]{2,1,0:T(8,128)(2,1)S(1)} %all-to-all-done.17.g_ref) | copy-start | bytes 4718596
  420.6 34.5 %all-to-all-start.18 = ((bf16[4,640,256]{2,1,0:T(8,128)(2,1)}), bf16[4,640,256]{2,1,0:T(8,128)(2,1)S(1)}, u32[]{:S(2)}, u32[]{:S(2)}) async-start(bf16[4,640,256]{2,1,0:T(8,128)(2,1)} %get-tuple-element.81), calls=%async_computation.18 | async-start | bytes 2621440 | tf_op jit(solution)/shard_map/all_to_all | solution.py:622
  455.1 14.8 %all-to-all-start.6 = ((bf16[16,64,128]{2,1,0:T(8,128)(2,1)}), bf16[16,64,128]{2,1,0:T(8,128)(2,1)}, u32[]{:S(2)}, u32[]{:S(2)}) async-start(bf16[16,64,128]{2,1,0:T(8,128)(2,1)} %bitcast.166), calls=%async_computation.6 | async-start | bytes 524288 | tf_op jit(solution)/shard_map/all_to_all | solution.py:593
  469.9 23.0 %all-to-all-start.11 = ((bf16[8,384,128]{2,1,0:T(8,128)(2,1)}), bf16[8,384,128]{2,1,0:T(8,128)(2,1)S(1)}, u32[]{:S(2)}, u32[]{:S(2)}) async-start(bf16[8,384,128]{2,1,0:T(8,128)(2,1)} %copy-done.13), calls=%async_computation.11 | async-start | bytes 1572864 | tf_op jit(solution)/shard_map/all_to_all | solution.py:503
  475.0 137.2 %reduce-scatter.4.cloned.1.call-start = ((), (), s32[]{:S(2)}) async-start(), calls=%async_computation.25 | async-start | bytes 3342336
  493.0 22.6 %all-to-all-start.15 = ((bf16[4,768,256]{2,1,0:T(8,128)(2,1)}), bf16[4,768,256]{2,1,0:T(8,128)(2,1)S(1)}, u32[]{:S(2)}, u32[]{:S(2)}) async-start(bf16[4,768,256]{2,1,0:T(8,128)(2,1)} %copy-done.6), calls=%async_computation.15 | async-start | bytes 3145728 | tf_op jit(solution)/shard_map/all_to_all | solution.py:604
  504.3 20.5 %copy-start.16 = (f32[1024,128]{1,0:T(8,128)}, f32[1024,128]{1,0:T(8,128)S(1)}, u32[]{:S(2)}) copy-start(f32[1024,128]{1,0:T(8,128)S(1)} %get-tuple-element.71) | copy-start | bytes 1572868
  504.3 32.6 %copy-start.41 = (f32[128]{0:T(128)S(1)}, f32[128]{0:T(128)}, u32[]{:S(2)}) copy-start(f32[128]{0:T(128)} %copy-done.39) | copy-start | bytes 1540
  504.3 24.1 %copy-start.28 = (bf16[1024,128]{1,0:T(8,128)(2,1)S(1)}, bf16[1024,128]{1,0:T(8,128)(2,1)}, u32[]{:S(2)}) copy-start(bf16[1024,128]{1,0:T(8,128)(2,1)} %copy-done.27) | copy-start | bytes 786436
  524.8 14.7 %all-to-all-start.13 = ((bf16[4,640,256]{2,1,0:T(8,128)(2,1)}), bf16[4,640,256]{2,1,0:T(8,128)(2,1)S(1)}, u32[]{:S(2)}, u32[]{:S(2)}) async-start(bf16[4,640,256]{2,1,0:T(8,128)(2,1)} %get-tuple-element.73), calls=%async_computation.13 | async-start | bytes 2621440 | tf_op jit(solution)/shard_map/all_to_all | solution.py:622
  528.4 8.5 %collective-permute-start.8 = (bf16[1024,128]{1,0:T(8,128)(2,1)S(1)}, bf16[1024,128]{1,0:T(8,128)(2,1)S(1)}, u32[]{:S(2)}, u32[]{:S(2)}) collective-permute-start(bf16[1024,128]{1,0:T(8,128)(2,1)S(1)} %copy-done.28), channel_id=1, source_target_pairs={{0,16},{16,0},{1,17},{17,1},{2,18},{18,2},{3,19},{19,3},{4,20},{20... | collective-permute-start | bytes 786440 | tf_op jit(solution)/shard_map/ppermute | solution.py:43
  539.5 12.6 %all-to-all-start.12 = ((bf16[16,64,128]{2,1,0:T(8,128)(2,1)}), bf16[16,64,128]{2,1,0:T(8,128)(2,1)S(1)}, u32[]{:S(2)}, u32[]{:S(2)}) async-start(bf16[16,64,128]{2,1,0:T(8,128)(2,1)} %bitcast.25), calls=%async_computation.12 | async-start | bytes 524288 | tf_op jit(solution)/shard_map/all_to_all | solution.py:643
  552.1 17.8 %all-to-all-start.14 = ((bf16[16,256,128]{2,1,0:T(8,128)(2,1)}), bf16[16,256,128]{2,1,0:T(8,128)(2,1)S(1)}, u32[]{:S(2)}, u32[]{:S(2)}) async-start(bf16[16,256,128]{2,1,0:T(8,128)(2,1)} %bitcast.135), calls=%async_computation.14 | async-start | bytes 2097152 | tf_op jit(solution)/shard_map/all_to_all | solution.py:55
  569.9 41.7 %all-to-all-start.16 = ((bf16[16,512,128]{2,1,0:T(8,128)(2,1)}), bf16[16,512,128]{2,1,0:T(8,128)(2,1)S(1)}, u32[]{:S(2)}, u32[]{:S(2)}) async-start(bf16[16,512,128]{2,1,0:T(8,128)(2,1)} %bitcast.29), calls=%async_computation.16 | async-start | bytes 4194304 | tf_op jit(solution)/shard_map/all_to_all | solution.py:55
  573.7 20.6 %collective-permute-start.12 = (f32[12,128]{1,0:T(8,128)S(1)}, f32[12,128]{1,0:T(8,128)S(1)}, u32[]{:S(2)}, u32[]{:S(2)}) collective-permute-start(f32[12,128]{1,0:T(8,128)S(1)} %reduce_sum.309), channel_id=1, source_target_pairs={{0,64},{32,96},{64,0},{96,32},{1,65},{33,97},{65,1},{97,33},{2,66}... | collective-permute-start | bytes 18440 | tf_op jit(solution)/shard_map/ppermute | solution.py:73
  576.5 17.8 %collective-permute-start.11 = (f32[12,128]{1,0:T(8,128)S(1)}, f32[12,128]{1,0:T(8,128)S(1)}, u32[]{:S(2)}, u32[]{:S(2)}) collective-permute-start(f32[12,128]{1,0:T(8,128)S(1)} %reduce_sum.309), channel_id=1, source_target_pairs={{0,96},{32,0},{64,32},{96,64},{1,97},{33,1},{65,33},{97,65},{2,98}... | collective-permute-start | bytes 18440 | tf_op jit(solution)/shard_map/ppermute | solution.py:73
  577.4 16.9 %collective-permute-start.10 = (f32[12,128]{1,0:T(8,128)S(1)}, f32[12,128]{1,0:T(8,128)S(1)}, u32[]{:S(2)}, u32[]{:S(2)}) collective-permute-start(f32[12,128]{1,0:T(8,128)S(1)} %reduce_sum.309), channel_id=1, source_target_pairs={{0,32},{32,64},{64,96},{96,0},{1,33},{33,65},{65,97},{97,1},{2,34}... | collective-permute-start | bytes 18440 | tf_op jit(solution)/shard_map/ppermute | solution.py:73
  594.3 11.1 %collective-permute-start.13 = (f32[12,128]{1,0:T(8,128)S(1)}, f32[12,128]{1,0:T(8,128)S(1)}, u32[]{:S(2)}, u32[]{:S(2)}) collective-permute-start(f32[12,128]{1,0:T(8,128)S(1)} %add_add_fusion.7), channel_id=1, source_target_pairs={{0,16},{16,0},{1,17},{17,1},{2,18},{18,2},{3,19},{19,3},{4,20},{20... | collective-permute-start | bytes 18440 | tf_op jit(solution)/shard_map/ppermute | solution.py:655
  611.9 14.0 %copy-start.1 = (bf16[64,2048]{1,0:T(8,128)(2,1)S(1)}, bf16[64,2048]{1,0:T(8,128)(2,1)}, u32[]{:S(2)}) copy-start(bf16[64,2048]{1,0:T(8,128)(2,1)} %param.14) | copy-start | bytes 786436
  615.6 8.8 %collective-permute-start.9 = (bf16[2,448,128]{2,1,0:T(8,128)(2,1)S(1)}, bf16[2,448,128]{2,1,0:T(8,128)(2,1)S(1)}, u32[]{:S(2)}, u32[]{:S(2)}) collective-permute-start(bf16[2,448,128]{2,1,0:T(8,128)(2,1)S(1)} %pad_maximum_fusion.6), channel_id=1, source_target_pairs={{0,0},{2,16},{16,2},{18,18},{1,1},{3,17},{17,3},{19,19},{4,4},{6,2... | collective-permute-start | bytes 688136 | tf_op jit(solution)/shard_map/ppermute | solution.py:47
  (37 other events, 117.4 us)
Sparse Core Ops, SparseCore 0:
  20.7 92.8 all-gather.6
  116.9 91.9 all-gather.8
  268.7 101.1 all-gather.12
  371.5 131.7 all-gather.10
  506.4 82.0 reduce-scatter.3

commit v4 on v3

--- a/solution.py
+++ b/solution.py
@@ -55,6 +55,22 @@
     return jnp.sum(lax.all_to_all(g, axes, 0, 0, tiled=True).astype(f32), axis=0)
 
 
+SHIFTS = (0, 1, 3, 2)
+
+
+def along(values, axes, shift):
+    return lax.ppermute(values, axes, [(i, (i + shift) % 4) for i in range(4)])
+
+
+def exchange(parts, axes):
+    me = lax.axis_index(axes)
+    return [pick(parts, me, 0)] + [along(pick(parts, (me + i) % 4, 0), axes, i) for i in SHIFTS[1:]]
+
+
+def everyone(values, axes):
+    return [values] + [along(values, axes, i) for i in SHIFTS[1:]]
+
+
 def after(values, *others):
     return lax.optimization_barrier((values, *others))[0]
 
@@ -63,6 +79,7 @@
     qo: jax.Array
     up: jax.Array
     down: jax.Array
+    qo_at: int
     up_at: int
     down_at: int
 
@@ -111,12 +128,12 @@
 PAIR = (out_whole((D, 128), f32), out_whole((D, 128), bf16))
 
 
-def w_qkv_spec():
-    return pl.BlockSpec((4, 1, 2, 2, 192, 128), lambda g: (0, g, 0, 0, 0, 0))
-
-
-def w_out_spec():
-    return pl.BlockSpec((4, 4, 2, 2, 64, 128), lambda g: (0, 0, 0, 0, 3, 0))
+def w_qkv_spec(i):
+    return pl.BlockSpec((4, 1, 2, 2, 256, 128), lambda g: (0, g, 0, 0, i, 0))
+
+
+def w_out_spec(i):
+    return pl.BlockSpec((4, 4, 2, 2, 64, 128), lambda g: (0, 0, 0, 0, 4 * i + 3, 0))
 
 
 def w_up_spec(i):
@@ -127,8 +144,8 @@
     return pl.BlockSpec((1, 4, 2, 2, 256, 128), lambda g: (g, 0, 0, 0, i, 0))
 
 
-def rows_by_inputs(w_ref, b):
-    return jnp.concatenate([w_ref[y, 0, a, b] for y in range(4) for a in range(2)], axis=1)
+def rows_by_inputs(w_ref, b, rows=256):
+    return jnp.concatenate([w_ref[y, 0, a, b, :rows] for y in range(4) for a in range(2)], axis=1)
 
 
 def down_block(w_ref):
@@ -153,7 +170,7 @@
 def qkv_kernel(w_ref, x_ref, bias_ref, o_ref):
     x = x_ref[...]
     for b in range(2):
-        r = mm(rows_by_inputs(w_ref, b), x, NN)
+        r = mm(rows_by_inputs(w_ref, b, 192), x, NN)
         for s in range(2):
             v = (r[:, s * 128 : (s + 1) * 128] + bias_ref[0, b]).astype(bf16)
             for j in range(3):
@@ -165,7 +182,7 @@
         qkv_kernel,
         (4,),
         [
-            (w_qkv_spec(), w.qo),
+            (w_qkv_spec(w.qo_at), w.qo),
             whole(seen),
             (pl.BlockSpec((1, 2, 192, 128), lambda g: (g, 0, 0, 0)), bias),
         ],
@@ -197,7 +214,7 @@
     keep, send, blended = call(
         out_kernel,
         (1,),
-        [scalar(core), (w_out_spec(), w.qo), whole(arrived)],
+        [scalar(core), (w_out_spec(w.qo_at), w.qo), whole(arrived)],
         [*PAIR, out_whole((512, 256), bf16)],
         flops=2 * 1024 * 512 * 256,
         moved=2 << 20,
@@ -265,8 +282,7 @@
     low = low_ref[...]
     gu = (mm(down_block(down_ref), low, TN) * slope_ref[...]).astype(bf16)
     bias_ref[...] = jnp.sum(gu.astype(f32), axis=1, keepdims=True)
-    g_ref[0, 0:256] = low_ref[pl.ds(pl.multiple_of(g * 256, 256), 256), :]
-    g_ref[0, 256:768] = gu
+    g_ref[0] = gu
     up = jnp.concatenate([rows_by_inputs(up_ref, b) for b in range(2)], axis=0)
     part = mm(up, gu, TN)
 
@@ -297,7 +313,7 @@
         [
             *PAIR,
             (by_step(512, 1), jax.ShapeDtypeStruct((2048, 1), f32)),
-            (pl.BlockSpec((1, 768, 256), lambda g: (g, 0, 0)), jax.ShapeDtypeStruct((4, 768, 256), bf16)),
+            (pl.BlockSpec((1, 512, 256), lambda g: (g, 0, 0)), jax.ShapeDtypeStruct((4, 512, 256), bf16)),
         ],
         [pltpu.VMEM((D, 256), f32)],
         flops=4 * 2048 * 1024 * 256,
@@ -306,57 +322,85 @@
     return (keep, send), grads, bias
 
 
-def wide(ref, top, rows):
-    return jnp.concatenate([ref[i, top : top + rows] for i in range(4)], axis=1)
-
-
-def ffn_grad_kernel(g_ref, act_ref, seen_ref, o_ref):
-    gd = mm(wide(g_ref, 0, 256), wide(act_ref, 0, 512), NT).astype(bf16)
-    gu = mm(wide(g_ref, 256, 512), wide(seen_ref, 0, 256), NT).astype(bf16)
+def wide(refs, top, rows):
+    return jnp.concatenate([ref[top : top + rows] for ref in refs], axis=1)
+
+
+def from_chips(src_ref, refs):
+    if len(refs) == 4:
+        return jnp.concatenate([ref[...] for ref in refs], axis=1)
+    return jnp.concatenate([refs[0][src_ref[i]] for i in range(4)], axis=1)
+
+
+def down_grad_kernel(*refs):
+    o_ref = refs[-1]
+    gd = mm(wide(refs[:4], 0, 256), jnp.concatenate([ref[0] for ref in refs[4:8]], axis=1), NT).astype(bf16)
+    for z in range(4):
+        for j in range(4):
+            o_ref[0, z, j * 64 : (j + 1) * 64, :] = gd[z * 64 : (z + 1) * 64, j * 128 : (j + 1) * 128]
+
+
+def run_down_grad(l, low, active):
+    return call(
+        down_grad_kernel,
+        (4,),
+        [*[(by_step(256, 256), v) for v in low], *[(pl.BlockSpec((1, 512, 256), lambda g: (l, 0, 0)), v) for v in active]],
+        [(pl.BlockSpec((1, 4, 256, 128), lambda g: (g, 0, 0, 0)), jax.ShapeDtypeStruct((4, 4, 256, 128), bf16))],
+        flops=2 * 1024 * 1024 * 512,
+        moved=6 << 20,
+    )[0]
+
+
+def up_grad_kernel(src_ref, *refs):
+    o_ref = refs[-1]
+    gu = mm(wide(refs[:4], 0, 512), from_chips(src_ref, refs[4:-1]), NT).astype(bf16)
     for a in range(2):
         for b in range(2):
-            z = a * 2 + b
-            o_ref[0, z, 0:256, :] = gu[b * 256 : (b + 1) * 256, a * 128 : (a + 1) * 128]
-            for j in range(4):
-                o_ref[0, z, 256 + j * 64 : 320 + j * 64, :] = gd[z * 64 : (z + 1) * 64, j * 128 : (j + 1) * 128]
-
-
-def inputs_spec(rows, base):
-    return pl.BlockSpec((4, rows, 256), lambda g: (0, base + g, 0))
-
-
-def run_ffn_grad(arrived, inputs):
-    return call(
-        ffn_grad_kernel,
-        (4,),
-        [whole(arrived), (inputs_spec(512, 0), inputs), (inputs_spec(256, 8), inputs)],
-        [(pl.BlockSpec((1, 4, 512, 128), lambda g: (g, 0, 0, 0)), jax.ShapeDtypeStruct((4, 4, 512, 128), bf16))],
-        flops=4 * 2048 * 1024 * 256,
-        moved=14 << 20,
-    )[0]
-
-
-def attend_grad_kernel(g_ref, bl_ref, seen_ref, o_ref):
-    go = mm(wide(g_ref, 0, 256), wide(bl_ref, 0, 128), NT).astype(bf16)
-    gq = mm(wide(g_ref, 256, 384), wide(seen_ref, 0, 256), NT).astype(bf16)
+            o_ref[0, a * 2 + b] = gu[b * 256 : (b + 1) * 256, a * 128 : (a + 1) * 128]
+
+
+def attend_grad_kernel(top, src_ref, *refs):
+    o_ref = refs[-1]
+    g_refs, others = refs[:4], refs[4:-1]
+    half = len(others) // 2
+    go = mm(wide(g_refs, top, 256), from_chips(src_ref, others[:half]), NT).astype(bf16)
+    gq = mm(wide(g_refs, top + 256, 384), from_chips(src_ref, others[half:]), NT).astype(bf16)
     for a in range(2):
         for b in range(2):
             z = a * 2 + b
             for j in range(3):
-                top = j * 128 + b * 64
-                o_ref[0, z, j * 64 : (j + 1) * 64, :] = gq[top : top + 64, a * 128 : (a + 1) * 128]
+                at = j * 128 + b * 64
+                o_ref[0, z, j * 64 : (j + 1) * 64, :] = gq[at : at + 64, a * 128 : (a + 1) * 128]
             o_ref[0, z, 192:256, :] = go[z * 64 : (z + 1) * 64]
 
 
-def run_attend_grad(arrived, inputs):
+def inputs_specs(inputs, rows, base):
+    if isinstance(inputs, list):
+        return [(pl.BlockSpec((rows, 256), lambda g: (base + g, 0)), v) for v in inputs]
+    return [(pl.BlockSpec((4, rows, 256), lambda g: (0, base + g, 0)), inputs)]
+
+
+def run_grad(kernel, src, arrived, inputs, *specs):
     return call(
-        attend_grad_kernel,
+        kernel,
         (4,),
-        [whole(arrived), (inputs_spec(128, 24), inputs), (inputs_spec(256, 14), inputs)],
+        [
+            scalar(src),
+            *[whole(v) for v in arrived],
+            *[one for spec in specs for one in inputs_specs(inputs, *spec)],
+        ],
         [(pl.BlockSpec((1, 4, 256, 128), lambda g: (g, 0, 0, 0)), jax.ShapeDtypeStruct((4, 4, 256, 128), bf16))],
-        flops=2 * 2048 * 1024 * 256,
-        moved=7 << 20,
+        flops=2 * 1024 * 1024 * 512,
+        moved=6 << 20,
     )[0]
+
+
+def run_up_grad(src, arrived, inputs):
+    return run_grad(up_grad_kernel, src, arrived, inputs, (256, 0))
+
+
+def run_attend_grad(top, src, arrived, inputs):
+    return run_grad(partial(attend_grad_kernel, top), src, arrived, inputs, (128, 8), (256, 6))
 
 
 def out_back_kernel(w_ref, low_ref, o_ref):
@@ -370,7 +414,7 @@
     return call(
         out_back_kernel,
         (1,),
-        [(w_out_spec(), w.qo), whole(low)],
+        [(w_out_spec(w.qo_at), w.qo), whole(low)],
         [out_whole((8, 128, 128), bf16)],
         flops=2 * 1024 * 512 * 256,
         moved=2 << 20,
@@ -386,7 +430,7 @@
     for b in range(2):
         gq = jnp.concatenate([both[j * 128 + b * 64 : j * 128 + b * 64 + 64] for j in range(3)], axis=0)
         bias_ref[0, b] = jnp.sum(gq.astype(f32), axis=1, keepdims=True)
-        term = mm(rows_by_inputs(w_ref, b), gq, TN)
+        term = mm(rows_by_inputs(w_ref, b, 192), gq, TN)
         part = term if part is None else part + term
 
     @pl.when(g == 0)
@@ -408,7 +452,7 @@
         (4,),
         [
             scalar(core),
-            (w_qkv_spec(), w.qo),
+            (w_qkv_spec(w.qo_at), w.qo),
             (pl.BlockSpec((2, 1, 384, 128), lambda g: (0, g, 0, 0)), arrived.reshape(2, 4, 384, 128)),
             (by_step(256, 256), low),
         ],
@@ -537,6 +581,7 @@
 ):
     core = lax.axis_index(CORE)
     here = core.astype(jnp.int32).reshape(1)
+    src = jnp.stack([(lax.axis_index(X) - i) % 4 for i in SHIFTS]).astype(jnp.int32)
     traded = trade(
         jnp.concatenate([w_qkv.reshape(LAYERS, 192, 128), w_up.reshape(LAYERS, 256, 128)], axis=1)
     )
@@ -549,10 +594,10 @@
         ],
         axis=1,
     )
-    weights = []
-    for l in range(LAYERS):
-        every = lax.all_gather(pack[l], CHIPS, axis=0, tiled=False).reshape(4, 4, 2, 2, 768, 128)
-        weights.append(Weights(every, every, every, 1, 2))
+    head = jnp.concatenate([pack[0], pack[1, :256]], axis=0)
+    head = lax.all_gather(head, CHIPS, axis=0, tiled=False).reshape(4, 4, 2, 2, 1024, 128)
+    tail = lax.all_gather(pack[1, 256:], CHIPS, axis=0, tiled=False).reshape(4, 4, 2, 2, 512, 128)
+    weights = (Weights(head, head, head, 0, 1, 2), Weights(head, tail, tail, 3, 0, 1))
 
     small = jnp.concatenate(
         [
@@ -575,6 +620,7 @@
 
     stream = lax.all_to_all(tokens, COL, 1, 0, tiled=True).astype(f32)
     back = lax.all_to_all(cotangent, COL, 1, 0, tiled=True).astype(f32)
+    stream, back = lax.optimization_barrier((stream, back))
     stored = []
     for l in range(LAYERS):
         seen = core_gather(stream.astype(bf16))
@@ -587,28 +633,34 @@
         pair, active, slope = run_ffn(weights[l], here, first_seen, b_up[l])
         lower = core_add(pair) + b_down[l][:, None]
         stream, n_ffn, i_ffn = norm_forward(first + lower, g_ffn[l], s_ffn[l])
-        inputs = jnp.concatenate([active, first_seen, blended, seen], axis=0)
+        inputs = jnp.concatenate([first_seen, blended, seen], axis=0)
         inputs = lax.all_gather(inputs, X, axis=0, tiled=False)
-        stored.append((inputs, packed, log, n_attn, i_attn, slope, n_ffn, i_ffn))
-    result = lax.all_to_all(stream.astype(bf16), COL, 0, 1, tiled=True)
+        stored.append((inputs, active, packed, log, n_attn, i_attn, slope, n_ffn, i_ffn))
+    result = stream.astype(bf16)
+    active = jnp.stack([kept[1].reshape(4, 512, 256) for kept in stored], axis=1)
+    active = exchange(active, Y)
 
     minor = [None] * LAYERS
     for l in reversed(range(LAYERS)):
-        (inputs, packed, log, n_attn, i_attn, slope, n_ffn, i_ffn) = stored[l]
+        (inputs, _, packed, log, n_attn, i_attn, slope, n_ffn, i_ffn) = stored[l]
         grad_sum = norm_backward(back, n_ffn, i_ffn, g_ffn[l])
         p_gain_ffn = jnp.sum(back * n_ffn, axis=1)
         p_shift_ffn = jnp.sum(back, axis=1)
         low = grad_sum.astype(bf16)
         p_down = jnp.sum(low.astype(f32), axis=1)
-        pair, send_ud, p_up = run_ffn_back(weights[l], here, core_gather(low), slope)
-        g_ud = lax.all_to_all(send_ud, X, 0, 0, tiled=True)
+        low = core_gather(low)
+        g_down = everyone(low, Y)
+        pair, send_up, p_up = run_ffn_back(weights[l], here, low, slope)
         if l == 0:
+            g_up = exchange(send_up, X)
+        if l == 0:
+            late = after(late, send_up)
+            downs = jnp.stack(
+                [run_down_grad(0, g_down, active), run_down_grad(1, late[0], active)], axis=2
+            )
             rest = jnp.concatenate(
-                [run_ffn_grad(after(late[0], send_ud), late[2]), run_attend_grad(after(late[1], send_ud), late[2])],
-                axis=2,
+                [run_up_grad(src, late[1], late[2]), run_attend_grad(512, src, late[1], late[2])], axis=2
             )
-            rest = lax.psum_scatter(rest.reshape(16, 768, 128), ("y",) + Z, scatter_dimension=0)
-            ud = reduce_stage(run_ffn_grad(g_ud, inputs).reshape(16, 512, 128), ("y",) + Z)
         grad_first = core_add(pair) + grad_sum
         p_gain_attn = jnp.sum(grad_first * n_attn, axis=1)
         p_shift_attn = jnp.sum(grad_first, axis=1)
@@ -618,16 +670,27 @@
         low = core_gather(low)
         grad_blended = seq_swap(run_out_back(weights[l], low))
         grad_qkv = seq_swap(run_attend_back(packed, grad_blended, log))
+        if l == 0:
+            low, downs, rest, up_0 = lax.optimization_barrier(
+                (low, downs, rest, run_up_grad(src, g_up, inputs))
+            )
+            rest = lax.psum_scatter(rest.reshape(16, 512, 128), ("y",) + Z, scatter_dimension=0)
+            downs = reduce_stage(downs.reshape(16, 512, 128), COL)
         pair, send_qo, p_qkv = run_qkv_back(weights[l], here, grad_qkv, low)
-        g_qo = lax.all_to_all(send_qo, X, 0, 0, tiled=True)
         if l == 1:
-            late = (g_ud, g_qo, inputs)
+            late = (g_down, exchange(jnp.concatenate([send_up, send_qo], axis=1), X), inputs)
         else:
-            qo = reduce_stage(run_attend_grad(g_qo, inputs).reshape(16, 256, 128), ("y",) + Z)
+            send_qo = after(send_qo, downs)
+            g_qo = exchange(send_qo, X)
+            first = jnp.concatenate(
+                [up_0, run_attend_grad(0, src, g_qo, inputs)], axis=2
+            )
+            pair = after(pair, first)
+            first = reduce_stage(first.reshape(16, 512, 128), ("y",) + Z)
         back = core_add(pair) + grad_total
         minor[l] = (p_qkv, p_out, p_gain_attn, p_shift_attn, p_down, p_gain_ffn, p_shift_ffn, p_up)
     rest = after(rest, send_qo).astype(f32)
-    sums = ((ud[256:], ud[:256], qo), (rest[256:512], rest[:256], rest[512:]))
+    sums = ((downs[:256], first[:256], first[256:]), (downs[256:], rest[:256], rest[256:]))
     swapped = trade(
         jnp.stack([jnp.concatenate([q[:192], u], axis=0) for _, u, q in sums]).astype(bf16)
     ).astype(f32)
@@ -640,8 +703,6 @@
         )
         for l in range(LAYERS)
     ]
-    grad_tokens = lax.all_to_all(back.astype(bf16), COL, 0, 1, tiled=True).astype(f32)
-
     mine = (jnp.arange(2) == core).astype(f32)
     qv = jnp.stack([m[0].reshape(4, 2, 3, 64)[:, :, ::2] for m in minor])
     qv = qv.transpose(1, 2, 0, 3, 4)
@@ -650,8 +711,15 @@
     up = (up[:, None] * mine[None, :, None, None, None]).reshape(16, 512)
     feats = jnp.stack([jnp.stack([m[i] for m in minor]) for i in range(1, 7)])
     feats = feats.reshape(6, LAYERS, 16, 64).transpose(2, 0, 1, 3).reshape(16, 768)
-    sums = jnp.concatenate([qv, feats, up], axis=1).reshape(4, 4, 12, 128)
-    sums2 = sum_axis(reduce_stage(sums.reshape(16, 12, 128), COL), Y)
+    sums = jnp.concatenate([qv, feats, up], axis=1).reshape(16, 12, 128)
+    high = sums.astype(bf16)
+    low = (sums - high.astype(f32)).astype(bf16)
+    send = jnp.concatenate([result.reshape(16, 64, 128), back.astype(bf16).reshape(16, 64, 128), high, low], axis=1)
+    got = lax.all_to_all(send, COL, 0, 0, tiled=True)
+    result = got[:, :64].transpose(1, 0, 2).reshape(64, 2048)
+    grad_tokens = got[:, 64:128].astype(f32).transpose(1, 0, 2).reshape(64, 2048)
+    sums2 = jnp.sum(got[:, 128:140].astype(f32), axis=0) + jnp.sum(got[:, 140:].astype(f32), axis=0)
+    sums2 = sum_axis(sums2, Y)
     sums2 = sums2 + lax.ppermute(sums2, CORE, [(0, 1), (1, 0)])
     flat = sums2.reshape(1536)
     o_qv = flat[:256].reshape(LAYERS, 2, 64)

time: 644 us -> 579 us (0.90)
  waiting for transfers between devices: 217 us -> 163 us
  blocking collectives: 121 us -> 112 us
  Pallas kernels: 103 us -> 110 us
    all_to_all x6 -> x0, waiting for transfers between devices: 56.9 us -> none  [the longest x2 33.2 us: on_device(): g_ud = lax.all_to_all(send_ud, X, 0, 0, tiled=True)]
    all_gather x2, waiting for transfers between devices: 92.4 us -> 63.2 us  [the longest x1 63.2 us: on_device(): lax.all_gather(head, CHIPS, axis=0, tiled=False)]
    ppermute x0 -> x18, starting transfers between devices: none -> 26.3 us  [along(): return lax.ppermute(values, axes, [(i, (i + shift) % 4) for i in range(4)])]
    all_to_all x6 -> x0, starting transfers between devices: 24.1 us -> none  [the longest x2 7.26 us: on_device(): g_ud = lax.all_to_all(send_ud, X, 0, 0, tiled=True)]
    all_to_all x6 -> x5, blocking collectives: 86.8 us -> 67.5 us  [seq_swap(): return lax.all_to_all(values, SEQ, 0, 0, tiled=True)]
    ppermute x0 -> x18, waiting for transfers between devices: none -> 17.1 us  [along(): return lax.ppermute(values, axes, [(i, (i + shift) % 4) for i in range(4)])]
    all_to_all x2, waiting for transfers between devices: 5.69 us -> 13.5 us  [reduce_stage(): lax.all_to_all(g, axes, 0, 0, tiled=True).astype(f32)]
    ppermute x1, starting transfers between devices: 9.41 us -> 2.13 us  [on_device(): sums2 = sums2 + lax.ppermute(sums2, CORE, [(0, 1), (1, 0)])]
  transfers between devices with their start and end apart: 32 -> 45, of which waited for: 22 -> 21; matrix products, arithmetic and copies ran while one was open for 7% -> 9% of each run, Pallas kernels for 13% -> 19%
where the time goes in v4:
time: 579 us; the launch traced here: 568 us
  waiting for transfers between devices  163 us (28%)
  blocking collectives  112 us (19%)
  Pallas kernels  110 us (19%)
  starting transfers between devices  98 us (17%)
  local copies, waits for them, and re-layouts  39.3 us (7%)
  other arithmetic  30.1 us (5%)
  between operations  15.8 us (3%)
    pallas_call x22, Pallas kernels, call(): pl.pallas_call(kernel, grid=grid, in_specs=[spec for spec, _ in ins], out...  110 us
    all_to_all x5, blocking collectives, seq_swap(): return lax.all_to_all(values, SEQ, 0, 0, tiled=True)  67.5 us
    all_gather x1, waiting for transfers between devices, on_device(): lax.all_gather(head, CHIPS, axis=0, tiled=False)  63.2 us
    all_gather x8, blocking collectives, core_gather(): return lax.all_gather(values, CORE, axis=1, tiled=True)  27.9 us
    ppermute x18, starting transfers between devices, along(): return lax.ppermute(values, axes, [(i, (i + shift) % 4) for i in range(4)])  26.3 us
    ppermute x3, waiting for transfers between devices, sum_axis(): lax.ppermute(values, axes, [(i, (i + shift) % 4) for i in range(4)])  22.1 us
    ppermute x8, starting transfers between devices, core_add(): return keep + lax.ppermute(send, CORE, [(0, 1), (1, 0)]).astype(f32)  17.4 us
    ppermute x18, waiting for transfers between devices, along(): return lax.ppermute(values, axes, [(i, (i + shift) % 4) for i in range(4)])  17.1 us
  transfers between devices with their start and end apart: 45, of which 21 were waited for; matrix products, arithmetic and copies ran while one was open for 9% of the time, Pallas kernels for 19%

profile of v4, /device:TPU:1, one launch (start us, length us, event | category | flops | bytes accessed | tf_op | source)
XLA Modules:
  0.0 567.7 jit_solution(323830912609094546)
XLA Ops:
  8.4 6.9 %collective-permute-start = (bf16[2,448,128]{2,1,0:T(8,128)(2,1)S(1)}, bf16[2,448,128]{2,1,0:T(8,128)(2,1)S(1)}, u32[]{:S(2)}, u32[]{:S(2)}) collective-permute-start(bf16[2,448,128]{2,1,0:T(8,128)(2,1)S(1)} %pad_maximum_fusion.8), channel_id=1, source_target_pairs={{0,0},{2,16},{16,2},{18,18},{1,1},{3,17},{17,3},{19,19},{4,4},{6,2... | collective-permute-start | bytes 688136 | tf_op jit(solution)/shard_map/ppermute | solution.py:47
  23.4 4.6 all-to-all-start.2
  29.6 5.0 all-to-all-done.2
  34.6 3.5 all-to-all-start
  38.3 7.9 %all-to-all-done = bf16[64,16,128]{2,0,1:T(8,128)(2,1)S(1)} async-done(((bf16[64,16,128]{2,0,1:T(8,128)(2,1)}), bf16[64,16,128]{2,0,1:T(8,128)(2,1)S(1)}, u32[]{:S(2)}, u32[]{:S(2)}) %all-to-all-start) | async-done | bytes 262176 | tf_op jit(solution)/shard_map/all_to_all | solution.py:621
  46.2 3.5 all-to-all-start.1
  50.0 7.0 %all-to-all-done.1 = bf16[64,16,128]{2,0,1:T(8,128)(2,1)S(1)} async-done(((bf16[64,16,128]{2,0,1:T(8,128)(2,1)}), bf16[64,16,128]{2,0,1:T(8,128)(2,1)S(1)}, u32[]{:S(2)}, u32[]{:S(2)}) %all-to-all-start.1) | async-done | bytes 262176 | tf_op jit(solution)/shard_map/all_to_all | solution.py:622
  57.1 9.5 %all_gather.47.x_ref = bf16[1024,256]{1,0:T(8,128)(2,1)S(1)} all-gather(bf16[1024,128]{1,0:T(8,128)(2,1)S(1)} %convert_element_type.128), channel_id=1, replica_groups=mesh['y'=4,'k'=2,'xh'=2,'xl'=2,'zh'=2,'zl'=2] {'k'}, dimensions={1}, use_global_device_ids=true | all-gather | bytes 786432 | tf_op jit(solution)/shard_map/all_gather | solution.py:38
  66.6 63.2 %all-gather.10.cloned.1.call-done = bf16[65536,128]{1,0:T(8,128)(2,1)} async-done(((bf16[1024,128]{1,0:T(8,128)(2,1)}), bf16[65536,128]{1,0:T(8,128)(2,1)}) %all-gather.10.cloned.1.call-update) | async-done | bytes 16777232 | tf_op jit(solution)/shard_map/all_gather | solution.py:598
  130.1 3.8 shard_map.245
  133.8 15.9 %all_to_all.90.p_ref = bf16[8,384,128]{2,1,0:T(8,128)(2,1)S(1)} all-to-all(bf16[8,384,128]{2,1,0:T(8,128)(2,1)S(1)} %bitcast.153), channel_id=1, replica_groups=mesh['y'=4,'k'=2,'xh'=2,'xl'=2,'zh'=2,'zl'=2] {'xl','zh','zl'}, dimensions={0} | all-to-all | bytes 1572864 | tf_op jit(solution)/shard_map/all_to_all | solution.py:547
  149.8 6.5 %shard_map.246 = (bf16[8,128,128]{2,1,0:T(8,128)(2,1)S(1)}, f32[2,1024]{1,0:T(2,128)S(1)}) custom-call(bf16[8,384,128]{2,1,0:T(8,128)(2,1)S(1)} %all_to_all.90.p_ref), custom_call_target="tpu_custom_call" | custom-call | flops 1073741824 | bytes 1048576 | tf_op jit(solution)/shard_map/pallas_call | solution.py:95
  156.3 8.9 %all_to_all.91.b_ref = bf16[8,128,128]{2,1,0:T(8,128)(2,1)S(1)} all-to-all(bf16[8,128,128]{2,1,0:T(8,128)(2,1)S(1)} %get-tuple-element.68), channel_id=1, replica_groups=mesh['y'=4,'k'=2,'xh'=2,'xl'=2,'zh'=2,'zl'=2] {'xl','zh','zl'}, dimensions={0} | all-to-all | bytes 524288 | tf_op jit(solution)/shard_map/all_to_all | solution.py:547
  176.1 7.7 %shard_map.248 = (f32[1024,128]{1,0:T(8,128)S(1)}, bf16[1024,128]{1,0:T(8,128)(2,1)S(1)}, bf16[2048,256]{1,0:T(8,128)(2,1)S(1)}, f32[2048,256]{1,0:T(8,128)}) custom-call(s32[1]{0:T(128)} %bitcast.4.core_ref, bf16[4,4,2,2,1024,128]{5,4,3,2,1,0:T(8,128)(2,1)} %bitcast.161, bf16[4,4,2,2,1024,128]{5,4,3,2,1,0:T(8,128)(2,1)} %bitcast.162, ...), custom_call_target="tpu_custom_call" | custom-call | flops 2147483648 | bytes 13631488 | tf_op jit(solution)/shard_map/pallas_call | solution.py:95
  190.0 3.8 shard_map.249
  193.8 22.5 %all_to_all.92.p_ref = bf16[8,384,128]{2,1,0:T(8,128)(2,1)S(1)} all-to-all(bf16[8,384,128]{2,1,0:T(8,128)(2,1)S(1)} %bitcast.154), channel_id=1, replica_groups=mesh['y'=4,'k'=2,'xh'=2,'xl'=2,'zh'=2,'zl'=2] {'xl','zh','zl'}, dimensions={0} | all-to-all | bytes 1572864 | tf_op jit(solution)/shard_map/all_to_all | solution.py:547
  216.3 6.5 %shard_map.250 = (bf16[8,128,128]{2,1,0:T(8,128)(2,1)S(1)}, f32[2,1024]{1,0:T(2,128)S(1)}) custom-call(bf16[8,384,128]{2,1,0:T(8,128)(2,1)S(1)} %all_to_all.92.p_ref), custom_call_target="tpu_custom_call" | custom-call | flops 1073741824 | bytes 1048576 | tf_op jit(solution)/shard_map/pallas_call | solution.py:95
  222.9 9.2 %all_to_all.93.b_ref = bf16[8,128,128]{2,1,0:T(8,128)(2,1)S(1)} all-to-all(bf16[8,128,128]{2,1,0:T(8,128)(2,1)S(1)} %get-tuple-element.73), channel_id=1, replica_groups=mesh['y'=4,'k'=2,'xh'=2,'xl'=2,'zh'=2,'zl'=2] {'xl','zh','zl'}, dimensions={0} | all-to-all | bytes 524288 | tf_op jit(solution)/shard_map/all_to_all | solution.py:547
  241.4 7.7 %shard_map.252 = (f32[1024,128]{1,0:T(8,128)S(1)}, bf16[1024,128]{1,0:T(8,128)(2,1)S(1)}, bf16[2048,256]{1,0:T(8,128)(2,1)S(1)}, f32[2048,256]{1,0:T(8,128)}) custom-call(s32[1]{0:T(128)} %bitcast.4.core_ref, bf16[4,4,2,2,512,128]{5,4,3,2,1,0:T(8,128)(2,1)} %bitcast.171, bf16[4,4,2,2,512,128]{5,4,3,2,1,0:T(8,128)(2,1)} %bitcast.172, ...), custom_call_target="tpu_custom_call" | custom-call | flops 2147483648 | bytes 13631488 | tf_op jit(solution)/shard_map/pallas_call | solution.py:95
  256.5 7.9 %shard_map.253 = (f32[1024,128]{1,0:T(8,128)S(1)}, bf16[1024,128]{1,0:T(8,128)(2,1)S(1)}, f32[2048,1]{1,0:T(8,128)S(1)}, bf16[4,512,256]{2,1,0:T(8,128)(2,1)S(1)}) custom-call(s32[1]{0:T(128)} %bitcast.4.core_ref, bf16[4,4,2,2,512,128]{5,4,3,2,1,0:T(8,128)(2,1)} %bitcast.173, bf16[4,4,2,2,512,128]{5,4,3,2,1,0:T(8,128)(2,1)} %bitcast.174, ...), custom_call_target="tpu_custom_call" | custom-call | flops 2147483648 | bytes 14680064 | tf_op jit(solution)/shard_map/pallas_call | solution.py:95
  271.1 10.9 %all_to_all.94.b_ref = bf16[8,128,128]{2,1,0:T(8,128)(2,1)S(1)} all-to-all(bf16[8,128,128]{2,1,0:T(8,128)(2,1)S(1)} %shard_map.254), channel_id=1, replica_groups=mesh['y'=4,'k'=2,'xh'=2,'xl'=2,'zh'=2,'zl'=2] {'xl','zh','zl'}, dimensions={0} | all-to-all | bytes 524288 | tf_op jit(solution)/shard_map/all_to_all | solution.py:547
  282.0 6.8 %shard_map.255 = bf16[8,384,128]{2,1,0:T(8,128)(2,1)S(1)} custom-call(bf16[8,384,128]{2,1,0:T(8,128)(2,1)S(1)} %copy-done.23, bf16[8,128,128]{2,1,0:T(8,128)(2,1)S(1)} %all_to_all.94.b_ref, f32[2,1024]{1,0:T(2,128)S(1)} %get-tuple-element.82.log_ref), custom_call_target="tpu_custom_call" | custom-call | flops 2684354560 | bytes 2097152 | tf_op jit(solution)/shard_map/pallas_call | solution.py:95
  289.7 3.6 all-to-all-start.8
  293.3 16.4 %all-to-all-done.8 = bf16[8,384,128]{2,1,0:T(8,128)(2,1)S(1)} async-done(((bf16[8,384,128]{2,1,0:T(8,128)(2,1)}), bf16[8,384,128]{2,1,0:T(8,128)(2,1)S(1)}, u32[]{:S(2)}, u32[]{:S(2)}) %all-to-all-start.8) | async-done | bytes 786464 | tf_op jit(solution)/shard_map/all_to_all | solution.py:547
  309.7 5.4 shard_map.256
  315.1 3.6 collective-permute-start.6
  328.0 7.8 %shard_map.257 = (f32[1024,128]{1,0:T(8,128)S(1)}, bf16[1024,128]{1,0:T(8,128)(2,1)S(1)}, f32[2048,1]{1,0:T(8,128)S(1)}, bf16[4,512,256]{2,1,0:T(8,128)(2,1)S(1)}) custom-call(s32[1]{0:T(128)} %bitcast.4.core_ref, bf16[4,4,2,2,1024,128]{5,4,3,2,1,0:T(8,128)(2,1)} %bitcast.167, bf16[4,4,2,2,1024,128]{5,4,3,2,1,0:T(8,128)(2,1)} %bitcast.168, ...), custom_call_target="tpu_custom_call" | custom-call | flops 2147483648 | bytes 14680064 | tf_op jit(solution)/shard_map/pallas_call | solution.py:95
  346.5 4.1 all_gather.55.low_ref
  353.1 5.7 %all-to-all-start.9 = ((bf16[8,128,128]{2,1,0:T(8,128)(2,1)}), bf16[8,128,128]{2,1,0:T(8,128)(2,1)}, u32[]{:S(2)}, u32[]{:S(2)}) async-start(bf16[8,128,128]{2,1,0:T(8,128)(2,1)} %shard_map.258), calls=%async_computation.9 | async-start | bytes 524288 | tf_op jit(solution)/shard_map/all_to_all | solution.py:547
  371.5 6.3 %collective-permute-start.18 = (bf16[1152,256]{1,0:T(8,128)(2,1)}, bf16[1152,256]{1,0:T(8,128)(2,1)}, u32[]{:S(2)}, u32[]{:S(2)}) collective-permute-start(bf16[1152,256]{1,0:T(8,128)(2,1)} %get-tuple-element.178), channel_id=1, source_target_pairs={{0,12},{4,0},{8,4},{12,8},{1,13},{5,1},{9,5},{13,9},{2,14},{6,2},{... | collective-permute-start | bytes 1769480 | tf_op jit(solution)/shard_map/ppermute | solution.py:62
  382.9 7.7 %shard_map.259 = bf16[8,384,128]{2,1,0:T(8,128)(2,1)S(1)} custom-call(bf16[8,384,128]{2,1,0:T(8,128)(2,1)S(1)} %copy-done.20, bf16[8,128,128]{2,1,0:T(8,128)(2,1)} %all-to-all-done.9.b_ref, f32[2,1024]{1,0:T(2,128)S(1)} %get-tuple-element.88.log_ref), custom_call_target="tpu_custom_call" | custom-call | flops 2684354560 | bytes 2097152 | tf_op jit(solution)/shard_map/pallas_call | solution.py:95
  391.5 4.0 all-to-all-start.10
  397.6 4.6 shard_map.260
  406.0 3.6 shard_map.264
  410.7 4.5 shard_map.263
  415.3 4.3 shard_map.262
  419.6 4.5 shard_map.261
  428.6 6.6 %all-to-all-start.11 = ((bf16[16,512,128]{2,1,0:T(8,128)(2,1)}), bf16[16,512,128]{2,1,0:T(8,128)(2,1)}, u32[]{:S(2)}, u32[]{:S(2)}) async-start(bf16[16,512,128]{2,1,0:T(8,128)(2,1)} %bitcast.182), calls=%async_computation.11 | async-start | bytes 4194304 | tf_op jit(solution)/shard_map/all_to_all | solution.py:55
  441.2 5.2 shard_map.265
  447.0 13.5 %all-to-all-done.11 = bf16[16,512,128]{2,1,0:T(8,128)(2,1)} async-done(((bf16[16,512,128]{2,1,0:T(8,128)(2,1)}), bf16[16,512,128]{2,1,0:T(8,128)(2,1)}, u32[]{:S(2)}, u32[]{:S(2)}) %all-to-all-start.11) | async-done | bytes 2097184 | tf_op jit(solution)/shard_map/all_to_all | solution.py:55
  467.4 3.7 collective-permute-done.23.refs_1_
  473.7 4.3 collective-permute-done.25.refs_3_
  477.9 4.1 shard_map.266
  483.6 5.6 collective-permute-start.26
  490.7 16.4 %all_to_all.95 = bf16[16,152,128]{2,1,0:T(8,128)(2,1)S(1)} all-to-all(bf16[16,152,128]{2,1,0:T(8,128)(2,1)S(1)} %pad_maximum_fusion.5), channel_id=1, replica_groups=mesh['y'=4,'k'=2,'xh'=2,'xl'=2,'zh'=2,'zl'=2] {'xh','xl','zh','zl'}, dimensions={0} | all-to-all | bytes 1245184 | tf_op jit(solution)/shard_map/all_to_all | solution.py:718
  507.1 4.0 all-to-all-start.13
  516.6 22.1 %collective-permute-done.30 = f32[12,128]{1,0:T(8,128)S(1)} collective-permute-done((f32[12,128]{1,0:T(8,128)S(1)}, f32[12,128]{1,0:T(8,128)S(1)}, u32[]{:S(2)}, u32[]{:S(2)}) %collective-permute-start.30) | collective-permute-done | bytes 6176 | tf_op jit(solution)/shard_map/ppermute | solution.py:90
  550.5 5.1 collective-permute-start.27
  (441 shorter events, 145.8 us)
Async XLA Ops:
  7.3 122.5 %all-gather.10.cloned.1.call-start = ((), (), s32[]{:S(2)}) async-start(), calls=%async_computation.16 | async-start | bytes 17039360 | tf_op jit(solution)/shard_map/all_gather | solution.py:598
  8.4 10.6 %collective-permute-start = (bf16[2,448,128]{2,1,0:T(8,128)(2,1)S(1)}, bf16[2,448,128]{2,1,0:T(8,128)(2,1)S(1)}, u32[]{:S(2)}, u32[]{:S(2)}) collective-permute-start(bf16[2,448,128]{2,1,0:T(8,128)(2,1)S(1)} %pad_maximum_fusion.8), channel_id=1, source_target_pairs={{0,0},{2,16},{16,2},{18,18},{1,1},{3,17},{17,3},{19,19},{4,4},{6,2... | collective-permute-start | bytes 688136 | tf_op jit(solution)/shard_map/ppermute | solution.py:47
  21.3 219.8 %all-gather.8.cloned.1.call-start = ((), (), s32[]{:S(2)}) async-start(), calls=%async_computation.15 | async-start | bytes 8519680 | tf_op jit(solution)/shard_map/all_gather | solution.py:599
  23.4 11.2 %all-to-all-start.2 = ((f32[16,1,1536]{2,1,0:T(1,128)}), f32[16,1,1536]{2,1,0:T(1,128)S(1)}, u32[]{:S(2)}, u32[]{:S(2)}) async-start(f32[16,1,1536]{2,1,0:T(1,128)} %broadcast_in_dim.18), calls=%async_computation.2 | async-start | bytes 196608 | tf_op jit(solution)/shard_map/all_to_all | solution.py:608
  34.6 11.6 %all-to-all-start = ((bf16[64,16,128]{2,0,1:T(8,128)(2,1)}), bf16[64,16,128]{2,0,1:T(8,128)(2,1)S(1)}, u32[]{:S(2)}, u32[]{:S(2)}) async-start(bf16[64,16,128]{2,0,1:T(8,128)(2,1)} %copy_bitcast_fusion.3), calls=%async_computation | async-start | bytes 524288 | tf_op jit(solution)/shard_map/all_to_all | solution.py:621
  46.2 10.8 %all-to-all-start.1 = ((bf16[64,16,128]{2,0,1:T(8,128)(2,1)}), bf16[64,16,128]{2,0,1:T(8,128)(2,1)S(1)}, u32[]{:S(2)}, u32[]{:S(2)}) async-start(bf16[64,16,128]{2,0,1:T(8,128)(2,1)} %copy_bitcast_fusion.2), calls=%async_computation.1 | async-start | bytes 524288 | tf_op jit(solution)/shard_map/all_to_all | solution.py:622
  49.7 352.5 %all-gather.14.cloned.1.call-start = ((), (), s32[]{:S(2)}) async-start(), calls=%async_computation.18 | async-start | bytes 6553600 | tf_op jit(solution)/shard_map/all_gather | solution.py:637
  57.1 195.8 %copy-start.44 = (f32[64,16,128]{2,0,1:T(8,128)}, f32[64,16,128]{2,0,1:T(8,128)S(1)}, u32[]{:S(2)}) copy-start(f32[64,16,128]{2,0,1:T(8,128)S(1)} %convert_element_type.162) | copy-start | bytes 1572868
  167.0 4.5 collective-permute-start.1
  175.7 235.0 %all-gather.12.cloned.1.call-start = ((), (), s32[]{:S(2)}) async-start(), calls=%async_computation.17 | async-start | bytes 6553600 | tf_op jit(solution)/shard_map/all_gather | solution.py:637
  184.8 1.7 collective-permute-start.2
  187.1 50.8 %copy-start.39 = (f32[1024,128]{1,0:T(8,128)}, f32[1024,128]{1,0:T(8,128)S(1)}, u32[]{:S(2)}) copy-start(f32[1024,128]{1,0:T(8,128)S(1)} %get-tuple-element.174) | copy-start | bytes 1572868
  187.2 136.0 %copy-start.63 = (f32[128]{0:T(128)}, f32[128]{0:T(128)S(1)}, u32[]{:S(2)}) copy-start(f32[128]{0:T(128)S(1)} %add_rsqrt_fusion.2) | copy-start | bytes 1540
  233.8 4.0 collective-permute-start.3
  250.1 1.6 collective-permute-start.4
  264.4 1.6 collective-permute-start.5
  289.7 20.0 %all-to-all-start.8 = ((bf16[8,384,128]{2,1,0:T(8,128)(2,1)}), bf16[8,384,128]{2,1,0:T(8,128)(2,1)S(1)}, u32[]{:S(2)}, u32[]{:S(2)}) async-start(bf16[8,384,128]{2,1,0:T(8,128)(2,1)} %copy-done.21), calls=%async_computation.8 | async-start | bytes 1572864 | tf_op jit(solution)/shard_map/all_to_all | solution.py:547
  315.1 8.1 %collective-permute-start.6 = (bf16[1024,128]{1,0:T(8,128)(2,1)S(1)}, bf16[1024,128]{1,0:T(8,128)(2,1)S(1)}, u32[]{:S(2)}, u32[]{:S(2)}) collective-permute-start(bf16[1024,128]{1,0:T(8,128)(2,1)S(1)} %get-tuple-element.84), channel_id=1, source_target_pairs={{0,16},{16,0},{1,17},{17,1},{2,18},{18,2},{3,19},{19,3},{4,20},{20... | collective-permute-start | bytes 786440 | tf_op jit(solution)/shard_map/ppermute | solution.py:43
  319.0 21.2 %collective-permute-start.11 = (bf16[2,512,256]{2,1,0:T(8,128)(2,1)S(1)}, bf16[2,512,256]{2,1,0:T(8,128)(2,1)S(1)}, u32[]{:S(2)}, u32[]{:S(2)}) collective-permute-start(bf16[2,512,256]{2,1,0:T(8,128)(2,1)S(1)} %get-tuple-element.183), channel_id=1, source_target_pairs={{0,32},{32,64},{64,96},{96,0},{1,33},{33,65},{65,97},{97,1},{2,34}... | collective-permute-start | bytes 1572872 | tf_op jit(solution)/shard_map/ppermute | solution.py:62
  319.7 21.9 %collective-permute-start.12 = (bf16[2,512,256]{2,1,0:T(8,128)(2,1)S(1)}, bf16[2,512,256]{2,1,0:T(8,128)(2,1)S(1)}, u32[]{:S(2)}, u32[]{:S(2)}) collective-permute-start(bf16[2,512,256]{2,1,0:T(8,128)(2,1)S(1)} %get-tuple-element.184), channel_id=1, source_target_pairs={{0,96},{32,0},{64,32},{96,64},{1,97},{33,1},{65,33},{97,65},{2,98}... | collective-permute-start | bytes 1572872 | tf_op jit(solution)/shard_map/ppermute | solution.py:62
  321.7 23.8 %collective-permute-start.13 = (bf16[2,512,256]{2,1,0:T(8,128)(2,1)S(1)}, bf16[2,512,256]{2,1,0:T(8,128)(2,1)S(1)}, u32[]{:S(2)}, u32[]{:S(2)}) collective-permute-start(bf16[2,512,256]{2,1,0:T(8,128)(2,1)S(1)} %get-tuple-element.181), channel_id=1, source_target_pairs={{0,64},{32,96},{64,0},{96,32},{1,65},{33,97},{65,1},{97,33},{2,66}... | collective-permute-start | bytes 1572872 | tf_op jit(solution)/shard_map/ppermute | solution.py:62
  322.7 36.1 %collective-permute-start.14 = (bf16[1024,256]{1,0:T(8,128)(2,1)S(1)}, bf16[1024,256]{1,0:T(8,128)(2,1)S(1)}, u32[]{:S(2)}, u32[]{:S(2)}) collective-permute-start(bf16[1024,256]{1,0:T(8,128)(2,1)S(1)} %all_gather.52.low_ref.refs_0_), channel_id=1, source_target_pairs={{0,32},{32,64},{64,96},{96,0},{1,33},{33,65},{65,97},{97,1},{2,34}... | collective-permute-start | bytes 1572872 | tf_op jit(solution)/shard_map/ppermute | solution.py:62
  335.9 1.6 collective-permute-start.7
  337.5 40.4 %collective-permute-start.8 = (bf16[1024,256]{1,0:T(8,128)(2,1)S(1)}, bf16[1024,256]{1,0:T(8,128)(2,1)}, u32[]{:S(2)}, u32[]{:S(2)}) collective-permute-start(bf16[1024,256]{1,0:T(8,128)(2,1)S(1)} %all_gather.54.low_ref.refs_0_), channel_id=1, source_target_pairs={{0,32},{32,64},{64,96},{96,0},{1,33},{33,65},{65,97},{97,1},{2,34}... | collective-permute-start | bytes 1572872 | tf_op jit(solution)/shard_map/ppermute | solution.py:62
  340.2 38.3 %collective-permute-start.9 = (bf16[1024,256]{1,0:T(8,128)(2,1)S(1)}, bf16[1024,256]{1,0:T(8,128)(2,1)}, u32[]{:S(2)}, u32[]{:S(2)}) collective-permute-start(bf16[1024,256]{1,0:T(8,128)(2,1)S(1)} %all_gather.54.low_ref.refs_0_), channel_id=1, source_target_pairs={{0,96},{32,0},{64,32},{96,64},{1,97},{33,1},{65,33},{97,65},{2,98}... | collective-permute-start | bytes 1572872 | tf_op jit(solution)/shard_map/ppermute | solution.py:62
  341.6 38.5 %collective-permute-start.10 = (bf16[1024,256]{1,0:T(8,128)(2,1)S(1)}, bf16[1024,256]{1,0:T(8,128)(2,1)}, u32[]{:S(2)}, u32[]{:S(2)}) collective-permute-start(bf16[1024,256]{1,0:T(8,128)(2,1)S(1)} %all_gather.54.low_ref.refs_0_), channel_id=1, source_target_pairs={{0,64},{32,96},{64,0},{96,32},{1,65},{33,97},{65,1},{97,33},{2,66}... | collective-permute-start | bytes 1572872 | tf_op jit(solution)/shard_map/ppermute | solution.py:62
  345.5 16.2 %collective-permute-start.20 = (bf16[512,256]{1,0:T(8,128)(2,1)}, bf16[512,256]{1,0:T(8,128)(2,1)S(1)}, u32[]{:S(2)}, u32[]{:S(2)}) collective-permute-start(bf16[512,256]{1,0:T(8,128)(2,1)} %get-tuple-element.191), channel_id=1, source_target_pairs={{0,4},{4,8},{8,12},{12,0},{1,5},{5,9},{9,13},{13,1},{2,6},{6,10},{... | collective-permute-start | bytes 786440 | tf_op jit(solution)/shard_map/ppermute | solution.py:62
  353.1 29.8 %all-to-all-start.9 = ((bf16[8,128,128]{2,1,0:T(8,128)(2,1)}), bf16[8,128,128]{2,1,0:T(8,128)(2,1)}, u32[]{:S(2)}, u32[]{:S(2)}) async-start(bf16[8,128,128]{2,1,0:T(8,128)(2,1)} %shard_map.258), calls=%async_computation.9 | async-start | bytes 524288 | tf_op jit(solution)/shard_map/all_to_all | solution.py:547
  359.6 9.5 %collective-permute-start.21 = (bf16[512,256]{1,0:T(8,128)(2,1)}, bf16[512,256]{1,0:T(8,128)(2,1)S(1)}, u32[]{:S(2)}, u32[]{:S(2)}) collective-permute-start(bf16[512,256]{1,0:T(8,128)(2,1)} %get-tuple-element.190), channel_id=1, source_target_pairs={{0,12},{4,0},{8,4},{12,8},{1,13},{5,1},{9,5},{13,9},{2,14},{6,2},{... | collective-permute-start | bytes 786440 | tf_op jit(solution)/shard_map/ppermute | solution.py:62
  362.4 8.4 %collective-permute-start.22 = (bf16[512,256]{1,0:T(8,128)(2,1)}, bf16[512,256]{1,0:T(8,128)(2,1)S(1)}, u32[]{:S(2)}, u32[]{:S(2)}) collective-permute-start(bf16[512,256]{1,0:T(8,128)(2,1)} %get-tuple-element.189), channel_id=1, source_target_pairs={{0,8},{4,12},{8,0},{12,4},{1,9},{5,13},{9,1},{13,5},{2,10},{6,14},... | collective-permute-start | bytes 786440 | tf_op jit(solution)/shard_map/ppermute | solution.py:62
  369.8 40.8 %collective-permute-start.17 = (bf16[1152,256]{1,0:T(8,128)(2,1)}, bf16[1152,256]{1,0:T(8,128)(2,1)}, u32[]{:S(2)}, u32[]{:S(2)}) collective-permute-start(bf16[1152,256]{1,0:T(8,128)(2,1)} %get-tuple-element.179), channel_id=1, source_target_pairs={{0,4},{4,8},{8,12},{12,0},{1,5},{5,9},{9,13},{13,1},{2,6},{6,10},{... | collective-permute-start | bytes 1769480 | tf_op jit(solution)/shard_map/ppermute | solution.py:62
  371.5 39.1 %collective-permute-start.18 = (bf16[1152,256]{1,0:T(8,128)(2,1)}, bf16[1152,256]{1,0:T(8,128)(2,1)}, u32[]{:S(2)}, u32[]{:S(2)}) collective-permute-start(bf16[1152,256]{1,0:T(8,128)(2,1)} %get-tuple-element.178), channel_id=1, source_target_pairs={{0,12},{4,0},{8,4},{12,8},{1,13},{5,1},{9,5},{13,9},{2,14},{6,2},{... | collective-permute-start | bytes 1769480 | tf_op jit(solution)/shard_map/ppermute | solution.py:62
  377.8 32.8 %collective-permute-start.19 = (bf16[1152,256]{1,0:T(8,128)(2,1)}, bf16[1152,256]{1,0:T(8,128)(2,1)}, u32[]{:S(2)}, u32[]{:S(2)}) collective-permute-start(bf16[1152,256]{1,0:T(8,128)(2,1)} %get-tuple-element.177), channel_id=1, source_target_pairs={{0,8},{4,12},{8,0},{12,4},{1,9},{5,13},{9,1},{13,5},{2,10},{6,14},... | collective-permute-start | bytes 1769480 | tf_op jit(solution)/shard_map/ppermute | solution.py:62
  378.5 32.1 %collective-permute-start.15 = (bf16[1024,256]{1,0:T(8,128)(2,1)S(1)}, bf16[1024,256]{1,0:T(8,128)(2,1)}, u32[]{:S(2)}, u32[]{:S(2)}) collective-permute-start(bf16[1024,256]{1,0:T(8,128)(2,1)S(1)} %all_gather.52.low_ref.refs_0_), channel_id=1, source_target_pairs={{0,96},{32,0},{64,32},{96,64},{1,97},{33,1},{65,33},{97,65},{2,98}... | collective-permute-start | bytes 1572872 | tf_op jit(solution)/shard_map/ppermute | solution.py:62
  380.1 30.5 %collective-permute-start.16 = (bf16[1024,256]{1,0:T(8,128)(2,1)S(1)}, bf16[1024,256]{1,0:T(8,128)(2,1)}, u32[]{:S(2)}, u32[]{:S(2)}) collective-permute-start(bf16[1024,256]{1,0:T(8,128)(2,1)S(1)} %all_gather.52.low_ref.refs_0_), channel_id=1, source_target_pairs={{0,64},{32,96},{64,0},{96,32},{1,65},{33,97},{65,1},{97,33},{2,66}... | collective-permute-start | bytes 1572872 | tf_op jit(solution)/shard_map/ppermute | solution.py:62
  391.5 37.1 %all-to-all-start.10 = ((bf16[8,384,128]{2,1,0:T(8,128)(2,1)}), bf16[8,384,128]{2,1,0:T(8,128)(2,1)S(1)}, u32[]{:S(2)}, u32[]{:S(2)}) async-start(bf16[8,384,128]{2,1,0:T(8,128)(2,1)} %copy-done.24), calls=%async_computation.10 | async-start | bytes 1572864 | tf_op jit(solution)/shard_map/all_to_all | solution.py:547
  428.6 31.8 %all-to-all-start.11 = ((bf16[16,512,128]{2,1,0:T(8,128)(2,1)}), bf16[16,512,128]{2,1,0:T(8,128)(2,1)}, u32[]{:S(2)}, u32[]{:S(2)}) async-start(bf16[16,512,128]{2,1,0:T(8,128)(2,1)} %bitcast.182), calls=%async_computation.11 | async-start | bytes 4194304 | tf_op jit(solution)/shard_map/all_to_all | solution.py:55
  435.3 112.3 %reduce-scatter.4.cloned.1.call-start = ((), (), s32[]{:S(2)}) async-start(), calls=%async_computation.19 | async-start | bytes 2228224
  463.4 7.7 %collective-permute-start.23 = (bf16[640,256]{1,0:T(8,128)(2,1)}, bf16[640,256]{1,0:T(8,128)(2,1)S(1)}, u32[]{:S(2)}, u32[]{:S(2)}) collective-permute-start(bf16[640,256]{1,0:T(8,128)(2,1)} %get-tuple-element.187), channel_id=1, source_target_pairs={{0,4},{4,8},{8,12},{12,0},{1,5},{5,9},{9,13},{13,1},{2,6},{6,10},{... | collective-permute-start | bytes 983048 | tf_op jit(solution)/shard_map/ppermute | solution.py:62
  463.9 9.7 %collective-permute-start.24 = (bf16[640,256]{1,0:T(8,128)(2,1)}, bf16[640,256]{1,0:T(8,128)(2,1)S(1)}, u32[]{:S(2)}, u32[]{:S(2)}) collective-permute-start(bf16[640,256]{1,0:T(8,128)(2,1)} %get-tuple-element.186), channel_id=1, source_target_pairs={{0,12},{4,0},{8,4},{12,8},{1,13},{5,1},{9,5},{13,9},{2,14},{6,2},{... | collective-permute-start | bytes 983048 | tf_op jit(solution)/shard_map/ppermute | solution.py:62
  466.1 11.9 %collective-permute-start.25 = (bf16[640,256]{1,0:T(8,128)(2,1)}, bf16[640,256]{1,0:T(8,128)(2,1)S(1)}, u32[]{:S(2)}, u32[]{:S(2)}) collective-permute-start(bf16[640,256]{1,0:T(8,128)(2,1)} %get-tuple-element.185), channel_id=1, source_target_pairs={{0,8},{4,12},{8,0},{12,4},{1,9},{5,13},{9,1},{13,5},{2,10},{6,14},... | collective-permute-start | bytes 983048 | tf_op jit(solution)/shard_map/ppermute | solution.py:62
  483.6 6.8 %collective-permute-start.26 = (bf16[1024,128]{1,0:T(8,128)(2,1)S(1)}, bf16[1024,128]{1,0:T(8,128)(2,1)S(1)}, u32[]{:S(2)}, u32[]{:S(2)}) collective-permute-start(bf16[1024,128]{1,0:T(8,128)(2,1)S(1)} %copy-done.35), channel_id=1, source_target_pairs={{0,16},{16,0},{1,17},{17,1},{2,18},{18,2},{3,19},{19,3},{4,20},{20... | collective-permute-start | bytes 786440 | tf_op jit(solution)/shard_map/ppermute | solution.py:43
  507.1 43.0 %all-to-all-start.13 = ((bf16[16,512,128]{2,1,0:T(8,128)(2,1)}), bf16[16,512,128]{2,1,0:T(8,128)(2,1)S(1)}, u32[]{:S(2)}, u32[]{:S(2)}) async-start(bf16[16,512,128]{2,1,0:T(8,128)(2,1)} %bitcast.62), calls=%async_computation.13 | async-start | bytes 4194304 | tf_op jit(solution)/shard_map/all_to_all | solution.py:55
  511.5 27.2 %collective-permute-start.30 = (f32[12,128]{1,0:T(8,128)S(1)}, f32[12,128]{1,0:T(8,128)S(1)}, u32[]{:S(2)}, u32[]{:S(2)}) collective-permute-start(f32[12,128]{1,0:T(8,128)S(1)} %add.362), channel_id=1, source_target_pairs={{0,64},{32,96},{64,0},{96,32},{1,65},{33,97},{65,1},{97,33},{2,66}... | collective-permute-start | bytes 18440 | tf_op jit(solution)/shard_map/ppermute | solution.py:90
  514.4 24.3 %collective-permute-start.29 = (f32[12,128]{1,0:T(8,128)S(1)}, f32[12,128]{1,0:T(8,128)S(1)}, u32[]{:S(2)}, u32[]{:S(2)}) collective-permute-start(f32[12,128]{1,0:T(8,128)S(1)} %add.362), channel_id=1, source_target_pairs={{0,96},{32,0},{64,32},{96,64},{1,97},{33,1},{65,33},{97,65},{2,98}... | collective-permute-start | bytes 18440 | tf_op jit(solution)/shard_map/ppermute | solution.py:90
  515.3 23.4 %collective-permute-start.28 = (f32[12,128]{1,0:T(8,128)S(1)}, f32[12,128]{1,0:T(8,128)S(1)}, u32[]{:S(2)}, u32[]{:S(2)}) collective-permute-start(f32[12,128]{1,0:T(8,128)S(1)} %add.362), channel_id=1, source_target_pairs={{0,32},{32,64},{64,96},{96,0},{1,33},{33,65},{65,97},{97,1},{2,34}... | collective-permute-start | bytes 18440 | tf_op jit(solution)/shard_map/ppermute | solution.py:90
  538.7 3.8 collective-permute-start.31
  550.5 8.8 %collective-permute-start.27 = (bf16[2,448,128]{2,1,0:T(8,128)(2,1)S(1)}, bf16[2,448,128]{2,1,0:T(8,128)(2,1)S(1)}, u32[]{:S(2)}, u32[]{:S(2)}) collective-permute-start(bf16[2,448,128]{2,1,0:T(8,128)(2,1)S(1)} %pad_maximum_fusion.9), channel_id=1, source_target_pairs={{0,0},{2,16},{16,2},{18,18},{1,1},{3,17},{17,3},{19,19},{4,4},{6,2... | collective-permute-start | bytes 688136 | tf_op jit(solution)/shard_map/ppermute | solution.py:47
  (76 other events, 585.8 us)
Sparse Core Ops, SparseCore 0:
  21.4 108.3 all-gather.9
  133.3 86.8 all-gather.7
  221.8 56.9 all-gather.13
  280.3 66.5 all-gather.11
  441.1 100.5 reduce-scatter.3

commit v5 on v4

--- a/solution.py
+++ b/solution.py
@@ -674,7 +674,7 @@
             low, downs, rest, up_0 = lax.optimization_barrier(
                 (low, downs, rest, run_up_grad(src, g_up, inputs))
             )
-            rest = lax.psum_scatter(rest.reshape(16, 512, 128), ("y",) + Z, scatter_dimension=0)
+            rest = lax.psum_scatter(rest, Y, scatter_dimension=0)
             downs = reduce_stage(downs.reshape(16, 512, 128), COL)
         pair, send_qo, p_qkv = run_qkv_back(weights[l], here, grad_qkv, low)
         if l == 1:
@@ -686,6 +686,7 @@
                 [up_0, run_attend_grad(0, src, g_qo, inputs)], axis=2
             )
             pair = after(pair, first)
+            rest = lax.psum_scatter(after(rest, first), Z, scatter_dimension=0)
             first = reduce_stage(first.reshape(16, 512, 128), ("y",) + Z)
         back = core_add(pair) + grad_total
         minor[l] = (p_qkv, p_out, p_gain_attn, p_shift_attn, p_down, p_gain_ffn, p_shift_ffn, p_up)

time: 579 us -> 576 us (level)
  transfers between devices with their start and end apart: 45 -> 46, of which waited for: 21 -> 21; matrix products, arithmetic and copies ran while one was open for 9% -> 9% of each run, Pallas kernels for 19% -> 19%
where the time goes in v5:
time: 576 us; the launch traced here: 565 us
  waiting for transfers between devices  159 us (28%)
  blocking collectives  113 us (20%)
  Pallas kernels  110 us (19%)
  starting transfers between devices  98.4 us (17%)
  local copies, waits for them, and re-layouts  39.2 us (7%)
  other arithmetic  30.1 us (5%)
  between operations  16.1 us (3%)
    pallas_call x22, Pallas kernels, call(): pl.pallas_call(kernel, grid=grid, in_specs=[spec for spec, _ in ins], out...  110 us
    all_to_all x5, blocking collectives, seq_swap(): return lax.all_to_all(values, SEQ, 0, 0, tiled=True)  67.5 us
    all_gather x1, waiting for transfers between devices, on_device(): lax.all_gather(head, CHIPS, axis=0, tiled=False)  63.2 us
    all_gather x8, blocking collectives, core_gather(): return lax.all_gather(values, CORE, axis=1, tiled=True)  27.9 us
    ppermute x18, starting transfers between devices, along(): return lax.ppermute(values, axes, [(i, (i + shift) % 4) for i in range(4)])  25.9 us
    ppermute x3, waiting for transfers between devices, sum_axis(): lax.ppermute(values, axes, [(i, (i + shift) % 4) for i in range(4)])  19.1 us
    ppermute x8, starting transfers between devices, core_add(): return keep + lax.ppermute(send, CORE, [(0, 1), (1, 0)]).astype(f32)  17.8 us
    all_to_all x1, blocking collectives, on_device(): got = lax.all_to_all(send, COL, 0, 0, tiled=True)  17.3 us
  transfers between devices with their start and end apart: 46, of which 21 were waited for; matrix products, arithmetic and copies ran while one was open for 9% of the time, Pallas kernels for 19%

profile of v5, /device:TPU:1, one launch (start us, length us, event | category | flops | bytes accessed | tf_op | source)
XLA Modules:
  0.0 565.2 jit_solution(12069176137887867704)
XLA Ops:
  8.4 6.9 %collective-permute-start = (bf16[2,448,128]{2,1,0:T(8,128)(2,1)S(1)}, bf16[2,448,128]{2,1,0:T(8,128)(2,1)S(1)}, u32[]{:S(2)}, u32[]{:S(2)}) collective-permute-start(bf16[2,448,128]{2,1,0:T(8,128)(2,1)S(1)} %pad_maximum_fusion.8), channel_id=1, source_target_pairs={{0,0},{2,16},{16,2},{18,18},{1,1},{3,17},{17,3},{19,19},{4,4},{6,2... | collective-permute-start | bytes 688136 | tf_op jit(solution)/shard_map/ppermute | solution.py:47
  23.4 4.6 all-to-all-start.2
  29.6 5.0 all-to-all-done.2
  34.6 3.5 all-to-all-start
  38.3 7.9 %all-to-all-done = bf16[64,16,128]{2,0,1:T(8,128)(2,1)S(1)} async-done(((bf16[64,16,128]{2,0,1:T(8,128)(2,1)}), bf16[64,16,128]{2,0,1:T(8,128)(2,1)S(1)}, u32[]{:S(2)}, u32[]{:S(2)}) %all-to-all-start) | async-done | bytes 262176 | tf_op jit(solution)/shard_map/all_to_all | solution.py:621
  46.2 3.5 all-to-all-start.1
  50.0 7.0 %all-to-all-done.1 = bf16[64,16,128]{2,0,1:T(8,128)(2,1)S(1)} async-done(((bf16[64,16,128]{2,0,1:T(8,128)(2,1)}), bf16[64,16,128]{2,0,1:T(8,128)(2,1)S(1)}, u32[]{:S(2)}, u32[]{:S(2)}) %all-to-all-start.1) | async-done | bytes 262176 | tf_op jit(solution)/shard_map/all_to_all | solution.py:622
  57.1 9.5 %all_gather.47.x_ref = bf16[1024,256]{1,0:T(8,128)(2,1)S(1)} all-gather(bf16[1024,128]{1,0:T(8,128)(2,1)S(1)} %convert_element_type.128), channel_id=1, replica_groups=mesh['y'=4,'k'=2,'xh'=2,'xl'=2,'zh'=2,'zl'=2] {'k'}, dimensions={1}, use_global_device_ids=true | all-gather | bytes 786432 | tf_op jit(solution)/shard_map/all_gather | solution.py:38
  66.6 63.2 %all-gather.10.cloned.1.call-done = bf16[65536,128]{1,0:T(8,128)(2,1)} async-done(((bf16[1024,128]{1,0:T(8,128)(2,1)}), bf16[65536,128]{1,0:T(8,128)(2,1)}) %all-gather.10.cloned.1.call-update) | async-done | bytes 16777232 | tf_op jit(solution)/shard_map/all_gather | solution.py:598
  130.1 3.8 shard_map.245
  133.8 15.9 %all_to_all.90.p_ref = bf16[8,384,128]{2,1,0:T(8,128)(2,1)S(1)} all-to-all(bf16[8,384,128]{2,1,0:T(8,128)(2,1)S(1)} %bitcast.152), channel_id=1, replica_groups=mesh['y'=4,'k'=2,'xh'=2,'xl'=2,'zh'=2,'zl'=2] {'xl','zh','zl'}, dimensions={0} | all-to-all | bytes 1572864 | tf_op jit(solution)/shard_map/all_to_all | solution.py:547
  149.8 6.5 %shard_map.246 = (bf16[8,128,128]{2,1,0:T(8,128)(2,1)S(1)}, f32[2,1024]{1,0:T(2,128)S(1)}) custom-call(bf16[8,384,128]{2,1,0:T(8,128)(2,1)S(1)} %all_to_all.90.p_ref), custom_call_target="tpu_custom_call" | custom-call | flops 1073741824 | bytes 1048576 | tf_op jit(solution)/shard_map/pallas_call | solution.py:95
  156.3 8.9 %all_to_all.91.b_ref = bf16[8,128,128]{2,1,0:T(8,128)(2,1)S(1)} all-to-all(bf16[8,128,128]{2,1,0:T(8,128)(2,1)S(1)} %get-tuple-element.69), channel_id=1, replica_groups=mesh['y'=4,'k'=2,'xh'=2,'xl'=2,'zh'=2,'zl'=2] {'xl','zh','zl'}, dimensions={0} | all-to-all | bytes 524288 | tf_op jit(solution)/shard_map/all_to_all | solution.py:547
  176.1 7.7 %shard_map.248 = (f32[1024,128]{1,0:T(8,128)S(1)}, bf16[1024,128]{1,0:T(8,128)(2,1)S(1)}, bf16[2048,256]{1,0:T(8,128)(2,1)S(1)}, f32[2048,256]{1,0:T(8,128)}) custom-call(s32[1]{0:T(128)} %bitcast.4.core_ref, bf16[4,4,2,2,1024,128]{5,4,3,2,1,0:T(8,128)(2,1)} %bitcast.160, bf16[4,4,2,2,1024,128]{5,4,3,2,1,0:T(8,128)(2,1)} %bitcast.161, ...), custom_call_target="tpu_custom_call" | custom-call | flops 2147483648 | bytes 13631488 | tf_op jit(solution)/shard_map/pallas_call | solution.py:95
  190.0 3.8 shard_map.249
  193.8 22.5 %all_to_all.92.p_ref = bf16[8,384,128]{2,1,0:T(8,128)(2,1)S(1)} all-to-all(bf16[8,384,128]{2,1,0:T(8,128)(2,1)S(1)} %bitcast.153), channel_id=1, replica_groups=mesh['y'=4,'k'=2,'xh'=2,'xl'=2,'zh'=2,'zl'=2] {'xl','zh','zl'}, dimensions={0} | all-to-all | bytes 1572864 | tf_op jit(solution)/shard_map/all_to_all | solution.py:547
  216.3 6.5 %shard_map.250 = (bf16[8,128,128]{2,1,0:T(8,128)(2,1)S(1)}, f32[2,1024]{1,0:T(2,128)S(1)}) custom-call(bf16[8,384,128]{2,1,0:T(8,128)(2,1)S(1)} %all_to_all.92.p_ref), custom_call_target="tpu_custom_call" | custom-call | flops 1073741824 | bytes 1048576 | tf_op jit(solution)/shard_map/pallas_call | solution.py:95
  222.9 9.2 %all_to_all.93.b_ref = bf16[8,128,128]{2,1,0:T(8,128)(2,1)S(1)} all-to-all(bf16[8,128,128]{2,1,0:T(8,128)(2,1)S(1)} %get-tuple-element.74), channel_id=1, replica_groups=mesh['y'=4,'k'=2,'xh'=2,'xl'=2,'zh'=2,'zl'=2] {'xl','zh','zl'}, dimensions={0} | all-to-all | bytes 524288 | tf_op jit(solution)/shard_map/all_to_all | solution.py:547
  241.4 7.7 %shard_map.252 = (f32[1024,128]{1,0:T(8,128)S(1)}, bf16[1024,128]{1,0:T(8,128)(2,1)S(1)}, bf16[2048,256]{1,0:T(8,128)(2,1)S(1)}, f32[2048,256]{1,0:T(8,128)}) custom-call(s32[1]{0:T(128)} %bitcast.4.core_ref, bf16[4,4,2,2,512,128]{5,4,3,2,1,0:T(8,128)(2,1)} %bitcast.170, bf16[4,4,2,2,512,128]{5,4,3,2,1,0:T(8,128)(2,1)} %bitcast.171, ...), custom_call_target="tpu_custom_call" | custom-call | flops 2147483648 | bytes 13631488 | tf_op jit(solution)/shard_map/pallas_call | solution.py:95
  256.5 7.9 %shard_map.253 = (f32[1024,128]{1,0:T(8,128)S(1)}, bf16[1024,128]{1,0:T(8,128)(2,1)S(1)}, f32[2048,1]{1,0:T(8,128)S(1)}, bf16[4,512,256]{2,1,0:T(8,128)(2,1)S(1)}) custom-call(s32[1]{0:T(128)} %bitcast.4.core_ref, bf16[4,4,2,2,512,128]{5,4,3,2,1,0:T(8,128)(2,1)} %bitcast.172, bf16[4,4,2,2,512,128]{5,4,3,2,1,0:T(8,128)(2,1)} %bitcast.173, ...), custom_call_target="tpu_custom_call" | custom-call | flops 2147483648 | bytes 14680064 | tf_op jit(solution)/shard_map/pallas_call | solution.py:95
  271.1 10.9 %all_to_all.94.b_ref = bf16[8,128,128]{2,1,0:T(8,128)(2,1)S(1)} all-to-all(bf16[8,128,128]{2,1,0:T(8,128)(2,1)S(1)} %shard_map.254), channel_id=1, replica_groups=mesh['y'=4,'k'=2,'xh'=2,'xl'=2,'zh'=2,'zl'=2] {'xl','zh','zl'}, dimensions={0} | all-to-all | bytes 524288 | tf_op jit(solution)/shard_map/all_to_all | solution.py:547
  282.0 6.8 %shard_map.255 = bf16[8,384,128]{2,1,0:T(8,128)(2,1)S(1)} custom-call(bf16[8,384,128]{2,1,0:T(8,128)(2,1)S(1)} %copy-done.23, bf16[8,128,128]{2,1,0:T(8,128)(2,1)S(1)} %all_to_all.94.b_ref, f32[2,1024]{1,0:T(2,128)S(1)} %get-tuple-element.83.log_ref), custom_call_target="tpu_custom_call" | custom-call | flops 2684354560 | bytes 2097152 | tf_op jit(solution)/shard_map/pallas_call | solution.py:95
  289.7 3.6 all-to-all-start.8
  293.3 16.4 %all-to-all-done.8 = bf16[8,384,128]{2,1,0:T(8,128)(2,1)S(1)} async-done(((bf16[8,384,128]{2,1,0:T(8,128)(2,1)}), bf16[8,384,128]{2,1,0:T(8,128)(2,1)S(1)}, u32[]{:S(2)}, u32[]{:S(2)}) %all-to-all-start.8) | async-done | bytes 786464 | tf_op jit(solution)/shard_map/all_to_all | solution.py:547
  309.7 5.4 shard_map.256
  315.1 3.6 collective-permute-start.6
  328.0 7.8 %shard_map.257 = (f32[1024,128]{1,0:T(8,128)S(1)}, bf16[1024,128]{1,0:T(8,128)(2,1)S(1)}, f32[2048,1]{1,0:T(8,128)S(1)}, bf16[4,512,256]{2,1,0:T(8,128)(2,1)S(1)}) custom-call(s32[1]{0:T(128)} %bitcast.4.core_ref, bf16[4,4,2,2,1024,128]{5,4,3,2,1,0:T(8,128)(2,1)} %bitcast.166, bf16[4,4,2,2,1024,128]{5,4,3,2,1,0:T(8,128)(2,1)} %bitcast.167, ...), custom_call_target="tpu_custom_call" | custom-call | flops 2147483648 | bytes 14680064 | tf_op jit(solution)/shard_map/pallas_call | solution.py:95
  346.5 4.1 all_gather.55.low_ref
  353.1 5.7 %all-to-all-start.9 = ((bf16[8,128,128]{2,1,0:T(8,128)(2,1)}), bf16[8,128,128]{2,1,0:T(8,128)(2,1)}, u32[]{:S(2)}, u32[]{:S(2)}) async-start(bf16[8,128,128]{2,1,0:T(8,128)(2,1)} %shard_map.258), calls=%async_computation.9 | async-start | bytes 524288 | tf_op jit(solution)/shard_map/all_to_all | solution.py:547
  371.5 6.3 %collective-permute-start.18 = (bf16[1152,256]{1,0:T(8,128)(2,1)}, bf16[1152,256]{1,0:T(8,128)(2,1)}, u32[]{:S(2)}, u32[]{:S(2)}) collective-permute-start(bf16[1152,256]{1,0:T(8,128)(2,1)} %get-tuple-element.180), channel_id=1, source_target_pairs={{0,12},{4,0},{8,4},{12,8},{1,13},{5,1},{9,5},{13,9},{2,14},{6,2},{... | collective-permute-start | bytes 1769480 | tf_op jit(solution)/shard_map/ppermute | solution.py:62
  382.9 7.7 %shard_map.259 = bf16[8,384,128]{2,1,0:T(8,128)(2,1)S(1)} custom-call(bf16[8,384,128]{2,1,0:T(8,128)(2,1)S(1)} %copy-done.20, bf16[8,128,128]{2,1,0:T(8,128)(2,1)} %all-to-all-done.9.b_ref, f32[2,1024]{1,0:T(2,128)S(1)} %get-tuple-element.89.log_ref), custom_call_target="tpu_custom_call" | custom-call | flops 2684354560 | bytes 2097152 | tf_op jit(solution)/shard_map/pallas_call | solution.py:95
  391.5 4.0 all-to-all-start.10
  397.6 4.6 shard_map.260
  406.0 3.6 shard_map.264
  410.7 4.5 shard_map.263
  415.3 4.3 shard_map.262
  419.6 4.5 shard_map.261
  428.5 6.6 %all-to-all-start.11 = ((bf16[16,512,128]{2,1,0:T(8,128)(2,1)}), bf16[16,512,128]{2,1,0:T(8,128)(2,1)}, u32[]{:S(2)}, u32[]{:S(2)}) async-start(bf16[16,512,128]{2,1,0:T(8,128)(2,1)} %bitcast.180), calls=%async_computation.11 | async-start | bytes 4194304 | tf_op jit(solution)/shard_map/all_to_all | solution.py:55
  441.1 5.2 shard_map.265
  446.9 13.4 %all-to-all-done.11 = bf16[16,512,128]{2,1,0:T(8,128)(2,1)} async-done(((bf16[16,512,128]{2,1,0:T(8,128)(2,1)}), bf16[16,512,128]{2,1,0:T(8,128)(2,1)}, u32[]{:S(2)}, u32[]{:S(2)}) %all-to-all-start.11) | async-done | bytes 2097184 | tf_op jit(solution)/shard_map/all_to_all | solution.py:55
  466.9 4.1 collective-permute-done.23.refs_1_
  473.3 3.6 collective-permute-done.25.refs_3_
  477.0 4.0 shard_map.266
  482.6 6.0 %collective-permute-start.26 = (bf16[1024,128]{1,0:T(8,128)(2,1)S(1)}, bf16[1024,128]{1,0:T(8,128)(2,1)S(1)}, u32[]{:S(2)}, u32[]{:S(2)}) collective-permute-start(bf16[1024,128]{1,0:T(8,128)(2,1)S(1)} %copy-done.35), channel_id=1, source_target_pairs={{0,16},{16,0},{1,17},{17,1},{2,18},{18,2},{3,19},{19,3},{4,20},{20... | collective-permute-start | bytes 786440 | tf_op jit(solution)/shard_map/ppermute | solution.py:43
  490.2 17.3 %all_to_all.95 = bf16[16,152,128]{2,1,0:T(8,128)(2,1)S(1)} all-to-all(bf16[16,152,128]{2,1,0:T(8,128)(2,1)S(1)} %pad_maximum_fusion.5), channel_id=1, replica_groups=mesh['y'=4,'k'=2,'xh'=2,'xl'=2,'zh'=2,'zl'=2] {'xh','xl','zh','zl'}, dimensions={0} | all-to-all | bytes 1245184 | tf_op jit(solution)/shard_map/all_to_all | solution.py:719
  507.4 3.7 all-to-all-start.13
  516.7 19.1 %collective-permute-done.30 = f32[12,128]{1,0:T(8,128)S(1)} collective-permute-done((f32[12,128]{1,0:T(8,128)S(1)}, f32[12,128]{1,0:T(8,128)S(1)}, u32[]{:S(2)}, u32[]{:S(2)}) %collective-permute-start.30) | collective-permute-done | bytes 6176 | tf_op jit(solution)/shard_map/ppermute | solution.py:90
  547.6 5.2 collective-permute-start.27
  (444 shorter events, 145.0 us)
Async XLA Ops:
  7.3 122.5 %all-gather.10.cloned.1.call-start = ((), (), s32[]{:S(2)}) async-start(), calls=%async_computation.19 | async-start | bytes 17039360 | tf_op jit(solution)/shard_map/all_gather | solution.py:598
  8.4 10.6 %collective-permute-start = (bf16[2,448,128]{2,1,0:T(8,128)(2,1)S(1)}, bf16[2,448,128]{2,1,0:T(8,128)(2,1)S(1)}, u32[]{:S(2)}, u32[]{:S(2)}) collective-permute-start(bf16[2,448,128]{2,1,0:T(8,128)(2,1)S(1)} %pad_maximum_fusion.8), channel_id=1, source_target_pairs={{0,0},{2,16},{16,2},{18,18},{1,1},{3,17},{17,3},{19,19},{4,4},{6,2... | collective-permute-start | bytes 688136 | tf_op jit(solution)/shard_map/ppermute | solution.py:47
  21.3 219.8 %all-gather.8.cloned.1.call-start = ((), (), s32[]{:S(2)}) async-start(), calls=%async_computation.16 | async-start | bytes 8519680 | tf_op jit(solution)/shard_map/all_gather | solution.py:599
  23.4 11.2 %all-to-all-start.2 = ((f32[16,1,1536]{2,1,0:T(1,128)}), f32[16,1,1536]{2,1,0:T(1,128)S(1)}, u32[]{:S(2)}, u32[]{:S(2)}) async-start(f32[16,1,1536]{2,1,0:T(1,128)} %broadcast_in_dim.18), calls=%async_computation.2 | async-start | bytes 196608 | tf_op jit(solution)/shard_map/all_to_all | solution.py:608
  34.6 11.6 %all-to-all-start = ((bf16[64,16,128]{2,0,1:T(8,128)(2,1)}), bf16[64,16,128]{2,0,1:T(8,128)(2,1)S(1)}, u32[]{:S(2)}, u32[]{:S(2)}) async-start(bf16[64,16,128]{2,0,1:T(8,128)(2,1)} %copy_bitcast_fusion.3), calls=%async_computation | async-start | bytes 524288 | tf_op jit(solution)/shard_map/all_to_all | solution.py:621
  46.2 10.8 %all-to-all-start.1 = ((bf16[64,16,128]{2,0,1:T(8,128)(2,1)}), bf16[64,16,128]{2,0,1:T(8,128)(2,1)S(1)}, u32[]{:S(2)}, u32[]{:S(2)}) async-start(bf16[64,16,128]{2,0,1:T(8,128)(2,1)} %copy_bitcast_fusion.2), calls=%async_computation.1 | async-start | bytes 524288 | tf_op jit(solution)/shard_map/all_to_all | solution.py:622
  49.7 352.5 %all-gather.14.cloned.1.call-start = ((), (), s32[]{:S(2)}) async-start(), calls=%async_computation.21 | async-start | bytes 6553600 | tf_op jit(solution)/shard_map/all_gather | solution.py:637
  57.1 195.8 %copy-start.44 = (f32[64,16,128]{2,0,1:T(8,128)}, f32[64,16,128]{2,0,1:T(8,128)S(1)}, u32[]{:S(2)}) copy-start(f32[64,16,128]{2,0,1:T(8,128)S(1)} %convert_element_type.162) | copy-start | bytes 1572868
  167.0 4.5 collective-permute-start.1
  175.7 235.0 %all-gather.12.cloned.1.call-start = ((), (), s32[]{:S(2)}) async-start(), calls=%async_computation.20 | async-start | bytes 6553600 | tf_op jit(solution)/shard_map/all_gather | solution.py:637
  184.8 1.7 collective-permute-start.2
  187.2 136.0 %copy-start.63 = (f32[128]{0:T(128)}, f32[128]{0:T(128)S(1)}, u32[]{:S(2)}) copy-start(f32[128]{0:T(128)S(1)} %add_rsqrt_fusion.2) | copy-start | bytes 1540
  233.8 4.0 collective-permute-start.3
  250.1 1.6 collective-permute-start.4
  264.4 1.6 collective-permute-start.5
  289.7 20.0 %all-to-all-start.8 = ((bf16[8,384,128]{2,1,0:T(8,128)(2,1)}), bf16[8,384,128]{2,1,0:T(8,128)(2,1)S(1)}, u32[]{:S(2)}, u32[]{:S(2)}) async-start(bf16[8,384,128]{2,1,0:T(8,128)(2,1)} %copy-done.21), calls=%async_computation.8 | async-start | bytes 1572864 | tf_op jit(solution)/shard_map/all_to_all | solution.py:547
  315.1 8.1 %collective-permute-start.6 = (bf16[1024,128]{1,0:T(8,128)(2,1)S(1)}, bf16[1024,128]{1,0:T(8,128)(2,1)S(1)}, u32[]{:S(2)}, u32[]{:S(2)}) collective-permute-start(bf16[1024,128]{1,0:T(8,128)(2,1)S(1)} %get-tuple-element.85), channel_id=1, source_target_pairs={{0,16},{16,0},{1,17},{17,1},{2,18},{18,2},{3,19},{19,3},{4,20},{20... | collective-permute-start | bytes 786440 | tf_op jit(solution)/shard_map/ppermute | solution.py:43
  319.0 21.2 %collective-permute-start.11 = (bf16[2,512,256]{2,1,0:T(8,128)(2,1)S(1)}, bf16[2,512,256]{2,1,0:T(8,128)(2,1)S(1)}, u32[]{:S(2)}, u32[]{:S(2)}) collective-permute-start(bf16[2,512,256]{2,1,0:T(8,128)(2,1)S(1)} %get-tuple-element.185), channel_id=1, source_target_pairs={{0,32},{32,64},{64,96},{96,0},{1,33},{33,65},{65,97},{97,1},{2,34}... | collective-permute-start | bytes 1572872 | tf_op jit(solution)/shard_map/ppermute | solution.py:62
  319.7 21.9 %collective-permute-start.12 = (bf16[2,512,256]{2,1,0:T(8,128)(2,1)S(1)}, bf16[2,512,256]{2,1,0:T(8,128)(2,1)S(1)}, u32[]{:S(2)}, u32[]{:S(2)}) collective-permute-start(bf16[2,512,256]{2,1,0:T(8,128)(2,1)S(1)} %get-tuple-element.186), channel_id=1, source_target_pairs={{0,96},{32,0},{64,32},{96,64},{1,97},{33,1},{65,33},{97,65},{2,98}... | collective-permute-start | bytes 1572872 | tf_op jit(solution)/shard_map/ppermute | solution.py:62
  321.7 23.8 %collective-permute-start.13 = (bf16[2,512,256]{2,1,0:T(8,128)(2,1)S(1)}, bf16[2,512,256]{2,1,0:T(8,128)(2,1)S(1)}, u32[]{:S(2)}, u32[]{:S(2)}) collective-permute-start(bf16[2,512,256]{2,1,0:T(8,128)(2,1)S(1)} %get-tuple-element.183), channel_id=1, source_target_pairs={{0,64},{32,96},{64,0},{96,32},{1,65},{33,97},{65,1},{97,33},{2,66}... | collective-permute-start | bytes 1572872 | tf_op jit(solution)/shard_map/ppermute | solution.py:62
  322.7 36.1 %collective-permute-start.14 = (bf16[1024,256]{1,0:T(8,128)(2,1)S(1)}, bf16[1024,256]{1,0:T(8,128)(2,1)S(1)}, u32[]{:S(2)}, u32[]{:S(2)}) collective-permute-start(bf16[1024,256]{1,0:T(8,128)(2,1)S(1)} %all_gather.52.low_ref.refs_0_), channel_id=1, source_target_pairs={{0,32},{32,64},{64,96},{96,0},{1,33},{33,65},{65,97},{97,1},{2,34}... | collective-permute-start | bytes 1572872 | tf_op jit(solution)/shard_map/ppermute | solution.py:62
  335.9 1.6 collective-permute-start.7
  337.5 40.4 %collective-permute-start.8 = (bf16[1024,256]{1,0:T(8,128)(2,1)S(1)}, bf16[1024,256]{1,0:T(8,128)(2,1)}, u32[]{:S(2)}, u32[]{:S(2)}) collective-permute-start(bf16[1024,256]{1,0:T(8,128)(2,1)S(1)} %all_gather.54.low_ref.refs_0_), channel_id=1, source_target_pairs={{0,32},{32,64},{64,96},{96,0},{1,33},{33,65},{65,97},{97,1},{2,34}... | collective-permute-start | bytes 1572872 | tf_op jit(solution)/shard_map/ppermute | solution.py:62
  340.2 38.3 %collective-permute-start.9 = (bf16[1024,256]{1,0:T(8,128)(2,1)S(1)}, bf16[1024,256]{1,0:T(8,128)(2,1)}, u32[]{:S(2)}, u32[]{:S(2)}) collective-permute-start(bf16[1024,256]{1,0:T(8,128)(2,1)S(1)} %all_gather.54.low_ref.refs_0_), channel_id=1, source_target_pairs={{0,96},{32,0},{64,32},{96,64},{1,97},{33,1},{65,33},{97,65},{2,98}... | collective-permute-start | bytes 1572872 | tf_op jit(solution)/shard_map/ppermute | solution.py:62
  341.6 38.5 %collective-permute-start.10 = (bf16[1024,256]{1,0:T(8,128)(2,1)S(1)}, bf16[1024,256]{1,0:T(8,128)(2,1)}, u32[]{:S(2)}, u32[]{:S(2)}) collective-permute-start(bf16[1024,256]{1,0:T(8,128)(2,1)S(1)} %all_gather.54.low_ref.refs_0_), channel_id=1, source_target_pairs={{0,64},{32,96},{64,0},{96,32},{1,65},{33,97},{65,1},{97,33},{2,66}... | collective-permute-start | bytes 1572872 | tf_op jit(solution)/shard_map/ppermute | solution.py:62
  345.5 16.2 %collective-permute-start.20 = (bf16[512,256]{1,0:T(8,128)(2,1)}, bf16[512,256]{1,0:T(8,128)(2,1)S(1)}, u32[]{:S(2)}, u32[]{:S(2)}) collective-permute-start(bf16[512,256]{1,0:T(8,128)(2,1)} %get-tuple-element.193), channel_id=1, source_target_pairs={{0,4},{4,8},{8,12},{12,0},{1,5},{5,9},{9,13},{13,1},{2,6},{6,10},{... | collective-permute-start | bytes 786440 | tf_op jit(solution)/shard_map/ppermute | solution.py:62
  353.1 29.8 %all-to-all-start.9 = ((bf16[8,128,128]{2,1,0:T(8,128)(2,1)}), bf16[8,128,128]{2,1,0:T(8,128)(2,1)}, u32[]{:S(2)}, u32[]{:S(2)}) async-start(bf16[8,128,128]{2,1,0:T(8,128)(2,1)} %shard_map.258), calls=%async_computation.9 | async-start | bytes 524288 | tf_op jit(solution)/shard_map/all_to_all | solution.py:547
  359.6 9.5 %collective-permute-start.21 = (bf16[512,256]{1,0:T(8,128)(2,1)}, bf16[512,256]{1,0:T(8,128)(2,1)S(1)}, u32[]{:S(2)}, u32[]{:S(2)}) collective-permute-start(bf16[512,256]{1,0:T(8,128)(2,1)} %get-tuple-element.192), channel_id=1, source_target_pairs={{0,12},{4,0},{8,4},{12,8},{1,13},{5,1},{9,5},{13,9},{2,14},{6,2},{... | collective-permute-start | bytes 786440 | tf_op jit(solution)/shard_map/ppermute | solution.py:62
  362.4 8.4 %collective-permute-start.22 = (bf16[512,256]{1,0:T(8,128)(2,1)}, bf16[512,256]{1,0:T(8,128)(2,1)S(1)}, u32[]{:S(2)}, u32[]{:S(2)}) collective-permute-start(bf16[512,256]{1,0:T(8,128)(2,1)} %get-tuple-element.191), channel_id=1, source_target_pairs={{0,8},{4,12},{8,0},{12,4},{1,9},{5,13},{9,1},{13,5},{2,10},{6,14},... | collective-permute-start | bytes 786440 | tf_op jit(solution)/shard_map/ppermute | solution.py:62
  369.8 40.8 %collective-permute-start.17 = (bf16[1152,256]{1,0:T(8,128)(2,1)}, bf16[1152,256]{1,0:T(8,128)(2,1)}, u32[]{:S(2)}, u32[]{:S(2)}) collective-permute-start(bf16[1152,256]{1,0:T(8,128)(2,1)} %get-tuple-element.181), channel_id=1, source_target_pairs={{0,4},{4,8},{8,12},{12,0},{1,5},{5,9},{9,13},{13,1},{2,6},{6,10},{... | collective-permute-start | bytes 1769480 | tf_op jit(solution)/shard_map/ppermute | solution.py:62
  371.5 39.1 %collective-permute-start.18 = (bf16[1152,256]{1,0:T(8,128)(2,1)}, bf16[1152,256]{1,0:T(8,128)(2,1)}, u32[]{:S(2)}, u32[]{:S(2)}) collective-permute-start(bf16[1152,256]{1,0:T(8,128)(2,1)} %get-tuple-element.180), channel_id=1, source_target_pairs={{0,12},{4,0},{8,4},{12,8},{1,13},{5,1},{9,5},{13,9},{2,14},{6,2},{... | collective-permute-start | bytes 1769480 | tf_op jit(solution)/shard_map/ppermute | solution.py:62
  377.8 32.8 %collective-permute-start.19 = (bf16[1152,256]{1,0:T(8,128)(2,1)}, bf16[1152,256]{1,0:T(8,128)(2,1)}, u32[]{:S(2)}, u32[]{:S(2)}) collective-permute-start(bf16[1152,256]{1,0:T(8,128)(2,1)} %get-tuple-element.179), channel_id=1, source_target_pairs={{0,8},{4,12},{8,0},{12,4},{1,9},{5,13},{9,1},{13,5},{2,10},{6,14},... | collective-permute-start | bytes 1769480 | tf_op jit(solution)/shard_map/ppermute | solution.py:62
  378.5 32.1 %collective-permute-start.15 = (bf16[1024,256]{1,0:T(8,128)(2,1)S(1)}, bf16[1024,256]{1,0:T(8,128)(2,1)}, u32[]{:S(2)}, u32[]{:S(2)}) collective-permute-start(bf16[1024,256]{1,0:T(8,128)(2,1)S(1)} %all_gather.52.low_ref.refs_0_), channel_id=1, source_target_pairs={{0,96},{32,0},{64,32},{96,64},{1,97},{33,1},{65,33},{97,65},{2,98}... | collective-permute-start | bytes 1572872 | tf_op jit(solution)/shard_map/ppermute | solution.py:62
  380.1 30.5 %collective-permute-start.16 = (bf16[1024,256]{1,0:T(8,128)(2,1)S(1)}, bf16[1024,256]{1,0:T(8,128)(2,1)}, u32[]{:S(2)}, u32[]{:S(2)}) collective-permute-start(bf16[1024,256]{1,0:T(8,128)(2,1)S(1)} %all_gather.52.low_ref.refs_0_), channel_id=1, source_target_pairs={{0,64},{32,96},{64,0},{96,32},{1,65},{33,97},{65,1},{97,33},{2,66}... | collective-permute-start | bytes 1572872 | tf_op jit(solution)/shard_map/ppermute | solution.py:62
  391.5 37.0 %all-to-all-start.10 = ((bf16[8,384,128]{2,1,0:T(8,128)(2,1)}), bf16[8,384,128]{2,1,0:T(8,128)(2,1)S(1)}, u32[]{:S(2)}, u32[]{:S(2)}) async-start(bf16[8,384,128]{2,1,0:T(8,128)(2,1)} %copy-done.24), calls=%async_computation.10 | async-start | bytes 1572864 | tf_op jit(solution)/shard_map/all_to_all | solution.py:547
  428.5 31.8 %all-to-all-start.11 = ((bf16[16,512,128]{2,1,0:T(8,128)(2,1)}), bf16[16,512,128]{2,1,0:T(8,128)(2,1)}, u32[]{:S(2)}, u32[]{:S(2)}) async-start(bf16[16,512,128]{2,1,0:T(8,128)(2,1)} %bitcast.180), calls=%async_computation.11 | async-start | bytes 4194304 | tf_op jit(solution)/shard_map/all_to_all | solution.py:55
  435.2 81.5 %reduce-scatter.3.cloned.1.call-start = ((), (), s32[]{:S(2)}) async-start(), calls=%async_computation.17 | async-start | bytes 2621440 | tf_op jit(solution)/shard_map/reduce_scatter | solution.py:677
  463.2 7.7 %collective-permute-start.23 = (bf16[640,256]{1,0:T(8,128)(2,1)}, bf16[640,256]{1,0:T(8,128)(2,1)S(1)}, u32[]{:S(2)}, u32[]{:S(2)}) collective-permute-start(bf16[640,256]{1,0:T(8,128)(2,1)} %get-tuple-element.189), channel_id=1, source_target_pairs={{0,4},{4,8},{8,12},{12,0},{1,5},{5,9},{9,13},{13,1},{2,6},{6,10},{... | collective-permute-start | bytes 983048 | tf_op jit(solution)/shard_map/ppermute | solution.py:62
  463.9 9.5 %collective-permute-start.24 = (bf16[640,256]{1,0:T(8,128)(2,1)}, bf16[640,256]{1,0:T(8,128)(2,1)S(1)}, u32[]{:S(2)}, u32[]{:S(2)}) collective-permute-start(bf16[640,256]{1,0:T(8,128)(2,1)} %get-tuple-element.188), channel_id=1, source_target_pairs={{0,12},{4,0},{8,4},{12,8},{1,13},{5,1},{9,5},{13,9},{2,14},{6,2},{... | collective-permute-start | bytes 983048 | tf_op jit(solution)/shard_map/ppermute | solution.py:62
  465.9 11.0 %collective-permute-start.25 = (bf16[640,256]{1,0:T(8,128)(2,1)}, bf16[640,256]{1,0:T(8,128)(2,1)S(1)}, u32[]{:S(2)}, u32[]{:S(2)}) collective-permute-start(bf16[640,256]{1,0:T(8,128)(2,1)} %get-tuple-element.187), channel_id=1, source_target_pairs={{0,8},{4,12},{8,0},{12,4},{1,9},{5,13},{9,1},{13,5},{2,10},{6,14},... | collective-permute-start | bytes 983048 | tf_op jit(solution)/shard_map/ppermute | solution.py:62
  482.6 7.2 %collective-permute-start.26 = (bf16[1024,128]{1,0:T(8,128)(2,1)S(1)}, bf16[1024,128]{1,0:T(8,128)(2,1)S(1)}, u32[]{:S(2)}, u32[]{:S(2)}) collective-permute-start(bf16[1024,128]{1,0:T(8,128)(2,1)S(1)} %copy-done.35), channel_id=1, source_target_pairs={{0,16},{16,0},{1,17},{17,1},{2,18},{18,2},{3,19},{19,3},{4,20},{20... | collective-permute-start | bytes 786440 | tf_op jit(solution)/shard_map/ppermute | solution.py:43
  507.4 38.0 %all-to-all-start.13 = ((bf16[16,512,128]{2,1,0:T(8,128)(2,1)}), bf16[16,512,128]{2,1,0:T(8,128)(2,1)S(1)}, u32[]{:S(2)}, u32[]{:S(2)}) async-start(bf16[16,512,128]{2,1,0:T(8,128)(2,1)} %bitcast.62), calls=%async_computation.13 | async-start | bytes 4194304 | tf_op jit(solution)/shard_map/all_to_all | solution.py:55
  511.2 34.7 %reduce-scatter.5.cloned.1.call-start = ((), (), s32[]{:S(2)}) async-start(), calls=%async_computation.18 | async-start | bytes 655360 | tf_op jit(solution)/shard_map/reduce_scatter | solution.py:689
  511.6 24.2 %collective-permute-start.30 = (f32[12,128]{1,0:T(8,128)S(1)}, f32[12,128]{1,0:T(8,128)S(1)}, u32[]{:S(2)}, u32[]{:S(2)}) collective-permute-start(f32[12,128]{1,0:T(8,128)S(1)} %add.364), channel_id=1, source_target_pairs={{0,64},{32,96},{64,0},{96,32},{1,65},{33,97},{65,1},{97,33},{2,66}... | collective-permute-start | bytes 18440 | tf_op jit(solution)/shard_map/ppermute | solution.py:90
  514.5 21.4 %collective-permute-start.29 = (f32[12,128]{1,0:T(8,128)S(1)}, f32[12,128]{1,0:T(8,128)S(1)}, u32[]{:S(2)}, u32[]{:S(2)}) collective-permute-start(f32[12,128]{1,0:T(8,128)S(1)} %add.364), channel_id=1, source_target_pairs={{0,96},{32,0},{64,32},{96,64},{1,97},{33,1},{65,33},{97,65},{2,98}... | collective-permute-start | bytes 18440 | tf_op jit(solution)/shard_map/ppermute | solution.py:90
  515.3 20.5 %collective-permute-start.28 = (f32[12,128]{1,0:T(8,128)S(1)}, f32[12,128]{1,0:T(8,128)S(1)}, u32[]{:S(2)}, u32[]{:S(2)}) collective-permute-start(f32[12,128]{1,0:T(8,128)S(1)} %add.364), channel_id=1, source_target_pairs={{0,32},{32,64},{64,96},{96,0},{1,33},{33,65},{65,97},{97,1},{2,34}... | collective-permute-start | bytes 18440 | tf_op jit(solution)/shard_map/ppermute | solution.py:90
  535.9 4.5 collective-permute-start.31
  547.6 8.9 %collective-permute-start.27 = (bf16[2,448,128]{2,1,0:T(8,128)(2,1)S(1)}, bf16[2,448,128]{2,1,0:T(8,128)(2,1)S(1)}, u32[]{:S(2)}, u32[]{:S(2)}) collective-permute-start(bf16[2,448,128]{2,1,0:T(8,128)(2,1)S(1)} %pad_maximum_fusion.9), channel_id=1, source_target_pairs={{0,0},{2,16},{16,2},{18,18},{1,1},{3,17},{17,3},{19,19},{4,4},{6,2... | collective-permute-start | bytes 688136 | tf_op jit(solution)/shard_map/ppermute | solution.py:47
  (77 other events, 639.9 us)
Sparse Core Ops, SparseCore 0:
  21.4 108.3 all-gather.9
  133.3 86.8 all-gather.7
  221.8 56.9 all-gather.13
  280.3 66.5 all-gather.11
  441.0 31.7 reduce-scatter.2
  516.8 28.8 reduce-scatter.4
